TPU v7x, 32 devices: a whole 2x2x4 slice. The times are simulated.
32 devices in a mesh: dp: 8 (over z, x), row: 2 (over y), col: 2 (over core).
Axes of the slice: x: 2, y: 2, z: 4, core: 2. Of those that a mesh axis runs over, the one named last changes fastest.
Arguments:
- layer_input: bfloat16 [16384, 768], P(('dp', 'col'), 'row'), may hold values from -6 to 6
- teacher: bfloat16 [16384, 768], P(('dp', 'col'), 'row'), may hold values from -6 to 6
- valid_mask: int32 [16384], P(('dp', 'col')), may hold values from 0 to 1, as said below
- routes: int32 [16384, 2], P('dp'), may hold values from 0 to 3, all different within a row; in each aligned block of 1024 rows (0 to 1023, 1024 to 2047, ...) at most 640 rows name the same one
- segments: int32 [16, 1024], P('dp'), may hold values from 0 to 3, never falling along the last dimension, each value on 1 to 512 neighbouring positions
- gain_attn: float32 [768], P('row'), may hold values from 0.5 to 1.5
- gain_ffn: float32 [768], P('row'), may hold values from 0.5 to 1.5
- w_qkv: bfloat16 [768, 3, 768], P('row', None, 'col'), may hold values from -0.21875 to 0.21875
- w_out: bfloat16 [768, 768], P('col', 'row'), may hold values from -0.625 to 0.625
- w_router: bfloat16 [768, 4], P('row'), may hold values from -0.15625 to 0.15625
- w_shared_up: bfloat16 [768, 2, 2048], P('row', None, 'col'), may hold values from -0.21875 to 0.21875
- w_shared_down: bfloat16 [2048, 768], P('col', 'row'), may hold values from -0.125 to 0.125
- w_expert_up: bfloat16 [4, 768, 2, 2048], P(None, 'row', None, 'col'), may hold values from -0.21875 to 0.21875
- w_expert_down: bfloat16 [4, 2048, 768], P(None, 'col', 'row'), may hold values from -0.125 to 0.125
Outputs:
- output: float32 [16384, 768], P(('dp', 'col'), 'row')
- loss: float32 [], replicated
- input_grad: float32 [16384, 768], P(('dp', 'col'), 'row')
- gain_attn_grad: float32 [768], P('row')
- gain_ffn_grad: float32 [768], P('row')
- w_qkv_grad: float32 [768, 3, 768], P('row', None, 'col')
- w_out_grad: float32 [768, 768], P('col', 'row')
- w_router_grad: float32 [768, 4], P('row')
- w_shared_up_grad: float32 [768, 2, 2048], P('row', None, 'col')
- w_shared_down_grad: float32 [2048, 768], P('col', 'row')
- w_expert_up_grad: float32 [4, 768, 2, 2048], P(None, 'row', None, 'col')
- w_expert_down_grad: float32 [4, 2048, 768], P(None, 'col', 'row')
Inputs may be any that keep to these rules, and one draw needn't show every extreme that they name: The first token of every sequence has valid_mask 1. `routes`: each token names two different experts; among the 1024 tokens of one residual-stream device (aligned blocks of rows) no expert is named more than 640 times, a bound that some block reaches. `segments`: document numbers never fall along a sequence; every document has 1 to 512 tokens and one has exactly 512.
All inputs are finite; a program needn't handle non-finite values.
Results may differ from a plain program's by a relative error of at most 0.02.
Values may be sent and summed in bfloat16 or wider, within the bound.
A program may use at most 320 MiB of HBM per device.

v0:
```python
import jax
import jax.numpy as jnp
from jax import lax
from jax.sharding import PartitionSpec as P

D = 768
HEAD_DIM = 64
E = 4
LEN = 1024
ABLOCK = 256
CAP = 640


def gather_tokens(values):
    return lax.all_gather(values, "col", axis=0, tiled=True)


def sum_tokens(values):
    return lax.psum_scatter(values, "col", scatter_dimension=0, tiled=True)


def sum_features(values):
    return lax.psum(values, "row")


def sum_rows(values):
    return lax.psum_scatter(values, "row", scatter_dimension=0, tiled=True)


def gather_rows(values):
    return lax.all_gather(values, "row", axis=0, tiled=True)


def norm_forward(values, gain_vec, full_width):
    squares = sum_features(jnp.sum(values * values, axis=1))
    rstd_rows = lax.rsqrt(squares / full_width + 1e-06)
    return (rstd_rows, values * rstd_rows[:, None] * gain_vec)


def norm_backward(values, rstd_rows, gain_vec, incoming, full_width):
    scaled = incoming * gain_vec
    inner_sum = sum_features(jnp.sum(scaled * values, axis=1))
    gain_grad = jnp.sum(incoming * values * rstd_rows[:, None], axis=0)
    result = rstd_rows[:, None] * scaled - values * (rstd_rows**3 * inner_sum / full_width)[:, None]
    return (result, gain_grad)


def rope_tables(length):
    half_dim = HEAD_DIM // 2
    freqs = 10000.0 ** (-jnp.arange(half_dim, dtype=jnp.float32) * 2.0 / HEAD_DIM)
    angles = jnp.arange(length, dtype=jnp.float32)[:, None] * freqs[None, :]
    angles = jnp.concatenate([angles, angles], axis=1)
    return (jnp.cos(angles), jnp.sin(angles))


def rotate(values, cosine, sine):
    half_dim = values.shape[-1] // 2
    turned = jnp.concatenate([-values[..., half_dim:], values[..., :half_dim]], axis=-1)
    return values * cosine[:, None, :] + turned * sine[:, None, :]


def unrotate(incoming, cosine, sine):
    half_dim = incoming.shape[-1] // 2
    moved = incoming * sine[:, None, :]
    return incoming * cosine[:, None, :] + jnp.concatenate(
        [moved[..., half_dim:], -moved[..., :half_dim]], axis=-1
    )


def silu_parts(values):
    sigma = jax.nn.sigmoid(values)
    return (values * sigma, sigma * (1.0 + values * (1.0 - sigma)))


def allowed_pairs(segment_ids, first_row, query_rows):
    query_pos = first_row + jnp.arange(query_rows)
    key_pos = jnp.arange(segment_ids.shape[0])
    query_seg = lax.dynamic_slice_in_dim(segment_ids, first_row, query_rows, 0)
    return (query_seg[:, None] == segment_ids[None, :]) & (
        key_pos[None, :] // ABLOCK <= query_pos[:, None] // ABLOCK
    )


def attend_forward(query_all, key_all, value_all, segment_ids, query_rows):
    length = key_all.shape[0]
    rescale = HEAD_DIM ** (-0.5)

    def one_block(block_index):
        first_row = block_index * query_rows
        query_part = lax.dynamic_slice_in_dim(query_all, first_row, query_rows, 0)
        scores = (
            jnp.einsum("qhd,khd->hqk", query_part, key_all, preferred_element_type=jnp.float32)
            * rescale
        )
        scores = jnp.where(allowed_pairs(segment_ids, first_row, query_rows)[None], scores, -1e30)
        highest = jnp.max(scores, axis=2, keepdims=True)
        weight = jnp.exp(scores - highest)
        totals = jnp.sum(weight, axis=2, keepdims=True)
        shares_low = (weight / totals).astype(jnp.bfloat16)
        context = jnp.einsum(
            "hqk,khd->qhd", shares_low, value_all, preferred_element_type=jnp.float32
        )
        return (context, jnp.transpose((highest + jnp.log(totals))[:, :, 0]))

    context, log_totals = lax.map(one_block, jnp.arange(length // query_rows))
    return (context.reshape(key_all.shape), log_totals.reshape(length, -1))


def attend_backward(
    query_all, key_all, value_all, context_grad, log_totals, segment_ids, query_rows
):
    length = key_all.shape[0]
    rescale = HEAD_DIM ** (-0.5)

    def one_block(carry, block_index):
        key_grad, value_grad = carry
        first_row = block_index * query_rows
        query_part = lax.dynamic_slice_in_dim(query_all, first_row, query_rows, 0)
        grad_part = lax.dynamic_slice_in_dim(context_grad, first_row, query_rows, 0)
        total_part = jnp.transpose(lax.dynamic_slice_in_dim(log_totals, first_row, query_rows, 0))
        scores = (
            jnp.einsum("qhd,khd->hqk", query_part, key_all, preferred_element_type=jnp.float32)
            * rescale
        )
        scores = jnp.where(allowed_pairs(segment_ids, first_row, query_rows)[None], scores, -1e30)
        shares = jnp.exp(scores - total_part[:, :, None])
        value_grad = value_grad + jnp.einsum(
            "hqk,qhd->khd",
            shares.astype(jnp.bfloat16),
            grad_part,
            preferred_element_type=jnp.float32,
        )
        share_grad = jnp.einsum(
            "qhd,khd->hqk", grad_part, value_all, preferred_element_type=jnp.float32
        )
        centre = jnp.sum(shares * share_grad, axis=2, keepdims=True)
        score_grad = (shares * (share_grad - centre)).astype(jnp.bfloat16)
        query_grad = (
            jnp.einsum("hqk,khd->qhd", score_grad, key_all, preferred_element_type=jnp.float32)
            * rescale
        )
        key_grad = (
            key_grad
            + jnp.einsum("hqk,qhd->khd", score_grad, query_part, preferred_element_type=jnp.float32)
            * rescale
        )
        return ((key_grad, value_grad), query_grad)

    zero_grads = jnp.zeros(key_all.shape, jnp.float32)
    (key_grad, value_grad), query_grad = lax.scan(
        one_block, (zero_grads, zero_grads), jnp.arange(length // query_rows)
    )
    return (query_grad.reshape(key_all.shape), key_grad, value_grad)


def slot_tables(route_ids, groups, local_rows, capacity, expert_count):
    picks = (
        route_ids[:, :, None] == jnp.arange(expert_count, dtype=jnp.int32)[None, None, :]
    ).astype(jnp.int32)
    halves = picks.reshape(groups, local_rows * 2, expert_count)
    ranks = jnp.cumsum(halves, axis=1) - 1
    ranks = jnp.sum(ranks * halves, axis=2).reshape(groups * local_rows, 2)
    group_of = (jnp.arange(groups * local_rows, dtype=jnp.int32) // local_rows)[:, None]
    flat_of = (group_of * capacity + ranks) * expert_count + route_ids
    total_slots = groups * capacity * expert_count
    token_ids = jnp.broadcast_to(
        jnp.arange(groups * local_rows, dtype=jnp.int32)[:, None], (groups * local_rows, 2)
    )
    owner = jnp.zeros((total_slots,), jnp.int32).at[flat_of.reshape(-1)].set(token_ids.reshape(-1))
    filled = jnp.zeros((total_slots,), jnp.int32).at[flat_of.reshape(-1)].set(1)
    return (flat_of, owner, filled)


def local(
    layer_input,
    teacher,
    valid_mask,
    routes,
    segments,
    gain_attn,
    gain_ffn,
    w_qkv,
    w_out,
    w_router,
    w_shared_up,
    w_shared_down,
    w_expert_up,
    w_expert_down,
):
    row_rank = lax.axis_index("row")
    groups = lax.axis_size("col")
    local_rows = layer_input.shape[0]
    half_width = layer_input.shape[1]
    seq_count = local_rows // LEN
    query_rows = min(512, LEN)
    slot_count = CAP * E
    valid_float = valid_mask.astype(jnp.float32)
    count = lax.psum(jnp.sum(valid_float), ("dp", "col"))
    residual = layer_input.astype(jnp.float32)
    rstd_attn, normed = norm_forward(residual, gain_attn, D)
    normed_attn = gather_tokens(normed.astype(jnp.bfloat16))
    qkv_part = jnp.einsum("td,dke->tke", normed_attn, w_qkv, preferred_element_type=jnp.float32)
    qkv_pre = sum_rows(qkv_part)
    heads_local = qkv_pre.shape[2] // HEAD_DIM
    qkv_pre = qkv_pre.reshape(seq_count, LEN, 3, heads_local, HEAD_DIM)
    cosine, sine = rope_tables(LEN)
    queries = rotate(qkv_pre[:, :, 0], cosine, sine).astype(jnp.bfloat16)
    keys_rot = rotate(qkv_pre[:, :, 1], cosine, sine).astype(jnp.bfloat16)
    values_low = qkv_pre[:, :, 2].astype(jnp.bfloat16)
    local_segments = lax.dynamic_slice_in_dim(segments, row_rank * seq_count, seq_count, 0)
    context, log_totals = lax.map(
        lambda pieces: attend_forward(pieces[0], pieces[1], pieces[2], pieces[3], query_rows),
        (queries, keys_rot, values_low, local_segments),
    )
    context_low = context.reshape(local_rows, -1).astype(jnp.bfloat16)
    context_full = gather_rows(context_low)
    attention = sum_tokens(jnp.dot(context_full, w_out, preferred_element_type=jnp.float32))
    hidden = residual + attention
    rstd_ffn, normed = norm_forward(hidden, gain_ffn, D)
    normed_ffn = gather_tokens(normed.astype(jnp.bfloat16))
    flat_of, owner, filled = slot_tables(routes, groups, local_rows, CAP, E)
    slot_inputs = normed_ffn[owner].reshape(groups * CAP, E, half_width)
    shared_part = jnp.einsum(
        "td,dkf->tkf", normed_ffn, w_shared_up, preferred_element_type=jnp.float32
    )
    router_part = jnp.dot(normed_ffn, w_router, preferred_element_type=jnp.float32)
    expert_part = jnp.einsum(
        "sed,edkh->sekh", slot_inputs, w_expert_up, preferred_element_type=jnp.float32
    )
    shared_pre, logits, expert_pre = (
        lax.psum_scatter(
            shared_part.astype(jnp.bfloat16), "row", scatter_dimension=0, tiled=True
        ).astype(jnp.float32),
        lax.psum_scatter(
            router_part.astype(jnp.bfloat16), "row", scatter_dimension=0, tiled=True
        ).astype(jnp.float32),
        lax.psum_scatter(
            expert_part.astype(jnp.bfloat16), "row", scatter_dimension=0, tiled=True
        ).astype(jnp.float32),
    )
    local_routes = lax.dynamic_slice_in_dim(routes, row_rank * local_rows, local_rows, 0)
    local_flat = (
        lax.dynamic_slice_in_dim(flat_of, row_rank * local_rows, local_rows, 0)
        - row_rank * slot_count
    )
    picks = (local_routes[:, :, None] == jnp.arange(E, dtype=jnp.int32)[None, None, :]).astype(
        jnp.float32
    )
    chosen = jnp.sum(picks * logits[:, None, :], axis=2)
    chosen = chosen - jnp.max(chosen, axis=1, keepdims=True)
    gate_pair = jnp.exp(chosen)
    gate_pair = gate_pair / jnp.sum(gate_pair, axis=1, keepdims=True)
    slot_gate = (
        jnp.zeros((slot_count,), jnp.float32)
        .at[local_flat.reshape(-1)]
        .set(gate_pair.reshape(-1))
        .reshape(CAP, E)
    )
    shared_silu, shared_slope = silu_parts(shared_pre[:, 0])
    shared_act = (shared_silu * shared_pre[:, 1]).astype(jnp.bfloat16)
    expert_silu, expert_slope = silu_parts(expert_pre[:, :, 0])
    expert_act = (expert_silu * expert_pre[:, :, 1] * slot_gate[:, :, None]).astype(jnp.bfloat16)
    shared_full, expert_full = (
        lax.all_gather(shared_act, "row", axis=0, tiled=True),
        lax.all_gather(expert_act, "row", axis=0, tiled=True),
    )
    branch_part = jnp.dot(shared_full, w_shared_down, preferred_element_type=jnp.float32)
    expert_out = jnp.einsum(
        "seh,ehd->sed", expert_full, w_expert_down, preferred_element_type=jnp.float32
    ).reshape(groups * slot_count, half_width)
    branch_part = branch_part + expert_out[flat_of[:, 0]] + expert_out[flat_of[:, 1]]
    output = hidden + sum_tokens(branch_part)
    error = output - teacher.astype(jnp.float32)
    token_error = sum_features(jnp.sum(error * error, axis=1))
    loss_part = jnp.sum(valid_float * token_error)
    total_tokens = local_rows * groups * lax.axis_size("dp")
    grad_out = total_tokens / count * valid_float[:, None] * error
    grad_rows = gather_tokens(grad_out.astype(jnp.bfloat16))
    w_shared_down_grad = jnp.einsum(
        "tf,td->fd", shared_full, grad_rows, preferred_element_type=jnp.float32
    )
    slot_grad = (grad_rows[owner] * filled[:, None].astype(jnp.bfloat16)).reshape(
        groups * CAP, E, half_width
    )
    w_expert_down_grad = jnp.einsum(
        "seh,sed->ehd", expert_full, slot_grad, preferred_element_type=jnp.float32
    )
    shared_back = jnp.einsum(
        "td,fd->tf", grad_rows, w_shared_down, preferred_element_type=jnp.float32
    )
    expert_back = jnp.einsum(
        "sed,ehd->seh", slot_grad, w_expert_down, preferred_element_type=jnp.float32
    )
    shared_grad, expert_grad = (
        lax.psum_scatter(
            shared_back.astype(jnp.bfloat16), "row", scatter_dimension=0, tiled=True
        ).astype(jnp.float32),
        lax.psum_scatter(
            expert_back.astype(jnp.bfloat16), "row", scatter_dimension=0, tiled=True
        ).astype(jnp.float32),
    )
    shared_pre_grad = jnp.stack(
        (shared_grad * shared_pre[:, 1] * shared_slope, shared_grad * shared_silu), axis=1
    ).astype(jnp.bfloat16)
    gate_grad = lax.psum(jnp.sum(expert_grad * expert_silu * expert_pre[:, :, 1], axis=2), "col")
    gated_grad = expert_grad * slot_gate[:, :, None]
    expert_pre_grad = jnp.stack(
        (gated_grad * expert_pre[:, :, 1] * expert_slope, gated_grad * expert_silu), axis=2
    ).astype(jnp.bfloat16)
    pair_grad = gate_grad.reshape(-1)[local_flat]
    centre = jnp.sum(gate_pair * pair_grad, axis=1, keepdims=True)
    logit_pair = gate_pair * (pair_grad - centre)
    logit_grad = jnp.sum(picks * logit_pair[:, :, None], axis=1).astype(jnp.bfloat16)
    shared_pre_full, logit_full, expert_pre_full = (
        lax.all_gather(shared_pre_grad, "row", axis=0, tiled=True),
        lax.all_gather(logit_grad, "row", axis=0, tiled=True),
        lax.all_gather(expert_pre_grad, "row", axis=0, tiled=True),
    )
    w_shared_up_grad = jnp.einsum(
        "td,tkf->dkf", normed_ffn, shared_pre_full, preferred_element_type=jnp.float32
    )
    w_router_grad = jnp.einsum(
        "td,te->de", normed_ffn, logit_full, preferred_element_type=jnp.float32
    )
    w_expert_up_grad = jnp.einsum(
        "sed,sekh->edkh", slot_inputs, expert_pre_full, preferred_element_type=jnp.float32
    )
    input_part = jnp.einsum(
        "tkf,dkf->td", shared_pre_full, w_shared_up, preferred_element_type=jnp.float32
    )
    input_part = input_part + 0.5 * jnp.einsum(
        "te,de->td", logit_full, w_router, preferred_element_type=jnp.float32
    )
    expert_input = jnp.einsum(
        "sekh,edkh->sed", expert_pre_full, w_expert_up, preferred_element_type=jnp.float32
    ).reshape(groups * slot_count, half_width)
    input_part = input_part + expert_input[flat_of[:, 0]] + expert_input[flat_of[:, 1]]
    normed_ffn_grad = sum_tokens(input_part)
    hidden_back, gain_ffn_grad = norm_backward(hidden, rstd_ffn, gain_ffn, normed_ffn_grad, D)
    hidden_grad = grad_out + hidden_back
    attn_rows = gather_tokens(hidden_grad.astype(jnp.bfloat16))
    w_out_grad = jnp.einsum(
        "tc,td->cd", context_full, attn_rows, preferred_element_type=jnp.float32
    )
    context_grad = sum_rows(
        jnp.einsum("td,cd->tc", attn_rows, w_out, preferred_element_type=jnp.float32)
    )
    context_grad = context_grad.astype(jnp.bfloat16).reshape(seq_count, LEN, heads_local, HEAD_DIM)
    query_grad, key_grad, value_grad = lax.map(
        lambda pieces: attend_backward(
            pieces[0], pieces[1], pieces[2], pieces[3], pieces[4], pieces[5], query_rows
        ),
        (queries, keys_rot, values_low, context_grad, log_totals, local_segments),
    )
    query_grad = unrotate(query_grad, cosine, sine)
    key_grad = unrotate(key_grad, cosine, sine)
    qkv_grad = (
        jnp.stack((query_grad, key_grad, value_grad), axis=2)
        .reshape(local_rows, 3, -1)
        .astype(jnp.bfloat16)
    )
    qkv_full = gather_rows(qkv_grad)
    w_qkv_grad = jnp.einsum(
        "td,tke->dke", normed_attn, qkv_full, preferred_element_type=jnp.float32
    )
    normed_attn_grad = sum_tokens(
        jnp.einsum("tke,dke->td", qkv_full, w_qkv, preferred_element_type=jnp.float32)
    )
    input_back, gain_attn_grad = norm_backward(residual, rstd_attn, gain_attn, normed_attn_grad, D)
    input_grad = hidden_grad + input_back
    gain_attn_grad, gain_ffn_grad, loss_total = lax.psum(
        (gain_attn_grad, gain_ffn_grad, loss_part), ("dp", "col")
    )
    loss = loss_total / (2.0 * count)
    summed = (
        lax.psum(w_qkv_grad.astype(jnp.bfloat16), "dp").astype(jnp.float32),
        lax.psum(w_out_grad.astype(jnp.bfloat16), "dp").astype(jnp.float32),
        lax.psum(w_router_grad.astype(jnp.bfloat16), "dp").astype(jnp.float32),
        lax.psum(w_shared_up_grad.astype(jnp.bfloat16), "dp").astype(jnp.float32),
        lax.psum(w_shared_down_grad.astype(jnp.bfloat16), "dp").astype(jnp.float32),
        lax.psum(w_expert_up_grad.astype(jnp.bfloat16), "dp").astype(jnp.float32),
        lax.psum(w_expert_down_grad.astype(jnp.bfloat16), "dp").astype(jnp.float32),
    )
    return (
        output,
        loss,
        input_grad,
        gain_attn_grad,
        gain_ffn_grad,
        summed[0],
        summed[1],
        summed[2],
        summed[3],
        summed[4],
        summed[5],
        summed[6],
    )


def solution(mesh):
    return jax.shard_map(
        local,
        mesh=mesh,
        in_specs=(
            P(("dp", "col"), "row"),
            P(("dp", "col"), "row"),
            P(("dp", "col")),
            P("dp", None),
            P("dp", None),
            P("row"),
            P("row"),
            P("row", None, "col"),
            P("col", "row"),
            P("row", None),
            P("row", None, "col"),
            P("col", "row"),
            P(None, "row", None, "col"),
            P(None, "col", "row"),
        ),
        out_specs=(
            P(("dp", "col"), "row"),
            P(),
            P(("dp", "col"), "row"),
            P("row"),
            P("row"),
            P("row", None, "col"),
            P("col", "row"),
            P("row", None),
            P("row", None, "col"),
            P("col", "row"),
            P(None, "row", None, "col"),
            P(None, "col", "row"),
        ),
        check_vma=False,
    )
```

profile of v0, /device:TPU:27, one launch (start us, length us, event | category | flops | bytes accessed | tf_op | source)
XLA Modules:
  0.0 2327.9 jit_solution(79181839450816345)
XLA Ops:
  15.5 12.7 all-gather.11.cloned.1.call-done
  39.4 108.2 %reduce-scatter.14.cloned.1.call-done = f32[1024,3,384]{2,0,1:T(8,128)} async-done(((f32[2048,3,384]{2,0,1:T(8,128)}), f32[1024,3,384]{2,0,1:T(8,128)}) %reduce-scatter.14.cloned.1.call-update) | async-done | bytes 4718608 | tf_op jit(solution)/shard_map/reduce_scatter | solution.py:27
  161.3 31.7 %while.53 = (s32[]{:T(128)}, bf16[2,512,6,64]{1,3,2,0:T(8,128)(2,1)}, f32[2,512,6]{1,2,0:T(8,128)}, s32[2]{0:T(128)S(1)}, s32[1024]{0:T(1024)}, /*index=5*/bf16[...) while((s32[]{:T(128)}, ...), condition=%wide.region_6.7_spmd, body=%wide.region_3.6_spmd.sunk | while | flops 844641280 | bytes 52168988 | solution.py:105
  196.1 27.3 %all-gather.13.cloned.1.call-done = bf16[2048,384]{0,1:T(8,128)(2,1)} async-done(((bf16[1024,384]{0,1:T(8,128)(2,1)}), bf16[2048,384]{0,1:T(8,128)(2,1)}) %all-gather.13.cloned.1.call-update) | async-done | bytes 1572880 | tf_op jit(solution)/shard_map/all_gather | solution.py:31
  256.9 15.5 scatter_custom_fusion
  275.7 22.3 gather_fusion
  313.5 19.0 fusion.43
  361.2 207.2 %reduce-scatter.20.cloned.1.call-done = bf16[640,4,2,1024]{3,0,2,1:T(8,128)(2,1)} async-done(((bf16[1280,4,2,1024]{3,0,2,1:T(8,128)(2,1)}), bf16[640,4,2,1024]{3,0,2,1:T(8,128)(2,1)}) %reduce-scatter.20.cloned.1.call-update) | async-done | bytes 10485776 | tf_op jit(solution)/shard_map/reduce_scatter | solution.py:237
  568.4 14.4 convert_element_type.185
  593.0 77.6 %reduce-scatter.18.cloned.1.call-done = bf16[1024,2,1024]{2,0,1:T(8,128)(2,1)} async-done(((bf16[2048,2,1024]{2,0,1:T(8,128)(2,1)}), bf16[1024,2,1024]{2,0,1:T(8,128)(2,1)}) %reduce-scatter.18.cloned.1.call-update) | async-done | bytes 4194320 | tf_op jit(solution)/shard_map/reduce_scatter | solution.py:231
  682.9 119.1 %all-gather.19.cloned.1.call-done = bf16[1280,4,1024]{2,0,1:T(8,128)(2,1)} async-done(((bf16[640,4,1024]{2,0,1:T(8,128)(2,1)}), bf16[1280,4,1024]{2,0,1:T(8,128)(2,1)}) %all-gather.19.cloned.1.call-update) | async-done | bytes 10485776 | tf_op jit(solution)/shard_map/all_gather | solution.py:265
  810.4 14.0 copy.173
  888.3 29.6 %psum.123 = f32[]{:T(128)} all-reduce(f32[]{:T(128)} %get-tuple-element.478), channel_id=1, replica_groups=mesh['dp'=8,'row'=2,'col'=2] {'dp','col'}, use_global_device_ids=true, to_apply=%region_27.28 | all-reduce | flops 1 | bytes 8 | tf_op jit(solution)/shard_map/psum | solution.py:198
  940.1 15.5 scatter_custom_fusion.2
  956.5 22.4 gather_fusion.3
  1004.2 115.5 %reduce-scatter.26.cloned.1.call-done = bf16[640,4,1024]{2,0,1:T(8,128)(2,1)} async-done(((bf16[1280,4,1024]{2,0,1:T(8,128)(2,1)}), bf16[640,4,1024]{2,0,1:T(8,128)(2,1)}) %reduce-scatter.26.cloned.1.call-update) | async-done | bytes 5242896 | tf_op jit(solution)/shard_map/reduce_scatter | solution.py:298
  1119.7 16.3 fusion.60
  1147.4 77.8 %all-gather.23.cloned.1.call-done = bf16[2048,2,1024]{2,0,1:T(8,128)(2,1)} async-done(((bf16[1024,2,1024]{2,0,1:T(8,128)(2,1)}), bf16[2048,2,1024]{2,0,1:T(8,128)(2,1)}) %all-gather.23.cloned.1.call-update) | async-done | bytes 8388624 | tf_op jit(solution)/shard_map/all_gather | solution.py:315
  1254.5 219.9 %all-gather.25.cloned.1.call-done = bf16[1280,4,2,1024]{3,0,1,2:T(8,128)(2,1)} async-done(((bf16[640,4,2,1024]{3,0,1,2:T(8,128)(2,1)}), bf16[1280,4,2,1024]{3,0,1,2:T(8,128)(2,1)}) %all-gather.25.cloned.1.call-update) | async-done | bytes 20971536 | tf_op jit(solution)/shard_map/all_gather | solution.py:317
  1474.3 18.9 fusion.56
  1493.2 15.0 copy.181
  1589.7 38.6 %reduce-scatter.30.cloned.1.call-done = f32[1024,384]{1,0:T(8,128)} async-done(((f32[2048,384]{1,0:T(8,128)}), f32[1024,384]{1,0:T(8,128)}) %reduce-scatter.30.cloned.1.call-update) | async-done | bytes 1572880 | tf_op jit(solution)/shard_map/reduce_scatter | solution.py:27
  1631.0 90.7 %while.54 = (s32[]{:T(128)}, f32[1024,6,64]{0,2,1:T(8,128)S(1)}, f32[1024,6,64]{0,2,1:T(8,128)}, f32[2,512,6,64]{1,0,3,2:T(2,128)}, s32[2]{0:T(128)S(1)}, /*inde...) while((s32[]{:T(128)}, f32[1024,6,64]{0,2,1:T(8,128)S(1)}, ...), condition=%wide.region_41.42_spmd.clone, body=%wide.region_39.41_spmd.clone.sunk | while | flops 2064200704 | bytes 120179024 | solution.py:150
  1660.7 15.0 dynamic_update_slice.43
  1706.7 15.0 dynamic_update_slice.43
  1750.0 62.8 %all-gather.29.cloned.1.call-done = bf16[2048,3,384]{2,0,1:T(8,128)(2,1)} async-done(((bf16[1024,3,384]{2,0,1:T(8,128)(2,1)}), bf16[2048,3,384]{2,0,1:T(8,128)(2,1)}) %all-gather.29.cloned.1.call-update) | async-done | bytes 4718608 | tf_op jit(solution)/shard_map/all_gather | solution.py:31
  1826.6 13.9 fusion.71
  1848.6 15.5 fusion.65
  1874.3 14.0 psum.131
  1891.2 37.3 %all-reduce = (f32[]{:T(128)}, f32[384]{0:T(512)}, f32[384]{0:T(512)}) all-reduce(f32[]{:T(128)} %get-tuple-element.479, f32[384]{0:T(512)S(1)} %get-tuple-element.474, f32[384]{0:T(512)S(1)} %copy-done.61), channel_id=1, replica_groups=mesh['dp'=8,'row'=2,'col'=2] {'dp','col'}, use_global_device_ids=true, to_apply=%region_25.26 | all-reduce | flops 769 | bytes 6152 | tf_op jit(solution)/shard_map/psum | solution.py:371
  1936.3 349.1 %all-reduce.4.cloned.1.call-done = (bf16[384,2,1024]{2,0,1:T(8,128)(2,1)}, bf16[4,384,2,1024]{3,1,2,0:T(8,128)(2,1)}, bf16[384,3,384]{2,0,1:T(8,128)(2,1)}, bf16...) async-done(((bf16[384,2,1024]{2,0,1:T(8,128)(2,1)}, bf16[4,384,2,1024]{3,1,2,0:T(8,128)(2,1)}, bf16[384,3,384]{2,0,1:T(8,128)(2,1)}, ...) | async-done | bytes 12976144 | tf_op jit(solution)/shard_map/psum | solution.py:379
  2299.1 20.7 copy.195
  (396 shorter events, 556.4 us)
Async XLA Ops:
  7.2 794.8 %copy-start = (bf16[4,1024,384]{2,1,0:T(8,128)(2,1)S(1)}, bf16[4,1024,384]{2,1,0:T(8,128)(2,1)}, u32[]{:S(2)}) copy-start(bf16[4,1024,384]{2,1,0:T(8,128)(2,1)} %param.31) | copy-start | bytes 9437188
  7.2 21.1 all-gather.11.cloned.1.call-start
  15.5 132.1 %reduce-scatter.14.cloned.1.call-start = ((), (), s32[]{:S(2)}) async-start(), calls=%async_computation.12 | async-start | bytes 14155776 | tf_op jit(solution)/shard_map/reduce_scatter | solution.py:27
  36.4 187.0 %all-gather.13.cloned.1.call-start = ((), (), s32[]{:S(2)}) async-start(), calls=%async_computation.13 | async-start | bytes 2359296 | tf_op jit(solution)/shard_map/all_gather | solution.py:31
  39.4 119.3 %copy-start.15 = (f32[1024,64]{0,1:T(8,128)}, f32[1024,64]{0,1:T(8,128)S(1)}, u32[]{:S(2)}) copy-start(f32[1024,64]{0,1:T(8,128)S(1)} %get-tuple-element.556) | copy-start | bytes 786436
  193.0 30.4 %copy-start.22 = (bf16[384,384]{1,0:T(8,128)(2,1)S(1)}, bf16[384,384]{1,0:T(8,128)(2,1)}, u32[]{:S(2)}) copy-start(bf16[384,384]{1,0:T(8,128)(2,1)} %param.26) | copy-start | bytes 884740
  196.0 43.5 %reduce-scatter.16.cloned.1.call-start = ((), (), s32[]{:S(2)}) async-start(), calls=%async_computation.14 | async-start | bytes 4718592 | tf_op jit(solution)/shard_map/reduce_scatter | solution.py:19
  227.7 44.8 %all-gather.15.cloned.1.call-start = ((), (), s32[]{:S(2)}) async-start(), calls=%async_computation.15 | async-start | bytes 2359296 | tf_op jit(solution)/shard_map/all_gather | solution.py:15
  249.4 99.7 %reduce-scatter.34.cloned.1.call-start = ((), (), s32[]{:S(2)}) async-start(), calls=%async_computation.31 | async-start | bytes 786432
  275.5 292.9 %reduce-scatter.20.cloned.1.call-start = ((), (), s32[]{:S(2)}) async-start(), calls=%async_computation.18 | async-start | bytes 31457280 | tf_op jit(solution)/shard_map/reduce_scatter | solution.py:237
  332.5 338.1 %reduce-scatter.18.cloned.1.call-start = ((), (), s32[]{:S(2)}) async-start(), calls=%async_computation.16 | async-start | bytes 12582912 | tf_op jit(solution)/shard_map/reduce_scatter | solution.py:231
  342.7 459.4 %all-gather.19.cloned.1.call-start = ((), (), s32[]{:S(2)}) async-start(), calls=%async_computation.19 | async-start | bytes 15728640 | tf_op jit(solution)/shard_map/all_gather | solution.py:265
  592.9 267.3 %all-gather.17.cloned.1.call-start = ((), (), s32[]{:S(2)}) async-start(), calls=%async_computation.17 | async-start | bytes 6291456 | tf_op jit(solution)/shard_map/all_gather | solution.py:264
  679.8 200.6 %reduce-scatter.22.cloned.1.call-start = ((), (), s32[]{:S(2)}) async-start(), calls=%async_computation.20 | async-start | bytes 4718592 | tf_op jit(solution)/shard_map/reduce_scatter | solution.py:19
  682.9 151.3 %copy-start.38 = (s32[2048]{0:T(1024)}, s32[2048]{0:T(1024)S(1)}, u32[]{:S(2)}) copy-start(s32[2048]{0:T(1024)S(1)} %get-tuple-element.560) | copy-start | bytes 24580
  682.9 163.6 %copy-start.36 = (s32[2048]{0:T(1024)}, s32[2048]{0:T(1024)S(1)}, u32[]{:S(2)}) copy-start(s32[2048]{0:T(1024)S(1)} %get-tuple-element.561) | copy-start | bytes 24580
  868.6 65.4 %all-gather.21.cloned.1.call-start = ((), (), s32[]{:S(2)}) async-start(), calls=%async_computation.21 | async-start | bytes 2359296 | tf_op jit(solution)/shard_map/all_gather | solution.py:15
  921.9 74.7 %reduce-scatter.24.cloned.1.call-start = ((), (), s32[]{:S(2)}) async-start(), calls=%async_computation.22 | async-start | bytes 6291456 | tf_op jit(solution)/shard_map/reduce_scatter | solution.py:295
  940.0 179.7 %reduce-scatter.26.cloned.1.call-start = ((), (), s32[]{:S(2)}) async-start(), calls=%async_computation.24 | async-start | bytes 15728640 | tf_op jit(solution)/shard_map/reduce_scatter | solution.py:298
  996.5 228.7 %all-gather.23.cloned.1.call-start = ((), (), s32[]{:S(2)}) async-start(), calls=%async_computation.23 | async-start | bytes 12582912 | tf_op jit(solution)/shard_map/all_gather | solution.py:315
  1004.2 470.2 %all-gather.25.cloned.1.call-start = ((), (), s32[]{:S(2)}) async-start(), calls=%async_computation.25 | async-start | bytes 31457280 | tf_op jit(solution)/shard_map/all_gather | solution.py:317
  1146.1 79.1 %copy-start.63 = (bf16[384,2,1024]{2,1,0:T(2,128)(2,1)S(1)}, bf16[384,2,1024]{2,1,0:T(2,128)(2,1)}, u32[]{:S(2)}) copy-start(bf16[384,2,1024]{2,1,0:T(2,128)(2,1)} %param.28) | copy-start | bytes 4718596
  1146.1 411.8 %reduce-scatter.28.cloned.1.call-start = ((), (), s32[]{:S(2)}) async-start(), calls=%async_computation.26 | async-start | bytes 4718592 | tf_op jit(solution)/shard_map/reduce_scatter | solution.py:19
  1254.5 286.4 %copy-start.30 = (bf16[2048,4]{0,1:T(4,128)(2,1)}, bf16[2048,4]{0,1:T(4,128)(2,1)S(1)}, u32[]{:S(2)}) copy-start(bf16[2048,4]{0,1:T(4,128)(2,1)S(1)} %all_gather.40) | copy-start | bytes 49156
  1546.2 34.0 %all-gather.27.cloned.1.call-start = ((), (), s32[]{:S(2)}) async-start(), calls=%async_computation.27 | async-start | bytes 2359296 | tf_op jit(solution)/shard_map/all_gather | solution.py:15
  1567.8 60.5 %reduce-scatter.30.cloned.1.call-start = ((), (), s32[]{:S(2)}) async-start(), calls=%async_computation.28 | async-start | bytes 4718592 | tf_op jit(solution)/shard_map/reduce_scatter | solution.py:27
  1584.4 228.4 %all-gather.29.cloned.1.call-start = ((), (), s32[]{:S(2)}) async-start(), calls=%async_computation.29 | async-start | bytes 7077888 | tf_op jit(solution)/shard_map/all_gather | solution.py:31
  1586.6 44.4 %copy-start.4 = (bf16[1024,6,64]{0,2,1:T(8,128)(2,1)S(1)}, bf16[1024,6,64]{0,2,1:T(8,128)(2,1)}, u32[]{:S(2)}) copy-start(bf16[1024,6,64]{0,2,1:T(8,128)(2,1)} %get-tuple-element.802) | copy-start | bytes 2359300
  1750.0 139.0 %reduce-scatter.32.cloned.1.call-start = ((), (), s32[]{:S(2)}) async-start(), calls=%async_computation.30 | async-start | bytes 4718592 | tf_op jit(solution)/shard_map/reduce_scatter | solution.py:19
  1819.8 465.6 %all-reduce.4.cloned.1.call-start = ((), (), s32[]{:S(2)}) async-start(), calls=%async_computation.32 | async-start | bytes 25952256 | tf_op jit(solution)/shard_map/psum | solution.py:379
  1873.3 60.0 %copy-start.50 = (f32[1024]{0:T(1024)S(1)}, f32[1024]{0:T(1024)}, u32[]{:S(2)}) copy-start(f32[1024]{0:T(1024)} %copy-done.49) | copy-start | bytes 12292
  1888.9 44.4 %copy-start.13 = (f32[1024,384]{1,0:T(8,128)S(1)}, f32[1024,384]{1,0:T(8,128)}, u32[]{:S(2)}) copy-start(f32[1024,384]{1,0:T(8,128)} %reduce-scatter.32.cloned.1.call-done) | copy-start | bytes 4718596
  (64 other events, 511.1 us)
Sparse Core Ops, SparseCore 0:
  15.6 12.6 all-gather.10
  36.5 110.9 reduce-scatter.13
  196.2 27.2 all-gather.12
  227.8 11.6 reduce-scatter.15
  249.5 12.0 all-gather.14
  275.6 16.1 reduce-scatter.33
  332.6 235.7 reduce-scatter.19
  571.3 99.2 reduce-scatter.17
  672.8 129.2 all-gather.18
  803.5 56.7 all-gather.16
  868.7 11.6 reduce-scatter.21
  922.0 11.9 all-gather.20
  940.2 54.7 reduce-scatter.23
  997.8 121.8 reduce-scatter.25
  1121.2 103.9 all-gather.22
  1227.2 247.0 all-gather.24
  1546.3 11.6 reduce-scatter.27
  1568.0 12.1 all-gather.26
  1584.5 43.7 reduce-scatter.29
  1750.1 62.6 all-gather.28
  1819.9 11.6 reduce-scatter.31
  1873.4 412.0 all-reduce.3
where the time goes:
time: 2340 us; the launch traced here: 2330 us
  waiting for transfers between devices  1470 us (63%)
  local copies, waits for them, and re-layouts  347 us (15%)
  matrix products  226 us (10%)
  other arithmetic  157 us (7%)
  blocking collectives  108 us (5%)
    psum x1, waiting for transfers between devices, local(): lax.psum(w_shared_up_grad.astype(jnp.bfloat16), 'dp').astype(jnp.float32)  349 us
    all_gather x1, waiting for transfers between devices, local(): lax.all_gather(expert_pre_grad, 'row', axis=0, tiled=True)  220 us
    reduce_scatter x1, waiting for transfers between devices, local(): lax.psum_scatter(expert_part.astype(jnp.bfloat16), 'row', scatter_dimensi...  207 us
    reduce_scatter x2, waiting for transfers between devices, sum_rows(): return lax.psum_scatter(values, 'row', scatter_dimension=0, tiled=True)  147 us
    all_gather x1, waiting for transfers between devices, local(): lax.all_gather(expert_act, 'row', axis=0, tiled=True)  119 us
    reduce_scatter x1, waiting for transfers between devices, local(): lax.psum_scatter(expert_back.astype(jnp.bfloat16), 'row', scatter_dimensi...  115 us
    all_gather x2, waiting for transfers between devices, gather_rows(): return lax.all_gather(values, 'row', axis=0, tiled=True)  90.1 us
    all_gather x1, waiting for transfers between devices, local(): lax.all_gather(shared_pre_grad, 'row', axis=0, tiled=True)  77.8 us
  transfers between devices with their start and end apart: 22, of which 18 were waited for; matrix products, arithmetic and copies ran while one was open for 17% of the time, Pallas kernels for 0%

commit v1 on v0

v1 whole, which is shorter than its diff:
```python
import jax
import jax.numpy as jnp
from jax import lax
from jax.sharding import PartitionSpec as P

D = 768
HEAD_DIM = 64
E = 4
LEN = 1024
ABLOCK = 256
BF = jnp.bfloat16
F32 = jnp.float32


def norm_forward(values, gain_vec):
    rstd_rows = lax.rsqrt(jnp.mean(values * values, axis=1) + 1e-06)
    return (rstd_rows, values * rstd_rows[:, None] * gain_vec)


def norm_backward(values, rstd_rows, gain_vec, incoming):
    scaled = incoming * gain_vec
    inner_sum = jnp.sum(scaled * values, axis=1)
    gain_grad = jnp.sum(incoming * values * rstd_rows[:, None], axis=0)
    result = rstd_rows[:, None] * scaled - values * (rstd_rows**3 * inner_sum / D)[:, None]
    return (result, gain_grad)


def rope_tables(length):
    half_dim = HEAD_DIM // 2
    freqs = 10000.0 ** (-jnp.arange(half_dim, dtype=jnp.float32) * 2.0 / HEAD_DIM)
    angles = jnp.arange(length, dtype=jnp.float32)[:, None] * freqs[None, :]
    angles = jnp.concatenate([angles, angles], axis=1)
    return (jnp.cos(angles), jnp.sin(angles))


def rotate(values, cosine, sine):
    half_dim = values.shape[-1] // 2
    turned = jnp.concatenate([-values[..., half_dim:], values[..., :half_dim]], axis=-1)
    return values * cosine[:, None, :] + turned * sine[:, None, :]


def unrotate(incoming, cosine, sine):
    half_dim = incoming.shape[-1] // 2
    moved = incoming * sine[:, None, :]
    return incoming * cosine[:, None, :] + jnp.concatenate(
        [moved[..., half_dim:], -moved[..., :half_dim]], axis=-1
    )


def allowed_pairs(segment_ids, first_row, query_rows):
    query_pos = first_row + jnp.arange(query_rows)
    key_pos = jnp.arange(segment_ids.shape[0])
    query_seg = lax.dynamic_slice_in_dim(segment_ids, first_row, query_rows, 0)
    return (query_seg[:, None] == segment_ids[None, :]) & (
        key_pos[None, :] // ABLOCK <= query_pos[:, None] // ABLOCK
    )


def attend_forward(query_all, key_all, value_all, segment_ids, query_rows):
    length = key_all.shape[0]
    rescale = HEAD_DIM ** (-0.5)

    def one_block(block_index):
        first_row = block_index * query_rows
        query_part = lax.dynamic_slice_in_dim(query_all, first_row, query_rows, 0)
        scores = (
            jnp.einsum("qhd,khd->hqk", query_part, key_all, preferred_element_type=jnp.float32)
            * rescale
        )
        scores = jnp.where(allowed_pairs(segment_ids, first_row, query_rows)[None], scores, -1e30)
        highest = jnp.max(scores, axis=2, keepdims=True)
        weight = jnp.exp(scores - highest)
        totals = jnp.sum(weight, axis=2, keepdims=True)
        shares_low = (weight / totals).astype(jnp.bfloat16)
        context = jnp.einsum(
            "hqk,khd->qhd", shares_low, value_all, preferred_element_type=jnp.float32
        )
        return (context, jnp.transpose((highest + jnp.log(totals))[:, :, 0]))

    context, log_totals = lax.map(one_block, jnp.arange(length // query_rows))
    return (context.reshape(key_all.shape), log_totals.reshape(length, -1))


def attend_backward(
    query_all, key_all, value_all, context_grad, log_totals, segment_ids, query_rows
):
    length = key_all.shape[0]
    rescale = HEAD_DIM ** (-0.5)

    def one_block(carry, block_index):
        key_grad, value_grad = carry
        first_row = block_index * query_rows
        query_part = lax.dynamic_slice_in_dim(query_all, first_row, query_rows, 0)
        grad_part = lax.dynamic_slice_in_dim(context_grad, first_row, query_rows, 0)
        total_part = jnp.transpose(lax.dynamic_slice_in_dim(log_totals, first_row, query_rows, 0))
        scores = (
            jnp.einsum("qhd,khd->hqk", query_part, key_all, preferred_element_type=jnp.float32)
            * rescale
        )
        scores = jnp.where(allowed_pairs(segment_ids, first_row, query_rows)[None], scores, -1e30)
        shares = jnp.exp(scores - total_part[:, :, None])
        value_grad = value_grad + jnp.einsum(
            "hqk,qhd->khd",
            shares.astype(jnp.bfloat16),
            grad_part,
            preferred_element_type=jnp.float32,
        )
        share_grad = jnp.einsum(
            "qhd,khd->hqk", grad_part, value_all, preferred_element_type=jnp.float32
        )
        centre = jnp.sum(shares * share_grad, axis=2, keepdims=True)
        score_grad = (shares * (share_grad - centre)).astype(jnp.bfloat16)
        query_grad = (
            jnp.einsum("hqk,khd->qhd", score_grad, key_all, preferred_element_type=jnp.float32)
            * rescale
        )
        key_grad = (
            key_grad
            + jnp.einsum("hqk,qhd->khd", score_grad, query_part, preferred_element_type=jnp.float32)
            * rescale
        )
        return ((key_grad, value_grad), query_grad)

    zero_grads = jnp.zeros(key_all.shape, jnp.float32)
    (key_grad, value_grad), query_grad = lax.scan(
        one_block, (zero_grads, zero_grads), jnp.arange(length // query_rows)
    )
    return (query_grad.reshape(key_all.shape), key_grad, value_grad)


def swap(values, axis):
    return lax.ppermute(values, axis, [(0, 1), (1, 0)])


def flip(values):
    half = values.shape[-1] // 2
    return jnp.concatenate([values[..., half:], values[..., :half]], axis=-1)


def dp_pairs(bit):
    n = lax.axis_size("dp")
    return [(i, i ^ (1 << bit)) for i in range(n)]


def dp_bits():
    count = lax.axis_size("dp").bit_length() - 1
    return [0] + list(range(count - 1, 0, -1)) if count else []


def my_bit(bit):
    return (lax.axis_index("dp") >> bit) & 1


def dp_reduce(values, axis):
    n = lax.axis_size("dp")
    count = n.bit_length() - 1
    shape = values.shape
    values = values.reshape(shape[:axis] + (2,) * count + shape[axis + 1 :])
    left = list(range(count - 1, -1, -1))
    for bit in dp_bits():
        at = axis + left.index(bit)
        mine = my_bit(bit)
        keep = lax.dynamic_index_in_dim(values, mine, at, keepdims=False)
        send = lax.dynamic_index_in_dim(values, 1 - mine, at, keepdims=False)
        recv = lax.ppermute(send, "dp", dp_pairs(bit))
        values = (keep.astype(F32) + recv.astype(F32)).astype(BF)
        left.remove(bit)
    return values


def order_pair(first_is_own, own, other, axis, stack=False):
    if stack:
        return jnp.where(first_is_own, jnp.stack([own, other], axis), jnp.stack([other, own], axis))
    return jnp.where(
        first_is_own, jnp.concatenate([own, other], axis), jnp.concatenate([other, own], axis)
    )


def dp_gather(values, axis):
    n = lax.axis_size("dp")
    have = []
    for bit in reversed(dp_bits()):
        have = sorted(have + [bit], reverse=True)
        at = axis + have.index(bit)
        recv = lax.ppermute(values, "dp", dp_pairs(bit))
        values = order_pair(my_bit(bit) == 0, values, recv, at, stack=True)
    shape = values.shape
    count = len(have)
    return values.reshape(shape[:axis] + (n,) + shape[axis + count :])


def silu_parts(values):
    sigma = jax.nn.sigmoid(values)
    return (values * sigma, sigma * (1.0 + values * (1.0 - sigma)))


def spread_tokens(own):
    near = swap(own, "col")
    far = swap(flip(own), "row")
    far_near = swap(far, "col")
    return jnp.stack([own, near, far, far_near])


def collect_tokens(parts):
    recv = swap(jnp.stack([parts[1], parts[3]]).astype(BF), "col").astype(F32)
    own = parts[0] + recv[0]
    far = parts[2] + recv[1]
    return own + swap(flip(far.astype(BF)), "row").astype(F32)


def to_sequence(values, r, c):
    other = lax.ppermute(values, ("row", "col"), [(1, 3), (2, 0)])
    pair = jnp.stack([values, other])
    copied = lax.ppermute(pair, ("row", "col"), [(0, 1), (3, 2)])
    return jnp.where(r == c, pair, copied)


def from_sequence(values, r, c):
    half = values.shape[1] // 2
    own, peer = values[:, :half], values[:, half:]
    diag = r == c
    send = jnp.where(diag, peer, own)
    kept = jnp.where(diag, own, peer)
    recv = swap(send, "col")
    whole = order_pair(c == 0, kept, recv, 0)
    moved = lax.ppermute(whole, ("row", "col"), [(1, 2), (2, 1)])
    return jnp.where(diag, whole, moved)


def local(
    layer_input,
    teacher,
    valid_mask,
    routes,
    segments,
    gain_attn,
    gain_ffn,
    w_qkv,
    w_out,
    w_router,
    w_shared_up,
    w_shared_down,
    w_expert_up,
    w_expert_down,
):
    r = lax.axis_index("row")
    c = lax.axis_index("col")
    n_dp = lax.axis_size("dp")
    rows = layer_input.shape[0]
    part = rows // 2
    half = layer_input.shape[1]
    heads = w_qkv.shape[2] // HEAD_DIM
    ff = w_shared_up.shape[2]
    quarter = ff // 2
    slots = E + 1

    x_pair = to_sequence(layer_input, r, c)
    x_seq = jnp.concatenate([x_pair[0], x_pair[1]], axis=1).astype(F32)
    w_qkv_full = jnp.concatenate([w_qkv, swap(w_qkv, "row")], axis=0)
    w_out_full = jnp.concatenate([w_out, swap(w_out, "row")], axis=1)
    gain_a = jnp.concatenate([gain_attn, swap(gain_attn, "row")])
    gain_f = jnp.concatenate([gain_ffn, swap(gain_ffn, "row")])
    w_r = jnp.concatenate([w_router, swap(w_router, "row")])
    t_pair = to_sequence(teacher, r, c)
    t_seq = jnp.concatenate([t_pair[0], t_pair[1]], axis=1)
    teacher_own = lax.dynamic_slice_in_dim(t_seq, c * part, part, 0).astype(F32)
    valid_other = swap(valid_mask, "col")
    valid_seq = jnp.where(r == c, valid_mask, valid_other).astype(F32)
    valid_own = lax.dynamic_slice_in_dim(valid_seq, c * part, part, 0)
    count = lax.psum(jnp.sum(valid_own), ("dp", "row", "col"))
    seg = lax.dynamic_slice_in_dim(segments, r, 1, 0)[0]
    route_blocks = routes.reshape(2, 2, part, 2)
    route_blocks = jnp.where(r == 0, route_blocks, route_blocks[::-1])
    route_blocks = jnp.where(c == 0, route_blocks, route_blocks[:, ::-1]).reshape(4 * part, 2)
    picks = (route_blocks[:, :, None] == jnp.arange(E, dtype=jnp.int32)[None, None, :]).astype(F32)

    up_all = jnp.concatenate([w_shared_up[None], w_expert_up], axis=0)
    down_all = jnp.concatenate([w_shared_down[None], w_expert_down], axis=0)
    up_keep = lax.dynamic_slice_in_dim(up_all, r * quarter, quarter, 3)
    up_send = lax.dynamic_slice_in_dim(up_all, (1 - r) * quarter, quarter, 3)
    down_keep = lax.dynamic_slice_in_dim(down_all, r * quarter, quarter, 1)
    down_send = lax.dynamic_slice_in_dim(down_all, (1 - r) * quarter, quarter, 1)
    w_up = jnp.concatenate([up_keep, swap(up_send, "row")], axis=1)
    w_down = jnp.concatenate([down_keep, swap(down_send, "row")], axis=2)

    rstd_seq, normed = norm_forward(x_seq, gain_a)
    normed_attn = normed.astype(BF)
    qkv_pre = jnp.einsum("td,dke->tke", normed_attn, w_qkv_full, preferred_element_type=F32)
    qkv_pre = qkv_pre.reshape(rows, 3, heads, HEAD_DIM)
    cosine, sine = rope_tables(rows)
    queries = rotate(qkv_pre[:, 0], cosine, sine).astype(BF)
    keys_rot = rotate(qkv_pre[:, 1], cosine, sine).astype(BF)
    values_low = qkv_pre[:, 2].astype(BF)
    query_rows = min(512, rows)
    context, log_totals = attend_forward(queries, keys_rot, values_low, seg, query_rows)
    context_low = context.reshape(rows, -1).astype(BF)
    attention = jnp.dot(context_low, w_out_full, preferred_element_type=F32)
    att_halves = attention.reshape(2, part, D)
    att_keep = lax.dynamic_index_in_dim(att_halves, c, 0, keepdims=False)
    att_send = lax.dynamic_index_in_dim(att_halves, 1 - c, 0, keepdims=False)
    x_own = lax.dynamic_slice_in_dim(x_seq, c * part, part, 0)
    rstd_attn = lax.dynamic_slice_in_dim(rstd_seq, c * part, part, 0)
    hidden = x_own + att_keep + swap(att_send.astype(BF), "col").astype(F32)

    rstd_ffn, normed = norm_forward(hidden, gain_f)
    normed_low = normed.astype(BF)
    tokens = spread_tokens(normed_low).reshape(4 * part, D)
    logits = jnp.dot(tokens, w_r, preferred_element_type=F32)
    chosen = jnp.sum(picks * logits[:, None, :], axis=2)
    chosen = chosen - jnp.max(chosen, axis=1, keepdims=True)
    gates = jnp.exp(chosen)
    gates = gates / jnp.sum(gates, axis=1, keepdims=True)
    mixing = jnp.sum(picks * gates[:, :, None], axis=1)
    mix_all = jnp.concatenate([jnp.ones((4 * part, 1), F32), mixing], axis=1).T
    pre = [
        jnp.dot(tokens, w_up[e].reshape(D, 2 * quarter), preferred_element_type=F32).astype(BF)
        for e in range(slots)
    ]
    acts = []
    for e in range(slots):
        gate_pre, up_pre = pre[e][:, :quarter].astype(F32), pre[e][:, quarter:].astype(F32)
        act = gate_pre * jax.nn.sigmoid(gate_pre) * up_pre
        acts.append((act * mix_all[e][:, None]).astype(BF))
    act_all = jnp.concatenate(acts, axis=1)
    branch = jnp.dot(act_all, w_down.reshape(slots * quarter, D), preferred_element_type=F32)
    output = hidden + collect_tokens(branch.reshape(4, part, D))

    error = output - teacher_own
    loss_part = jnp.sum(valid_own * jnp.sum(error * error, axis=1))
    total_tokens = part * 4 * n_dp
    grad_out = total_tokens / count * valid_own[:, None] * error

    grads = spread_tokens(grad_out.astype(BF)).reshape(4 * part, D)
    down_grad = jnp.dot(act_all.T, grads, preferred_element_type=F32).astype(BF)
    act_back = jnp.dot(
        grads, w_down.reshape(slots * quarter, D).T, preferred_element_type=F32
    ).astype(BF)
    pre_grads = []
    gate_sums = []
    for e in range(slots):
        gate_pre, up_pre = pre[e][:, :quarter].astype(F32), pre[e][:, quarter:].astype(F32)
        back = act_back[:, e * quarter : (e + 1) * quarter].astype(F32)
        act_silu, slope = silu_parts(gate_pre)
        if e:
            gate_sums.append(jnp.sum(back * act_silu * up_pre, axis=1))
        back = back * mix_all[e][:, None]
        pre_grads.append(
            jnp.concatenate([back * up_pre * slope, back * act_silu], axis=1).astype(BF)
        )
    up_grads = [
        jnp.dot(tokens.T, pre_grads[e], preferred_element_type=F32).astype(BF)
        for e in range(slots)
    ]
    input_part = jnp.zeros((4 * part, D), F32)
    for e in range(slots):
        input_part = input_part + jnp.dot(
            pre_grads[e], w_up[e].reshape(D, 2 * quarter).T, preferred_element_type=F32
        )
    normed_ffn_grad = collect_tokens(input_part.reshape(4, part, D))
    gate_parts = jnp.stack(gate_sums, axis=0).reshape(E, 4, part)
    recv = swap(jnp.stack([gate_parts[:, 1], gate_parts[:, 3]]), "col")
    gate_grad = gate_parts[:, 0] + recv[0] + swap(gate_parts[:, 2] + recv[1], "row")
    mix_own = mixing[:part].T
    centre = jnp.sum(mix_own * gate_grad, axis=0, keepdims=True)
    logit_grad = (mix_own * (gate_grad - centre)).T.astype(BF)
    normed_ffn_grad = normed_ffn_grad + jnp.dot(logit_grad, w_r.T, preferred_element_type=F32)
    router_grad = jnp.dot(normed_low.T, logit_grad, preferred_element_type=F32)
    hidden_back, gain_ffn_grad = norm_backward(hidden, rstd_ffn, gain_f, normed_ffn_grad)
    hidden_grad = grad_out + hidden_back

    owner_f = quarter // n_dp
    owner_d = half // n_dp
    down_split = dp_reduce(down_grad.reshape(slots, n_dp, owner_f, 2, half), 1)
    down_own = down_split[:, :, 0]
    down_peer = swap(down_split[:, :, 1], "row")
    up_split = dp_reduce(jnp.stack(up_grads).reshape(slots, 2, n_dp, owner_d, 2 * quarter), 2)
    up_own = up_split[:, 0]
    up_peer = swap(up_split[:, 1], "row")
    down_out = dp_gather(jnp.stack([down_own, down_peer], 1), 2).reshape(slots, 2, quarter, half)
    down_out = jnp.where(r == 0, down_out, down_out[:, ::-1]).astype(F32)
    down_out = down_out.reshape(slots, ff, half)
    up_out = dp_gather(jnp.stack([up_own, up_peer], 1), 2)
    up_out = up_out.reshape(slots, 2, half, 2, quarter)
    up_out = order_pair(r == 0, up_out[:, 0], up_out[:, 1], 3).astype(F32)

    low_own = hidden_grad.astype(BF)
    low_seq = order_pair(c == 0, low_own, swap(low_own, "col"), 0)
    w_out_grad = jnp.dot(context_low.T, low_seq, preferred_element_type=F32).astype(BF)
    context_grad = jnp.dot(low_seq, w_out_full.T, preferred_element_type=F32)
    context_grad = context_grad.astype(BF).reshape(rows, heads, HEAD_DIM)
    query_grad, key_grad, value_grad = attend_backward(
        queries, keys_rot, values_low, context_grad, log_totals, seg, query_rows
    )
    query_grad = unrotate(query_grad, cosine, sine)
    key_grad = unrotate(key_grad, cosine, sine)
    qkv_grad = jnp.stack((query_grad, key_grad, value_grad), axis=1).reshape(rows, -1).astype(BF)
    w_qkv_grad = jnp.dot(normed_attn.T, qkv_grad, preferred_element_type=F32).astype(BF)
    back_part = jnp.dot(qkv_grad, w_qkv_full.reshape(D, -1).T, preferred_element_type=F32)
    back_halves = back_part.reshape(2, part, D)
    back_keep = lax.dynamic_index_in_dim(back_halves, c, 0, keepdims=False)
    back_send = lax.dynamic_index_in_dim(back_halves, 1 - c, 0, keepdims=False)
    normed_attn_grad = back_keep + swap(back_send.astype(BF), "col").astype(F32)
    input_back, gain_attn_grad = norm_backward(x_own, rstd_attn, gain_a, normed_attn_grad)
    input_grad = hidden_grad + input_back

    out_split = dp_reduce(w_out_grad.reshape(n_dp, owner_d, 2, half), 0)
    out_sum = out_split[:, 0].astype(F32) + swap(out_split[:, 1], "row").astype(F32)
    out_sum = dp_gather(out_sum.astype(BF), 0).reshape(half, half).astype(F32)
    qkv_split = dp_reduce(w_qkv_grad.reshape(2, n_dp, owner_d, 3 * half), 1)
    qkv_sum = qkv_split[0].astype(F32) + swap(qkv_split[1], "row").astype(F32)
    qkv_sum = dp_gather(qkv_sum.astype(BF), 0).reshape(half, 3, half).astype(F32)

    small = jnp.concatenate([gain_attn_grad[None], gain_ffn_grad[None], router_grad.T], axis=0)
    small = jnp.where(r == 0, small, flip(small))
    small = jnp.concatenate([small.reshape(-1), loss_part[None]])
    small = lax.psum(small, ("dp", "row", "col"))
    loss = small[-1] / (2.0 * count)
    small = small[:-1].reshape(E + 2, D)
    small = lax.dynamic_slice_in_dim(small, r * half, half, 1)
    return (
        from_sequence(output, r, c),
        loss,
        from_sequence(input_grad, r, c),
        small[0],
        small[1],
        qkv_sum,
        out_sum,
        small[2:].T,
        up_out[0],
        down_out[0],
        up_out[1:],
        down_out[1:],
    )


def solution(mesh):
    return jax.shard_map(
        local,
        mesh=mesh,
        in_specs=(
            P(("dp", "col"), "row"),
            P(("dp", "col"), "row"),
            P(("dp", "col")),
            P("dp", None),
            P("dp", None),
            P("row"),
            P("row"),
            P("row", None, "col"),
            P("col", "row"),
            P("row", None),
            P("row", None, "col"),
            P("col", "row"),
            P(None, "row", None, "col"),
            P(None, "col", "row"),
        ),
        out_specs=(
            P(("dp", "col"), "row"),
            P(),
            P(("dp", "col"), "row"),
            P("row"),
            P("row"),
            P("row", None, "col"),
            P("col", "row"),
            P("row", None),
            P("row", None, "col"),
            P("col", "row"),
            P(None, "row", None, "col"),
            P(None, "col", "row"),
        ),
        check_vma=False,
    )
```

time: 2340 us -> 1280 us (0.55)
  waiting for transfers between devices: 1470 us -> 521 us
  local copies, waits for them, and re-layouts: 347 us -> 166 us
  starting transfers between devices: 3.2 us -> 75.1 us
  other arithmetic: 157 us -> 196 us
  blocking collectives: 108 us -> 82.7 us
  matrix products: 226 us -> 201 us
    reduce_scatter x10 -> x0, waiting for transfers between devices: 572 us -> none  [the longest x1 207 us: local(): lax.psum_scatter(expert_part.astype(jnp.bfloat16), 'row', scatter_dimensi...]
    all_gather x10 -> x0, waiting for transfers between devices: 545 us -> none  [the longest x1 220 us: local(): lax.all_gather(expert_pre_grad, 'row', axis=0, tiled=True)]
    ppermute x0 -> x59, waiting for transfers between devices: none -> 521 us  [the longest x12 282 us: dp_gather(): recv = lax.ppermute(values, 'dp', dp_pairs(bit))]
    psum x1 -> x0, waiting for transfers between devices: 349 us -> none  [local(): lax.psum(w_shared_up_grad.astype(jnp.bfloat16), 'dp').astype(jnp.float32)]
    gather x10 -> x0, local copies, waits for them, and re-layouts: 112 us -> none  [the longest x2 29.9 us: local(): grad_rows[owner] * filled[:, None].astype(jnp.bfloat16)]
    ppermute x0 -> x59, starting transfers between devices: none -> 75.1 us  [the longest x29 35.8 us: swap(): return lax.ppermute(values, axis, [(0, 1), (1, 0)])]
    scatter x3 -> x0, local copies, waits for them, and re-layouts: 39.1 us -> none  [the longest x1 15.5 us: slot_tables(): filled = jnp.zeros((total_slots,), jnp.int32).at[flat_of.reshape(-1)].set(1)]
    reshape x9 -> x4, local copies, waits for them, and re-layouts: 43.1 us -> 6.8 us  [the longest x2 6.05 us: attend_backward(): return (query_grad.reshape(key_all.shape), key_grad, value_grad)]
  transfers between devices with their start and end apart: 22 -> 59, of which waited for: 18 -> 20; matrix products, arithmetic and copies ran while one was open for 17% -> 39% of each run, Pallas kernels for 0% -> 0%
where the time goes in v1:
time: 1280 us; the launch traced here: 1260 us
  waiting for transfers between devices  521 us (41%)
  matrix products  201 us (16%)
  other arithmetic  196 us (15%)
  local copies, waits for them, and re-layouts  166 us (13%)
  blocking collectives  82.7 us (6%)
  starting transfers between devices  75.1 us (6%)
  loops' own time  13.5 us (1%)
    ppermute x12, waiting for transfers between devices, dp_gather(): recv = lax.ppermute(values, 'dp', dp_pairs(bit))  282 us
    ppermute x29, waiting for transfers between devices, swap(): return lax.ppermute(values, axis, [(0, 1), (1, 0)])  134 us
    ppermute x12, waiting for transfers between devices, dp_reduce(): recv = lax.ppermute(send, 'dp', dp_pairs(bit))  94.7 us
    psum x1, blocking collectives, local(): small = lax.psum(small, ('dp', 'row', 'col'))  44 us
    dot_general x5, matrix products, local(): jnp.dot(pre_grads[e], w_up[e].reshape(D, 2 * quarter).T, preferred_elemen...  40.3 us
    psum x1, blocking collectives, local(): count = lax.psum(jnp.sum(valid_own), ('dp', 'row', 'col'))  38.7 us
    ppermute x29, starting transfers between devices, swap(): return lax.ppermute(values, axis, [(0, 1), (1, 0)])  35.8 us
    unnamed x270, local copies, waits for them, and re-layouts  33.1 us
  transfers between devices with their start and end apart: 59, of which 20 were waited for; matrix products, arithmetic and copies ran while one was open for 39% of the time, Pallas kernels for 0%

profile of v1, /device:TPU:27, one launch (start us, length us, event | category | flops | bytes accessed | tf_op | source)
XLA Modules:
  0.0 1260.6 jit_solution(10861319898375349498)
XLA Ops:
  7.0 9.4 collective-permute-done
  20.2 10.5 fusion.100
  44.1 14.5 %collective-permute-done.3 = bf16[384,3,384]{0,2,1:T(8,128)(2,1)S(1)} collective-permute-done((bf16[384,3,384]{0,2,1:T(8,128)(2,1)S(1)}, bf16[384,3,384]{0,2,1:T(8,128)(2,1)S(1)}, u32[]{:S(2)}, u32[]{:S(2)}) %collective-permute-start.3) | collective-permute-done | bytes 884768 | tf_op jit(solution)/shard_map/ppermute | solution.py:132
  64.8 37.5 %while.33 = (s32[]{:T(128)}, bf16[2,512,6,64]{1,3,2,0:T(8,128)(2,1)S(1)}, f32[2,512,6]{1,2,0:T(8,128)S(1)}, s32[2]{0:T(128)S(1)}, s32[1024]{0:T(1024)S(1)}, /*in...) while((s32[]{:T(128)}, ...), condition=%wide.region_4.5_spmd, body=%wide.region_1.0_spmd.sunk | while | flops 844641280 | bytes 42739924 | solution.py:80
  127.5 57.6 %collective-permute-done.12 = bf16[5,512,384]{2,1,0:T(8,128)(2,1)} collective-permute-done((bf16[5,512,384]{2,1,0:T(8,128)(2,1)}, bf16[5,512,384]{2,1,0:T(8,128)(2,1)}, u32[]{:S(2)}, u32[]{:S(2)}) %collective-permute-start.12) | collective-permute-done | bytes 1966112 | tf_op jit(solution)/shard_map/ppermute | solution.py:132
  192.7 17.9 %collective-permute-done.8 = bf16[512,768]{1,0:T(8,128)(2,1)} collective-permute-done((bf16[512,768]{1,0:T(8,128)(2,1)}, bf16[512,768]{1,0:T(8,128)(2,1)}, u32[]{:S(2)}, u32[]{:S(2)}) %collective-permute-start.8) | collective-permute-done | bytes 786464 | tf_op jit(solution)/shard_map/ppermute | solution.py:132
  211.8 11.5 pad_maximum_fusion.29
  270.3 11.9 fusion.210
  291.5 15.7 %collective-permute-done.14 = bf16[512,768]{1,0:T(8,128)(2,1)S(1)} collective-permute-done((bf16[512,768]{1,0:T(8,128)(2,1)S(1)}, bf16[512,768]{1,0:T(8,128)(2,1)S(1)}, u32[]{:S(2)}, u32[]{:S(2)}) %collective-permute-start.14) | collective-permute-done | bytes 786464 | tf_op jit(solution)/shard_map/ppermute | solution.py:132
  309.5 38.7 %psum.14 = f32[]{:T(128)} all-reduce(f32[]{:T(128)} %get-tuple-element.427), channel_id=1, replica_groups=mesh['dp'=8,'row'=2,'col'=2] {'dp','row','col'}, use_global_device_ids=true, to_apply=%region_11.12 | all-reduce | flops 1 | bytes 8 | tf_op jit(solution)/shard_map/psum | solution.py:270
  355.6 13.1 %collective-permute-done.21 = bf16[512,768]{1,0:T(8,128)(2,1)} collective-permute-done((bf16[512,768]{1,0:T(8,128)(2,1)S(1)}, bf16[512,768]{1,0:T(8,128)(2,1)}, u32[]{:S(2)}, u32[]{:S(2)}) %collective-permute-start.21) | collective-permute-done | bytes 786464 | tf_op jit(solution)/shard_map/ppermute | solution.py:132
  385.3 12.6 convolution_convert_fusion.1
  397.8 8.9 convolution_convert_fusion
  412.6 10.2 fusion.96
  497.2 18.1 %fusion.211 = (bf16[2048,768]{1,0:T(8,128)(2,1)}, f32[2048,768]{1,0:T(8,128)}) fusion(bf16[768,1024]{1,0:T(8,128)(2,1)} %bitcast.489, bf16[2048,512]{0,1:T(8,128)(2,1)} %get-tuple-element.484, bf16[2048,512]{0,1:T(8,128)(2,1)} %get-tuple-element.483, f32[2048,768]{1,0:T(8,128)} %fusion.107, f32[2048,768]{1,0:T(8,128)} %fusion.109, ...), kind=kOutput, calls=%fused_computation.499 | convolution fusion | flops 3237478400 | bytes 40370176 | tf_op jit(solution)/shard_map/dot_general | solution.py:356
  538.5 13.7 %collective-permute-done.24 = bf16[512,768]{1,0:T(8,128)(2,1)S(1)} collective-permute-done((bf16[512,768]{1,0:T(8,128)(2,1)S(1)}, bf16[512,768]{1,0:T(8,128)(2,1)S(1)}, u32[]{:S(2)}, u32[]{:S(2)}) %collective-permute-start.24) | collective-permute-done | bytes 786464 | tf_op jit(solution)/shard_map/ppermute | solution.py:132
  560.2 21.4 %collective-permute-done.53 = bf16[5,2,64,2,384]{4,2,0,3,1:T(8,128)(2,1)S(1)} collective-permute-done((bf16[5,2,64,2,384]{4,2,0,3,1:T(8,128)(2,1)S(1)}, bf16[5,2,64,2,384]{4,2,0,3,1:T(8,128)(2,1)S(1)}, u32[]{:S(2)}, u32[]{:S(2)}) %collective-permute-start.53) | collective-permute-done | bytes 983072 | tf_op jit(solution)/shard_map/ppermute | solution.py:165
  585.7 93.5 %while.34 = (s32[]{:T(128)}, f32[1024,6,64]{0,2,1:T(8,128)S(1)}, f32[1024,6,64]{0,2,1:T(8,128)}, f32[2,512,6,64]{1,0,3,2:T(2,128)}, s32[2]{0:T(128)S(1)}, /*inde...) while((s32[]{:T(128)}, f32[1024,6,64]{0,2,1:T(8,128)S(1)}, ...), condition=%wide.region_20.21_spmd.clone, body=%wide.region_18.20_spmd.clone.sunk | while | flops 2064200704 | bytes 110733576 | solution.py:125
  596.3 8.8 multiply_reduce_fusion.11
  617.3 14.9 %dynamic_update_slice.31 = f32[2,512,6,64]{1,0,3,2:T(2,128)} dynamic-update-slice(f32[2,512,6,64]{1,0,3,2:T(2,128)} %get-tuple-element.773, f32[1,512,6,64]{1,0,3,2:T(1,128)S(1)} %copy.169, s32[]{:T(128)S(6)} %copy.194, s32[]{:T(128)} %constant.314.clone.1..sunk.1, s32[]{:T(128)} %constant.314.clone.1..sunk.1, s32[]{:T(128)} %constant.314.clone.1..sunk.1) | dynamic-update-slice | bytes 1572868 | tf_op jit(solution)/shard_map/while/body/jit(dynamic_update_index_in_dim)/dynamic_update_slice | solution.py:80
  664.1 14.9 %dynamic_update_slice.31 = f32[2,512,6,64]{1,0,3,2:T(2,128)} dynamic-update-slice(f32[2,512,6,64]{1,0,3,2:T(2,128)} %get-tuple-element.773, f32[1,512,6,64]{1,0,3,2:T(1,128)S(1)} %copy.169, s32[]{:T(128)S(6)} %copy.194, s32[]{:T(128)} %constant.314.clone.1..sunk.1, s32[]{:T(128)} %constant.314.clone.1..sunk.1, s32[]{:T(128)} %constant.314.clone.1..sunk.1) | dynamic-update-slice | bytes 1572868 | tf_op jit(solution)/shard_map/while/body/jit(dynamic_update_index_in_dim)/dynamic_update_slice | solution.py:80
  736.6 30.4 %collective-permute-done.42 = bf16[48,384]{1,0:T(8,128)(2,1)S(1)} collective-permute-done((bf16[48,384]{1,0:T(8,128)(2,1)S(1)}, bf16[48,384]{1,0:T(8,128)(2,1)S(1)}, u32[]{:S(2)}, u32[]{:S(2)}) %collective-permute-start.42) | collective-permute-done | bytes 36896 | tf_op jit(solution)/shard_map/ppermute | solution.py:185
  770.0 45.6 %collective-permute-done.43 = bf16[2,48,384]{2,1,0:T(8,128)(2,1)S(1)} collective-permute-done((bf16[2,48,384]{2,1,0:T(8,128)(2,1)S(1)}, bf16[2,48,384]{2,1,0:T(8,128)(2,1)S(1)}, u32[]{:S(2)}, u32[]{:S(2)}) %collective-permute-start.43) | collective-permute-done | bytes 73760 | tf_op jit(solution)/shard_map/ppermute | solution.py:185
  824.3 17.8 %collective-permute-done.47 = bf16[5,2,48,1024]{3,2,1,0:T(8,128)(2,1)} collective-permute-done((bf16[5,2,48,1024]{3,2,1,0:T(8,128)(2,1)}, bf16[5,2,48,1024]{3,2,1,0:T(8,128)(2,1)}, u32[]{:S(2)}, u32[]{:S(2)}) %collective-permute-start.47) | collective-permute-done | bytes 983072 | tf_op jit(solution)/shard_map/ppermute | solution.py:165
  846.3 44.0 %psum.15 = f32[4609]{0:T(1024)S(1)} all-reduce(f32[4609]{0:T(1024)S(1)} %pad_maximum_fusion.43), channel_id=1, replica_groups=mesh['dp'=8,'row'=2,'col'=2] {'dp','row','col'}, use_global_device_ids=true, to_apply=%region_25.26 | all-reduce | flops 4609 | bytes 36872 | tf_op jit(solution)/shard_map/psum | solution.py:416
  905.7 35.0 %collective-permute-done.49 = bf16[5,2,48,1024]{3,2,0,1:T(8,128)(2,1)S(1)} collective-permute-done((bf16[5,2,48,1024]{3,2,0,1:T(8,128)(2,1)S(1)}, bf16[5,2,48,1024]{3,2,0,1:T(8,128)(2,1)S(1)}, u32[]{:S(2)}, u32[]{:S(2)}) %collective-permute-start.49) | collective-permute-done | bytes 983072 | tf_op jit(solution)/shard_map/ppermute | solution.py:185
  945.8 51.2 %collective-permute-done.33 = bf16[2,48,1152]{2,1,0:T(8,128)(2,1)S(1)} collective-permute-done((bf16[2,48,1152]{2,1,0:T(8,128)(2,1)S(1)}, bf16[2,48,1152]{2,1,0:T(8,128)(2,1)S(1)}, u32[]{:S(2)}, u32[]{:S(2)}) %collective-permute-start.33) | collective-permute-done | bytes 221216 | tf_op jit(solution)/shard_map/ppermute | solution.py:165
  1004.6 43.5 %collective-permute-done.50 = bf16[5,2,2,48,1024]{4,3,0,1,2:T(8,128)(2,1)S(1)} collective-permute-done((bf16[5,2,2,48,1024]{4,3,0,1,2:T(8,128)(2,1)S(1)}, bf16[5,2,2,48,1024]{4,3,0,1,2:T(8,128)(2,1)S(1)}, u32[]{:S(2)}, u32[]{:S(2)}) %collective-permute-start.50) | collective-permute-done | bytes 1966112 | tf_op jit(solution)/shard_map/ppermute | solution.py:185
  1056.3 10.5 collective-permute-done.36
  1071.0 116.8 %collective-permute-done.37 = bf16[2,2,48,1152]{3,2,1,0:T(8,128)(2,1)S(1)} collective-permute-done((bf16[2,2,48,1152]{3,2,1,0:T(8,128)(2,1)S(1)}, bf16[2,2,48,1152]{3,2,1,0:T(8,128)(2,1)S(1)}, u32[]{:S(2)}, u32[]{:S(2)}) %collective-permute-start.37) | collective-permute-done | bytes 442400 | tf_op jit(solution)/shard_map/ppermute | solution.py:185
  1215.9 13.8 %select_n.575 = bf16[5,2,384,2,512]{4,3,2,0,1:T(2,128)(2,1)} reshape(bf16[5,2,2,2,2,48,1024]{6,5,4,3,2,0,1:T(8,128)(2,1)} %copy.113) | data formatting | bytes 15728640 | tf_op jit(solution)/shard_map/jit(_where)/select_n | solution.py:173
  1238.4 13.3 %fusion.41 = f32[5,384,2,1024]{3,2,1,0:T(2,128)S(1)} fusion(pred[]{:T(512)S(6)} %eq.100, bf16[5,384,2,512]{3,2,1,0:T(2,128)(2,1)} %get-tuple-element.502, bf16[5,384,2,512]{3,2,1,0:T(2,128)(2,1)} %get-tuple-element.501), kind=kLoop, calls=%fused_computation.73 | loop fusion | flops 39321600 | bytes 23592960 | tf_op jit(solution)/shard_map/convert_element_type | solution.py:384
  (631 shorter events, 494.6 us)
Async XLA Ops:
  4.1 109.2 %collective-permute-start.6 = (f32[384]{0:T(512)}, f32[384]{0:T(512)}, u32[]{:S(2)}, u32[]{:S(2)}) collective-permute-start(f32[384]{0:T(512)} %param.24), channel_id=1, source_target_pairs={{0,2},{2,0},{1,3},{3,1},{4,6},{6,4},{5,7},{7,5},{8,10},{10,8},{9,1... | collective-permute-start | bytes 4616 | tf_op jit(solution)/shard_map/ppermute | solution.py:132
  5.5 121.3 %collective-permute-start.11 = (bf16[384,4]{0,1:T(4,128)(2,1)}, bf16[384,4]{0,1:T(4,128)(2,1)}, u32[]{:S(2)}, u32[]{:S(2)}) collective-permute-start(bf16[384,4]{0,1:T(4,128)(2,1)} %param.27), channel_id=1, source_target_pairs={{0,2},{2,0},{1,3},{3,1},{4,6},{6,4},{5,7},{7,5},{8,10},{10,8},{9,1... | collective-permute-start | bytes 9224 | tf_op jit(solution)/shard_map/ppermute | solution.py:132
  5.6 34.4 %collective-permute-start.4 = (bf16[384,384]{1,0:T(8,128)(2,1)}, bf16[384,384]{1,0:T(8,128)(2,1)}, u32[]{:S(2)}, u32[]{:S(2)}) collective-permute-start(bf16[384,384]{1,0:T(8,128)(2,1)} %param.26), channel_id=1, source_target_pairs={{0,2},{2,0},{1,3},{3,1},{4,6},{6,4},{5,7},{7,5},{8,10},{10,8},{9,1... | collective-permute-start | bytes 884744 | tf_op jit(solution)/shard_map/ppermute | solution.py:132
  40.0 171.8 %collective-permute-start.10 = (bf16[5,384,2,512]{3,2,1,0:T(2,128)(2,1)}, bf16[5,384,2,512]{3,2,1,0:T(2,128)(2,1)}, u32[]{:S(2)}, u32[]{:S(2)}) collective-permute-start(bf16[5,384,2,512]{3,2,1,0:T(2,128)(2,1)} %get-tuple-element.508), channel_id=1, source_target_pairs={{0,2},{2,0},{1,3},{3,1},{4,6},{6,4},{5,7},{7,5},{8,10},{10,8},{9,1... | collective-permute-start | bytes 11796488 | tf_op jit(solution)/shard_map/ppermute | solution.py:132
  111.2 74.0 %collective-permute-start.12 = (bf16[5,512,384]{2,1,0:T(8,128)(2,1)}, bf16[5,512,384]{2,1,0:T(8,128)(2,1)}, u32[]{:S(2)}, u32[]{:S(2)}) collective-permute-start(bf16[5,512,384]{2,1,0:T(8,128)(2,1)} %get-tuple-element.517), channel_id=1, source_target_pairs={{0,2},{2,0},{1,3},{3,1},{4,6},{6,4},{5,7},{7,5},{8,10},{10,8},{9,1... | collective-permute-start | bytes 5898248 | tf_op jit(solution)/shard_map/ppermute | solution.py:132
  113.2 169.3 %collective-permute-start.18 = (bf16[1024,384]{1,0:T(8,128)(2,1)}, bf16[1024,384]{1,0:T(8,128)(2,1)}, u32[]{:S(2)}, u32[]{:S(2)}) collective-permute-start(bf16[1024,384]{1,0:T(8,128)(2,1)} %param.19), channel_id=1, source_target_pairs={{1,3},{2,0},{5,7},{6,4},{9,11},{10,8},{13,15},{14,12},{17,19},{18,... | collective-permute-start | bytes 2359304 | tf_op jit(solution)/shard_map/ppermute | solution.py:212
  124.8 85.8 %collective-permute-start.8 = (bf16[512,768]{1,0:T(8,128)(2,1)}, bf16[512,768]{1,0:T(8,128)(2,1)}, u32[]{:S(2)}, u32[]{:S(2)}) collective-permute-start(bf16[512,768]{1,0:T(8,128)(2,1)} %pad_maximum_fusion.35), channel_id=1, source_target_pairs={{0,2},{2,0},{1,3},{3,1},{4,6},{6,4},{5,7},{7,5},{8,10},{10,8},{9,1... | collective-permute-start | bytes 2359304 | tf_op jit(solution)/shard_map/ppermute | solution.py:132
  189.1 41.0 %collective-permute-start.7 = (bf16[512,768]{1,0:T(8,128)(2,1)S(1)}, bf16[512,768]{1,0:T(8,128)(2,1)S(1)}, u32[]{:S(2)}, u32[]{:S(2)}) collective-permute-start(bf16[512,768]{1,0:T(8,128)(2,1)S(1)} %copy-done.36), channel_id=1, source_target_pairs={{0,1},{1,0},{2,3},{3,2},{4,5},{5,4},{6,7},{7,6},{8,9},{9,8},{10,11... | collective-permute-start | bytes 2359304 | tf_op jit(solution)/shard_map/ppermute | solution.py:132
  380.8 176.1 %collective-permute-start.16 = (f32[1024,384]{1,0:T(8,128)}, f32[1024,384]{1,0:T(8,128)}, u32[]{:S(2)}, u32[]{:S(2)}) collective-permute-start(f32[1024,384]{1,0:T(8,128)} %maximum_select_fusion.8), channel_id=1, source_target_pairs={{1,2},{2,1},{5,6},{6,5},{9,10},{10,9},{13,14},{14,13},{17,18},{18,... | collective-permute-start | bytes 4718600 | tf_op jit(solution)/shard_map/ppermute | solution.py:226
  484.5 49.5 %collective-permute-start.52 = (bf16[5,2,2,64,2,384]{5,3,0,4,2,1:T(8,128)(2,1)}, bf16[5,2,2,64,2,384]{5,3,0,4,2,1:T(8,128)(2,1)}, u32[]{:S(2)}, u32[]{:S(2)}) collective-permute-start(bf16[5,2,2,64,2,384]{5,3,0,4,2,1:T(8,128)(2,1)} %bitcast.425), channel_id=1, source_target_pairs={{0,4},{4,0},{8,12},{12,8},{16,20},{20,16},{24,28},{28,24},{1,5},{5... | collective-permute-start | bytes 5898248 | tf_op jit(solution)/shard_map/ppermute | solution.py:165
  485.2 46.2 %collective-permute-start.25 = (f32[2,4,512]{2,1,0:T(4,128)S(1)}, f32[2,4,512]{2,1,0:T(4,128)S(1)}, u32[]{:S(2)}, u32[]{:S(2)}) collective-permute-start(f32[2,4,512]{2,1,0:T(4,128)S(1)} %pad_maximum_fusion.44), channel_id=1, source_target_pairs={{0,1},{1,0},{2,3},{3,2},{4,5},{5,4},{6,7},{7,6},{8,9},{9,8},{10,11... | collective-permute-start | bytes 49160 | tf_op jit(solution)/shard_map/ppermute | solution.py:132
  530.6 190.8 %collective-permute-start.45 = (bf16[5,2,2,2,48,1024]{5,4,3,2,1,0:T(8,128)(2,1)}, bf16[5,2,2,2,48,1024]{5,4,3,2,1,0:T(8,128)(2,1)}, u32[]{:S(2)}, u32[]{:S(2)}) collective-permute-start(bf16[5,2,2,2,48,1024]{5,4,3,2,1,0:T(8,128)(2,1)} %dynamic-slice_bitcast_fusion.1), channel_id=1, source_target_pairs={{0,4},{4,0},{8,12},{12,8},{16,20},{20,16},{24,28},{28,24},{1,5},{5... | collective-permute-start | bytes 11796488 | tf_op jit(solution)/shard_map/ppermute | solution.py:165
  537.0 44.6 %collective-permute-start.53 = (bf16[5,2,64,2,384]{4,2,0,3,1:T(8,128)(2,1)S(1)}, bf16[5,2,64,2,384]{4,2,0,3,1:T(8,128)(2,1)S(1)}, u32[]{:S(2)}, u32[]{:S(2)}) collective-permute-start(bf16[5,2,64,2,384]{4,2,0,3,1:T(8,128)(2,1)S(1)} %dynamic-slice_bitcast_fusion.3), channel_id=1, source_target_pairs={{0,16},{4,20},{8,24},{12,28},{16,0},{20,4},{24,8},{28,12},{1,17},{... | collective-permute-start | bytes 2949128 | tf_op jit(solution)/shard_map/ppermute | solution.py:165
  583.8 132.2 %collective-permute-start.54 = (bf16[5,64,2,384]{3,1,0,2:T(8,128)(2,1)}, bf16[5,64,2,384]{3,1,0,2:T(8,128)(2,1)}, u32[]{:S(2)}, u32[]{:S(2)}) collective-permute-start(bf16[5,64,2,384]{3,1,0,2:T(8,128)(2,1)} %dynamic-slice_bitcast_fusion.5), channel_id=1, source_target_pairs={{0,8},{4,12},{8,0},{12,4},{16,24},{20,28},{24,16},{28,20},{1,9},{5... | collective-permute-start | bytes 1474568 | tf_op jit(solution)/shard_map/ppermute | solution.py:165
  708.1 190.3 %collective-permute-start.31 = (bf16[2,2,2,48,1152]{4,3,0,2,1:T(8,128)(2,1)}, bf16[2,2,2,48,1152]{4,3,0,2,1:T(8,128)(2,1)}, u32[]{:S(2)}, u32[]{:S(2)}) collective-permute-start(bf16[2,2,2,48,1152]{4,3,0,2,1:T(8,128)(2,1)} %bitcast.426), channel_id=1, source_target_pairs={{0,4},{4,0},{8,12},{12,8},{16,20},{20,16},{24,28},{28,24},{1,5},{5... | collective-permute-start | bytes 2654216 | tf_op jit(solution)/shard_map/ppermute | solution.py:165
  725.9 91.2 %collective-permute-start.46 = (bf16[5,2,2,48,1024]{4,3,2,1,0:T(8,128)(2,1)S(1)}, bf16[5,2,2,48,1024]{4,3,2,1,0:T(8,128)(2,1)S(1)}, u32[]{:S(2)}, u32[]{:S(2)}) collective-permute-start(bf16[5,2,2,48,1024]{4,3,2,1,0:T(8,128)(2,1)S(1)} %dynamic-slice_bitcast_fusion.2), channel_id=1, source_target_pairs={{0,16},{4,20},{8,24},{12,28},{16,0},{20,4},{24,8},{28,12},{1,17},{... | collective-permute-start | bytes 5898248 | tf_op jit(solution)/shard_map/ppermute | solution.py:165
  729.4 87.0 %collective-permute-start.28 = (bf16[512,768]{1,0:T(8,128)(2,1)S(1)}, bf16[512,768]{1,0:T(8,128)(2,1)S(1)}, u32[]{:S(2)}, u32[]{:S(2)}) collective-permute-start(bf16[512,768]{1,0:T(8,128)(2,1)S(1)} %fusion.157), channel_id=1, source_target_pairs={{0,1},{1,0},{2,3},{3,2},{4,5},{5,4},{6,7},{7,6},{8,9},{9,8},{10,11... | collective-permute-start | bytes 2359304 | tf_op jit(solution)/shard_map/ppermute | solution.py:132
  735.2 168.7 %collective-permute-start.56 = (bf16[5,2,64,384]{3,2,0,1:T(8,128)(2,1)}, bf16[5,2,64,384]{3,2,0,1:T(8,128)(2,1)}, u32[]{:S(2)}, u32[]{:S(2)}) collective-permute-start(bf16[5,2,64,384]{3,2,0,1:T(8,128)(2,1)} %get-tuple-element.557), channel_id=1, source_target_pairs={{0,8},{4,12},{8,0},{12,4},{16,24},{20,28},{24,16},{28,20},{1,9},{5... | collective-permute-start | bytes 1474568 | tf_op jit(solution)/shard_map/ppermute | solution.py:185
  767.0 48.6 %collective-permute-start.43 = (bf16[2,48,384]{2,1,0:T(8,128)(2,1)S(1)}, bf16[2,48,384]{2,1,0:T(8,128)(2,1)S(1)}, u32[]{:S(2)}, u32[]{:S(2)}) collective-permute-start(bf16[2,48,384]{2,1,0:T(8,128)(2,1)S(1)} %maximum_select_fusion.23), channel_id=1, source_target_pairs={{0,16},{4,20},{8,24},{12,28},{16,0},{20,4},{24,8},{28,12},{1,17},{... | collective-permute-start | bytes 221192 | tf_op jit(solution)/shard_map/ppermute | solution.py:185
  816.3 85.6 %collective-permute-start.44 = (bf16[2,2,48,384]{3,2,1,0:T(8,128)(2,1)}, bf16[2,2,48,384]{3,2,1,0:T(8,128)(2,1)}, u32[]{:S(2)}, u32[]{:S(2)}) collective-permute-start(bf16[2,2,48,384]{3,2,1,0:T(8,128)(2,1)} %maximum_select_fusion.21), channel_id=1, source_target_pairs={{0,4},{4,0},{8,12},{12,8},{16,20},{20,16},{24,28},{28,24},{1,5},{5... | collective-permute-start | bytes 442376 | tf_op jit(solution)/shard_map/ppermute | solution.py:185
  844.5 51.5 %collective-permute-start.48 = (bf16[5,48,1024]{2,1,0:T(8,128)(2,1)S(1)}, bf16[5,48,1024]{2,1,0:T(8,128)(2,1)S(1)}, u32[]{:S(2)}, u32[]{:S(2)}) collective-permute-start(bf16[5,48,1024]{2,1,0:T(8,128)(2,1)S(1)} %get-tuple-element.544), channel_id=1, source_target_pairs={{0,2},{2,0},{1,3},{3,1},{4,6},{6,4},{5,7},{7,5},{8,10},{10,8},{9,1... | collective-permute-start | bytes 1474568 | tf_op jit(solution)/shard_map/ppermute | solution.py:132
  891.8 105.9 %collective-permute-start.29 = (f32[512,384]{1,0:T(8,128)}, f32[512,384]{1,0:T(8,128)}, u32[]{:S(2)}, u32[]{:S(2)}) collective-permute-start(f32[512,384]{1,0:T(8,128)} %get-tuple-element.525), channel_id=1, source_target_pairs={{0,1},{1,0},{2,3},{3,2},{4,5},{5,4},{6,7},{7,6},{8,9},{9,8},{10,11... | collective-permute-start | bytes 2359304 | tf_op jit(solution)/shard_map/ppermute | solution.py:132
  898.1 42.5 %collective-permute-start.49 = (bf16[5,2,48,1024]{3,2,0,1:T(8,128)(2,1)S(1)}, bf16[5,2,48,1024]{3,2,0,1:T(8,128)(2,1)S(1)}, u32[]{:S(2)}, u32[]{:S(2)}) collective-permute-start(bf16[5,2,48,1024]{3,2,0,1:T(8,128)(2,1)S(1)} %get-tuple-element.542), channel_id=1, source_target_pairs={{0,8},{4,12},{8,0},{12,4},{16,24},{20,28},{24,16},{28,20},{1,9},{5... | collective-permute-start | bytes 2949128 | tf_op jit(solution)/shard_map/ppermute | solution.py:185
  899.9 41.2 %collective-permute-start.32 = (bf16[2,2,48,1152]{3,2,0,1:T(8,128)(2,1)S(1)}, bf16[2,2,48,1152]{3,2,0,1:T(8,128)(2,1)S(1)}, u32[]{:S(2)}, u32[]{:S(2)}) collective-permute-start(bf16[2,2,48,1152]{3,2,0,1:T(8,128)(2,1)S(1)} %dynamic-slice_bitcast_fusion.6), channel_id=1, source_target_pairs={{0,16},{4,20},{8,24},{12,28},{16,0},{20,4},{24,8},{28,12},{1,17},{... | collective-permute-start | bytes 1327112 | tf_op jit(solution)/shard_map/ppermute | solution.py:165
  905.3 145.6 %collective-permute-start.57 = (bf16[5,2,2,64,384]{4,3,0,1,2:T(8,128)(2,1)S(1)}, bf16[5,2,2,64,384]{4,3,0,1,2:T(8,128)(2,1)S(1)}, u32[]{:S(2)}, u32[]{:S(2)}) collective-permute-start(bf16[5,2,2,64,384]{4,3,0,1,2:T(8,128)(2,1)S(1)} %maximum_select_fusion.12), channel_id=1, source_target_pairs={{0,16},{4,20},{8,24},{12,28},{16,0},{20,4},{24,8},{28,12},{1,17},{... | collective-permute-start | bytes 2949128 | tf_op jit(solution)/shard_map/ppermute | solution.py:185
  941.0 107.2 %collective-permute-start.50 = (bf16[5,2,2,48,1024]{4,3,0,1,2:T(8,128)(2,1)S(1)}, bf16[5,2,2,48,1024]{4,3,0,1,2:T(8,128)(2,1)S(1)}, u32[]{:S(2)}, u32[]{:S(2)}) collective-permute-start(bf16[5,2,2,48,1024]{4,3,0,1,2:T(8,128)(2,1)S(1)} %maximum_select_fusion.5), channel_id=1, source_target_pairs={{0,16},{4,20},{8,24},{12,28},{16,0},{20,4},{24,8},{28,12},{1,17},{... | collective-permute-start | bytes 5898248 | tf_op jit(solution)/shard_map/ppermute | solution.py:185
  941.2 55.8 %collective-permute-start.33 = (bf16[2,48,1152]{2,1,0:T(8,128)(2,1)S(1)}, bf16[2,48,1152]{2,1,0:T(8,128)(2,1)S(1)}, u32[]{:S(2)}, u32[]{:S(2)}) collective-permute-start(bf16[2,48,1152]{2,1,0:T(8,128)(2,1)S(1)} %dynamic-slice_bitcast_fusion.7), channel_id=1, source_target_pairs={{0,8},{4,12},{8,0},{12,4},{16,24},{20,28},{24,16},{28,20},{1,9},{5... | collective-permute-start | bytes 663560 | tf_op jit(solution)/shard_map/ppermute | solution.py:165
  997.1 53.7 %collective-permute-start.34 = (bf16[48,1152]{1,0:T(8,128)(2,1)S(1)}, bf16[48,1152]{1,0:T(8,128)(2,1)S(1)}, u32[]{:S(2)}, u32[]{:S(2)}) collective-permute-start(bf16[48,1152]{1,0:T(8,128)(2,1)S(1)} %slice_bitcast_fusion.22), channel_id=1, source_target_pairs={{0,2},{2,0},{1,3},{3,1},{4,6},{6,4},{5,7},{7,5},{8,10},{10,8},{9,1... | collective-permute-start | bytes 331784 | tf_op jit(solution)/shard_map/ppermute | solution.py:132
  1000.4 192.6 %collective-permute-start.30 = (f32[1024,384]{1,0:T(8,128)}, f32[1024,384]{1,0:T(8,128)}, u32[]{:S(2)}, u32[]{:S(2)}) collective-permute-start(f32[1024,384]{1,0:T(8,128)} %maximum_select_fusion.10), channel_id=1, source_target_pairs={{1,2},{2,1},{5,6},{6,5},{9,10},{10,9},{13,14},{14,13},{17,18},{18,... | collective-permute-start | bytes 4718600 | tf_op jit(solution)/shard_map/ppermute | solution.py:226
  1050.7 156.0 %collective-permute-start.51 = (bf16[5,2,2,2,48,1024]{5,4,0,1,3,2:T(8,128)(2,1)}, bf16[5,2,2,2,48,1024]{5,4,0,1,3,2:T(8,128)(2,1)}, u32[]{:S(2)}, u32[]{:S(2)}) collective-permute-start(bf16[5,2,2,2,48,1024]{5,4,0,1,3,2:T(8,128)(2,1)} %maximum_select_fusion.2), channel_id=1, source_target_pairs={{0,4},{4,0},{8,12},{12,8},{16,20},{20,16},{24,28},{28,24},{1,5},{5... | collective-permute-start | bytes 11796488 | tf_op jit(solution)/shard_map/ppermute | solution.py:185
  1052.5 143.5 %collective-permute-start.58 = (bf16[5,2,2,2,64,384]{5,4,0,1,3,2:T(8,128)(2,1)}, bf16[5,2,2,2,64,384]{5,4,0,1,3,2:T(8,128)(2,1)}, u32[]{:S(2)}, u32[]{:S(2)}) collective-permute-start(bf16[5,2,2,2,64,384]{5,4,0,1,3,2:T(8,128)(2,1)} %maximum_select_fusion.7), channel_id=1, source_target_pairs={{0,4},{4,0},{8,12},{12,8},{16,20},{20,16},{24,28},{28,24},{1,5},{5... | collective-permute-start | bytes 5898248 | tf_op jit(solution)/shard_map/ppermute | solution.py:185
  1066.8 121.0 %collective-permute-start.37 = (bf16[2,2,48,1152]{3,2,1,0:T(8,128)(2,1)S(1)}, bf16[2,2,48,1152]{3,2,1,0:T(8,128)(2,1)S(1)}, u32[]{:S(2)}, u32[]{:S(2)}) collective-permute-start(bf16[2,2,48,1152]{3,2,1,0:T(8,128)(2,1)S(1)} %maximum_select_fusion.14), channel_id=1, source_target_pairs={{0,4},{4,0},{8,12},{12,8},{16,20},{20,16},{24,28},{28,24},{1,5},{5... | collective-permute-start | bytes 1327112 | tf_op jit(solution)/shard_map/ppermute | solution.py:185
  (154 other events, 2122.5 us)

commit v2 on v1

v2 whole, which is shorter than its diff:
```python
import functools

import jax
import jax.numpy as jnp
from jax import lax
from jax.experimental import pallas as pl
from jax.experimental.pallas import tpu as pltpu
from jax.sharding import PartitionSpec as P

D = 768
HEAD_DIM = 64
E = 4
LEN = 1024
ABLOCK = 256
BF = jnp.bfloat16
F32 = jnp.float32


def norm_forward(values, gain_vec):
    rstd_rows = lax.rsqrt(jnp.mean(values * values, axis=1) + 1e-06)
    return (rstd_rows, values * rstd_rows[:, None] * gain_vec)


def norm_backward(values, rstd_rows, gain_vec, incoming):
    scaled = incoming * gain_vec
    inner_sum = jnp.sum(scaled * values, axis=1)
    gain_grad = jnp.sum(incoming * values * rstd_rows[:, None], axis=0)
    result = rstd_rows[:, None] * scaled - values * (rstd_rows**3 * inner_sum / D)[:, None]
    return (result, gain_grad)


def rope_tables(length):
    half_dim = HEAD_DIM // 2
    freqs = 10000.0 ** (-jnp.arange(half_dim, dtype=F32) * 2.0 / HEAD_DIM)
    angles = jnp.arange(length, dtype=F32)[:, None] * freqs[None, :]
    sine = jnp.sin(angles)
    return (jnp.tile(jnp.cos(angles), (1, 4)), jnp.tile(jnp.concatenate([-sine, sine], axis=1), (1, 2)))


def lanes_of(shape):
    return lax.broadcasted_iota(jnp.int32, shape, len(shape) - 1)


def turn(values, first):
    half_dim = HEAD_DIM // 2
    return jnp.where(
        first,
        pltpu.roll(values, PAIR - half_dim, values.ndim - 1),
        pltpu.roll(values, half_dim, values.ndim - 1),
    )


PAIR = 2 * HEAD_DIM
NT = (((1,), (1,)), ((), ()))


def shares_of(key_pair, query_head, seg_col, seg_row):
    scores = lax.dot_general(key_pair, query_head, NT, preferred_element_type=F32)
    scores = jnp.where(seg_col == seg_row, scores, -1e30)
    weight = jnp.exp(scores - jnp.max(scores, axis=0, keepdims=True))
    return weight * (1.0 / jnp.sum(weight, axis=0, keepdims=True))


def attend_kernel(pre, cosine, sine, seg_row, seg_col, queries, keys, values, context):
    rows = pre.shape[1]
    first = lanes_of((rows, PAIR)) % HEAD_DIM < HEAD_DIM // 2
    cos, sin = cosine[...], sine[...]
    query = pre[0]
    queries[...] = ((query * cos + turn(query, first) * sin) * HEAD_DIM**-0.5).astype(BF)
    key = pre[1]
    keys[...] = (key * cos + turn(key, first) * sin).astype(BF)
    value = pre[2]
    values[...] = value.astype(BF)
    value_t = value.T.astype(BF)
    lower = lanes_of((ABLOCK, PAIR)) < HEAD_DIM
    for block in range(rows // ABLOCK):
        start, stop = block * ABLOCK, (block + 1) * ABLOCK
        query = queries[start:stop]
        parts = []
        for head in range(2):
            query_head = jnp.where(lower == (head == 0), query, jnp.zeros_like(query))
            shares = shares_of(
                keys[:stop], query_head, seg_col[:stop], seg_row[:, start:stop]
            ).astype(BF)
            parts.append(jnp.dot(value_t[:, :stop], shares, preferred_element_type=F32))
        both = jnp.concatenate([parts[0][:HEAD_DIM], parts[1][HEAD_DIM:]], axis=0)
        context[start:stop] = both.T.astype(BF)


def attend_forward(pre, tables, seg_row, seg_col):
    _, rows, width = pre.shape
    block = pl.BlockSpec((rows, PAIR), lambda i: (0, i))
    whole = pl.BlockSpec((rows, PAIR), lambda i: (0, 0))
    return pl.pallas_call(
        attend_kernel,
        grid=(width // PAIR,),
        out_shape=[jax.ShapeDtypeStruct((rows, width), BF)] * 4,
        in_specs=[
            pl.BlockSpec((3, rows, PAIR), lambda i: (0, 0, i)),
            whole,
            whole,
            pl.BlockSpec((1, rows), lambda i: (0, 0)),
            pl.BlockSpec((rows, 1), lambda i: (0, 0)),
        ],
        out_specs=[block] * 4,
        compiler_params=pltpu.CompilerParams(vmem_limit_bytes=40 << 20),
        cost_estimate=pl.CostEstimate(
            flops=20_000_000_000, bytes_accessed=8 << 20, transcendentals=4 << 20
        ),
    )(pre, tables[0], tables[1], seg_row, seg_col)


def attend_back_kernel(
    queries, keys, values, context_grad, cosine, sine, seg_row, seg_col, out, key_sum, value_sum
):
    rows = queries.shape[0]
    key_t = keys[...].astype(F32).T.astype(BF)
    lower = lanes_of((ABLOCK, PAIR)) < HEAD_DIM
    first = lanes_of((ABLOCK, PAIR)) % HEAD_DIM < HEAD_DIM // 2
    for block in reversed(range(rows // ABLOCK)):
        start, stop = block * ABLOCK, (block + 1) * ABLOCK
        query, incoming = queries[start:stop], context_grad[start:stop]
        parts, key_part, value_part = [], None, None
        for head in range(2):
            mine = lower == (head == 0)
            query_head = jnp.where(mine, query, jnp.zeros_like(query))
            incoming_head = jnp.where(mine, incoming, jnp.zeros_like(incoming))
            shares = shares_of(keys[:stop], query_head, seg_col[:stop], seg_row[:, start:stop])
            share_grad = lax.dot_general(
                values[:stop], incoming_head, NT, preferred_element_type=F32
            )
            centre = jnp.sum(shares * share_grad, axis=0, keepdims=True)
            score_grad = (shares * (share_grad - centre)).astype(BF)
            parts.append(jnp.dot(key_t[:, :stop], score_grad, preferred_element_type=F32))
            more = jnp.dot(shares.astype(BF), incoming_head, preferred_element_type=F32)
            value_part = more if head == 0 else value_part + more
            more = jnp.dot(score_grad, query_head, preferred_element_type=F32)
            key_part = more if head == 0 else key_part + more
        both = jnp.concatenate([parts[0][:HEAD_DIM], parts[1][HEAD_DIM:]], axis=0)
        grad = both.T * HEAD_DIM**-0.5
        cos, sin = cosine[start:stop], sine[start:stop]
        out[0, start:stop] = (grad * cos + turn(grad * sin, first)).astype(BF)
        if stop == rows:
            key_sum[...] = key_part
            value_sum[...] = value_part
        else:
            key_sum[:stop] += key_part
            value_sum[:stop] += value_part
    for block in range(rows // ABLOCK):
        start, stop = block * ABLOCK, (block + 1) * ABLOCK
        grad = key_sum[start:stop]
        cos, sin = cosine[start:stop], sine[start:stop]
        out[1, start:stop] = (grad * cos + turn(grad * sin, first)).astype(BF)
        out[2, start:stop] = value_sum[start:stop].astype(BF)


def attend_backward(queries, keys, values, context_grad, tables, seg_row, seg_col, first_pair, pairs):
    rows = queries.shape[0]
    block = pl.BlockSpec((rows, PAIR), lambda i: (0, i + first_pair))
    whole = pl.BlockSpec((rows, PAIR), lambda i: (0, 0))
    return pl.pallas_call(
        attend_back_kernel,
        grid=(pairs,),
        out_shape=jax.ShapeDtypeStruct((3, rows, pairs * PAIR), BF),
        in_specs=[block] * 4
        + [
            whole,
            whole,
            pl.BlockSpec((1, rows), lambda i: (0, 0)),
            pl.BlockSpec((rows, 1), lambda i: (0, 0)),
        ],
        out_specs=pl.BlockSpec((3, rows, PAIR), lambda i: (0, 0, i)),
        scratch_shapes=[pltpu.VMEM((rows, PAIR), F32), pltpu.VMEM((rows, PAIR), F32)],
        compiler_params=pltpu.CompilerParams(vmem_limit_bytes=40 << 20),
        cost_estimate=pl.CostEstimate(
            flops=pairs * 14_000_000_000, bytes_accessed=4 << 20, transcendentals=2 << 20
        ),
    )(queries, keys, values, context_grad, tables[0], tables[1], seg_row, seg_col)


def swap(values, axis):
    return lax.ppermute(values, axis, [(0, 1), (1, 0)])


def flip(values):
    half = values.shape[-1] // 2
    return jnp.concatenate([values[..., half:], values[..., :half]], axis=-1)


def dp_pairs(bit):
    n = lax.axis_size("dp")
    return [(i, i ^ (1 << bit)) for i in range(n)]


def dp_sum(values):
    for bit in range(lax.axis_size("dp").bit_length() - 1):
        values = values + lax.ppermute(values, "dp", dp_pairs(bit))
    values = values + swap(values, "row")
    return values + swap(values, "col")


def remote(src, dst, send, recv, device):
    return pltpu.make_async_remote_copy(
        src_ref=src,
        dst_ref=dst,
        send_sem=send,
        recv_sem=recv,
        device_id=device,
        device_id_type=pl.DeviceIdType.MESH,
    )


def greet(devices):
    barrier = pltpu.get_barrier_semaphore()
    for device in devices:
        pl.semaphore_signal(
            barrier, inc=1, device_id=device, device_id_type=pl.DeviceIdType.MESH
        )
    pl.semaphore_wait(barrier, len(devices))


AHEAD = 3
BEHIND = 3


def reduce_kernel(n, slots, *refs):
    ups, (down, attn) = refs[:slots], refs[slots : slots + 2]
    up_out, down_out, attn_out = refs[slots + 2 : slots + 5]
    (
        up_keep, down_keep, attn_keep, up_x, down_x, attn_x, up_z, down_z, attn_z,
        up_done, down_done, attn_done, attn_y,
        keep_sem, x_send, x_recv, z_send, z_recv, out_sem, y_send, y_recv,
    ) = refs[slots + 5 :]
    me = lax.axis_index("dp")
    row = lax.axis_index("row")
    deep = n // 2
    z, x = me // 2, me % 2
    partner = {"dp": 2 * z + (1 - x)}
    peer = {"row": 1 - row}
    ahead = [lax.rem(z + k, deep) for k in range(deep)]
    greet([partner, peer] + [{"dp": 2 * ahead[k] + x} for k in range(1, deep)])

    items = [("down", e) for e in range(slots)]
    items += [("up", 2 * e + h) for e in range(slots) for h in (1, 0)]
    items += [("attn", 0)]
    count = len(items)
    last = count - 1

    def buffers(item):
        kind, at = items[item]
        if kind == "down":
            return down.at[at], down_keep.at[at], down_x.at[at], down_z.at[at], down_done.at[at]
        if kind == "up":
            return ups[at // 2].at[at % 2], up_keep.at[at], up_x.at[at], up_z.at[at], up_done.at[at]
        return None, attn_keep.at[:, x], attn_x, attn_z, attn_done

    y_first = remote(attn.at[1], attn_y, y_send.at[last], y_recv.at[last], peer)
    y_first.start()
    attn_load = pltpu.make_async_copy(attn.at[0], attn_keep, keep_sem.at[last])
    attn_load.start()
    loads, x_copies, z_copies, outs, y_copies = {}, {}, {}, [], [y_first]
    for item in range(last):
        source, keep, _, _, _ = buffers(item)
        loads[item] = pltpu.make_async_copy(source.at[:, x], keep, keep_sem.at[item])
        loads[item].start()

    def send_x(item):
        source, keep, landing, _, _ = buffers(item)
        if item == last:
            attn_load.wait()
            y_first.wait_recv()
            attn_keep[...] = (attn_keep[...].astype(F32) + attn_y[...].astype(F32)).astype(BF)
            given = attn_keep.at[:, 1 - x]
        else:
            given = source.at[:, 1 - x]
        x_copies[item] = remote(given, landing, x_send.at[item], x_recv.at[item], partner)
        x_copies[item].start()

    def send_z(item):
        _, keep, landing, arrivals, _ = buffers(item)
        if item in loads:
            loads[item].wait()
        x_copies[item].wait_recv()
        keep[...] = (keep[...].astype(F32) + landing[...].astype(F32)).astype(BF)
        for k in range(1, deep):
            copy = remote(
                keep.at[ahead[k]],
                arrivals.at[k - 1],
                z_send.at[item, k],
                z_recv.at[item, k],
                {"dp": 2 * ahead[k] + x},
            )
            copy.start()
            z_copies[item, k] = copy

    def finish(item):
        kind, at = items[item]
        _, keep, _, arrivals, done = buffers(item)
        total = keep[z].astype(F32)
        for k in range(1, deep):
            z_copies[item, k].wait_recv()
            total = total + arrivals[k - 1].astype(F32)
        done[...] = total.astype(BF)
        half = down.shape[4] // 2

        def keep_own(source, target):
            copy = pltpu.make_async_copy(source, target, out_sem.at[item])
            copy.start()
            outs.append(copy)

        def give_peer(source, target):
            copy = remote(source, target, y_send.at[item], y_recv.at[item], peer)
            copy.start()
            y_copies.append(copy)

        if kind == "down":
            keep_own(done.at[:, :half], down_out.at[0, at])
            give_peer(done.at[:, half:], down_out.at[1, at])
        elif kind == "attn":
            keep_own(done, attn_out)
        elif at % 2 == 0:
            keep_own(done, up_out.at[0, at // 2])
        else:
            give_peer(done, up_out.at[1, at // 2])

    for step in range(count + AHEAD + BEHIND):
        if step < count:
            send_x(step)
        if 0 <= step - AHEAD < count:
            send_z(step - AHEAD)
        if 0 <= step - AHEAD - BEHIND < count:
            finish(step - AHEAD - BEHIND)
    for copy in outs:
        copy.wait()
    y_first.wait_send()
    for copy in y_copies[1:]:
        copy.wait()
    for copy in list(x_copies.values()) + list(z_copies.values()):
        copy.wait_send()


def dp_reduce(up_grads, down_grad, attn_grad):
    n = lax.axis_size("dp")
    deep = n // 2
    slots = len(up_grads)
    up_tail, down_tail, attn_tail = up_grads[0].shape[3:], down_grad.shape[3:], attn_grad.shape[3:]
    sems = pltpu.SemaphoreType.DMA
    count = 3 * slots + 1
    vmem = lambda *shape: pltpu.VMEM(shape, BF)
    half = down_tail[1] // 2
    any_spec = pl.BlockSpec(memory_space=pl.ANY)
    return pl.pallas_call(
        functools.partial(reduce_kernel, n, slots),
        out_shape=[
            jax.ShapeDtypeStruct((2, slots) + up_tail, BF),
            jax.ShapeDtypeStruct((2, slots, down_tail[0], half), BF),
            jax.ShapeDtypeStruct(attn_tail, BF),
        ],
        in_specs=[any_spec] * (slots + 2),
        out_specs=[any_spec] * 3,
        scratch_shapes=[
            vmem(2 * slots, deep, *up_tail),
            vmem(slots, deep, *down_tail),
            vmem(deep, 2, *attn_tail),
            vmem(2 * slots, deep, *up_tail),
            vmem(slots, deep, *down_tail),
            vmem(deep, *attn_tail),
            vmem(2 * slots, deep - 1, *up_tail),
            vmem(slots, deep - 1, *down_tail),
            vmem(deep - 1, *attn_tail),
            vmem(2 * slots, *up_tail),
            vmem(slots, *down_tail),
            vmem(*attn_tail),
            vmem(deep, 2, *attn_tail),
            sems((count,)),
            sems((count,)),
            sems((count,)),
            sems((count, deep)),
            sems((count, deep)),
            sems((count,)),
            sems((count,)),
            sems((count,)),
        ],
        compiler_params=pltpu.CompilerParams(
            collective_id=1, has_side_effects=True, vmem_limit_bytes=48 << 20
        ),
    )(*up_grads, down_grad, attn_grad)


def order_pair(first_is_own, own, other, axis):
    return jnp.where(
        first_is_own, jnp.concatenate([own, other], axis), jnp.concatenate([other, own], axis)
    )


WINDOW = 2


def gather_kernel(n, plan, *refs):
    count = max(item[0] for item in plan) + 1
    pieces, fulls = refs[:count], refs[count : 2 * count]
    own_sem, z_send, z_recv, x_send, x_recv = refs[2 * count :]
    me = lax.axis_index("dp")
    deep = n // 2
    z, x = me // 2, me % 2
    partner = 2 * z + (1 - x)
    peers = [2 * lax.rem(z + k, deep) + x for k in range(1, deep)]
    sources = [2 * lax.rem(z + deep - k, deep) + x for k in range(deep)]

    greet([{"dp": device} for device in peers + [partner]])

    def region(item, owner):
        at, lead, rows = plan[item]
        full = fulls[at]
        for index in lead:
            full = full.at[index]
        if rows == 0:
            return full.at[owner]
        start = owner * rows
        if rows % 16 == 0:
            start = pl.multiple_of(start, 16)
        return full.at[pl.ds(start, rows)]

    def piece(item):
        at, lead, rows = plan[item]
        ref = pieces[at]
        for index in lead:
            ref = ref.at[index]
        return ref

    total = len(plan)
    local_copies = []
    z_copies = [[] for _ in range(total)]
    x_copies = [[] for _ in range(total)]
    for step in range(total + WINDOW):
        if step < total:
            here = region(step, me)
            for k in range(1, deep):
                copy = remote(
                    piece(step), here, z_send.at[step, k], z_recv.at[step, k], {"dp": peers[k - 1]}
                )
                copy.start()
                z_copies[step].append(copy)
            copy = remote(piece(step), here, x_send.at[step, 0], x_recv.at[step, 0], {"dp": partner})
            copy.start()
            x_copies[step].append(copy)
            copy = pltpu.make_async_copy(piece(step), here, own_sem.at[step])
            copy.start()
            local_copies.append(copy)
        if step >= WINDOW:
            item = step - WINDOW
            for k in range(1, deep):
                z_copies[item][k - 1].wait_recv()
                arrived = region(item, sources[k])
                copy = remote(
                    arrived, arrived, x_send.at[item, k], x_recv.at[item, k], {"dp": partner}
                )
                copy.start()
                x_copies[item].append(copy)
    for item in range(total):
        local_copies[item].wait()
        for copy in z_copies[item]:
            copy.wait_send()
        for copy in x_copies[item]:
            copy.wait()


def dp_gather(pieces, fulls, plan):
    n = lax.axis_size("dp")
    total = len(plan)
    sems = pltpu.SemaphoreType.DMA
    return pl.pallas_call(
        functools.partial(gather_kernel, n, plan),
        out_shape=[jax.ShapeDtypeStruct(shape, BF) for shape in fulls],
        in_specs=[pl.BlockSpec(memory_space=pl.ANY)] * len(pieces),
        out_specs=[pl.BlockSpec(memory_space=pl.ANY)] * len(fulls),
        scratch_shapes=[
            sems((total,)),
            sems((total, n // 2)),
            sems((total, n // 2)),
            sems((total, n // 2)),
            sems((total, n // 2)),
        ],
        compiler_params=pltpu.CompilerParams(collective_id=0, has_side_effects=True),
    )(*pieces)


def half_by_x(values, axis):
    size = values.shape[axis] // 2
    return lax.dynamic_slice_in_dim(values, (lax.axis_index("dp") % 2) * size, size, axis)


def fetch_row(values, axis):
    first = swap(half_by_x(values, axis), "row")
    second = lax.ppermute(first, "dp", dp_pairs(0))
    return order_pair(lax.axis_index("dp") % 2 == 0, first, second, axis)


def silu_parts(values):
    sigma = jax.nn.sigmoid(values)
    return (values * sigma, sigma * (1.0 + values * (1.0 - sigma)))


def spread_tokens(own):
    near = swap(own, "col")
    far = swap(flip(own), "row")
    far_near = swap(far, "col")
    return jnp.stack([own, near, far, far_near])


def collect_tokens(parts):
    recv = swap(jnp.stack([parts[1], parts[3]]).astype(BF), "col").astype(F32)
    own = parts[0] + recv[0]
    far = parts[2] + recv[1]
    return own + swap(flip(far.astype(BF)), "row").astype(F32)


def to_sequence(values, r, c):
    other = lax.ppermute(values, ("row", "col"), [(1, 3), (2, 0)])
    pair = jnp.stack([values, other])
    copied = lax.ppermute(pair, ("row", "col"), [(0, 1), (3, 2)])
    return jnp.where(r == c, pair, copied)


def from_sequence(values, r, c):
    half = values.shape[1] // 2
    own, peer = values[:, :half], values[:, half:]
    diag = r == c
    send = jnp.where(diag, peer, own)
    kept = jnp.where(diag, own, peer)
    recv = swap(send, "col")
    whole = order_pair(c == 0, kept, recv, 0)
    moved = lax.ppermute(whole, ("row", "col"), [(1, 2), (2, 1)])
    return jnp.where(diag, whole, moved)


def local(
    layer_input,
    teacher,
    valid_mask,
    routes,
    segments,
    gain_attn,
    gain_ffn,
    w_qkv,
    w_out,
    w_router,
    w_shared_up,
    w_shared_down,
    w_expert_up,
    w_expert_down,
):
    r = lax.axis_index("row")
    c = lax.axis_index("col")
    n_dp = lax.axis_size("dp")
    rows = layer_input.shape[0]
    part = rows // 2
    half = layer_input.shape[1]
    heads = w_qkv.shape[2] // HEAD_DIM
    ff = w_shared_up.shape[2]
    quarter = ff // 2
    slots = E + 1

    x_pair = to_sequence(layer_input, r, c)
    x_seq = jnp.concatenate([x_pair[0], x_pair[1]], axis=1).astype(F32)
    w_qkv_full = jnp.concatenate([w_qkv, swap(w_qkv, "row")], axis=0)
    w_out_full = jnp.concatenate([w_out, swap(w_out, "row")], axis=1)
    gain_a = jnp.concatenate([gain_attn, swap(gain_attn, "row")])
    gain_f = jnp.concatenate([gain_ffn, swap(gain_ffn, "row")])
    w_r = jnp.concatenate([w_router, swap(w_router, "row")])
    t_pair = to_sequence(teacher, r, c)
    t_seq = jnp.concatenate([t_pair[0], t_pair[1]], axis=1)
    teacher_own = lax.dynamic_slice_in_dim(t_seq, c * part, part, 0).astype(F32)
    valid_other = swap(valid_mask, "col")
    valid_seq = jnp.where(r == c, valid_mask, valid_other).astype(F32)
    valid_own = lax.dynamic_slice_in_dim(valid_seq, c * part, part, 0)
    count = dp_sum(jnp.full((128,), jnp.sum(valid_own), F32))[0]
    seg = lax.dynamic_slice_in_dim(segments, r, 1, 0)[0]
    route_blocks = routes.reshape(2, 2, part, 2)
    route_blocks = jnp.where(r == 0, route_blocks, route_blocks[::-1])
    route_blocks = jnp.where(c == 0, route_blocks, route_blocks[:, ::-1]).reshape(4 * part, 2)
    picks = (route_blocks[:, :, None] == jnp.arange(E, dtype=jnp.int32)[None, None, :]).astype(F32)

    up_parts = [w_shared_up] + [w_expert_up[e] for e in range(E)]
    down_parts = [w_shared_down] + [w_expert_down[e] for e in range(E)]
    w_up, w_down = [], []
    for e in range(slots):
        keep = lax.dynamic_slice_in_dim(up_parts[e], r * quarter, quarter, 2)
        send = lax.dynamic_slice_in_dim(up_parts[e], (1 - r) * quarter, quarter, 2)
        w_up.append(
            jnp.concatenate([keep, fetch_row(send, 0)], axis=0).reshape(D, 2 * quarter)
        )
        keep = lax.dynamic_slice_in_dim(down_parts[e], r * quarter, quarter, 0)
        send = lax.dynamic_slice_in_dim(down_parts[e], (1 - r) * quarter, quarter, 0)
        w_down.append(jnp.concatenate([keep, fetch_row(send, 0)], axis=1))
    w_down = jnp.concatenate(w_down, axis=0)

    rstd_seq, normed = norm_forward(x_seq, gain_a)
    normed_attn = normed.astype(BF)
    qkv_pre = jnp.einsum("td,dke->kte", normed_attn, w_qkv_full, preferred_element_type=F32)
    tables = rope_tables(rows)
    seg_row, seg_col = seg[None, :], seg[:, None]
    queries, keys_rot, values_low, context_low = attend_forward(qkv_pre, tables, seg_row, seg_col)
    attention = jnp.dot(context_low, w_out_full, preferred_element_type=F32)
    att_halves = attention.reshape(2, part, D)
    att_keep = lax.dynamic_index_in_dim(att_halves, c, 0, keepdims=False)
    att_send = lax.dynamic_index_in_dim(att_halves, 1 - c, 0, keepdims=False)
    x_own = lax.dynamic_slice_in_dim(x_seq, c * part, part, 0)
    rstd_attn = lax.dynamic_slice_in_dim(rstd_seq, c * part, part, 0)
    hidden = x_own + att_keep + swap(att_send.astype(BF), "col").astype(F32)

    rstd_ffn, normed = norm_forward(hidden, gain_f)
    normed_low = normed.astype(BF)
    tokens = spread_tokens(normed_low).reshape(4 * part, D)
    logits = jnp.dot(tokens, w_r, preferred_element_type=F32)
    chosen = jnp.sum(picks * logits[:, None, :], axis=2)
    chosen = chosen - jnp.max(chosen, axis=1, keepdims=True)
    gates = jnp.exp(chosen)
    gates = gates / jnp.sum(gates, axis=1, keepdims=True)
    mixing = jnp.sum(picks * gates[:, :, None], axis=1)
    mix_all = jnp.concatenate([jnp.ones((4 * part, 1), F32), mixing], axis=1).T
    pre = [
        jnp.dot(tokens, w_up[e], preferred_element_type=F32).astype(BF)
        for e in range(slots)
    ]
    acts = []
    for e in range(slots):
        gate_pre, up_pre = pre[e][:, :quarter].astype(F32), pre[e][:, quarter:].astype(F32)
        act = gate_pre * jax.nn.sigmoid(gate_pre) * up_pre
        acts.append((act * mix_all[e][:, None]).astype(BF))
    act_all = jnp.concatenate(acts, axis=1)
    branch = jnp.dot(act_all, w_down, preferred_element_type=F32)
    output = hidden + collect_tokens(branch.reshape(4, part, D))

    error = output - teacher_own
    loss_part = jnp.sum(valid_own * jnp.sum(error * error, axis=1))
    total_tokens = part * 4 * n_dp
    grad_out = total_tokens / count * valid_own[:, None] * error

    grads = spread_tokens(grad_out.astype(BF)).reshape(4 * part, D)
    down_grad = jnp.dot(act_all.T, grads, preferred_element_type=F32).astype(BF)
    act_back = jnp.dot(
        grads, w_down.T, preferred_element_type=F32
    ).astype(BF)
    pre_grads = []
    gate_sums = []
    for e in range(slots):
        gate_pre, up_pre = pre[e][:, :quarter].astype(F32), pre[e][:, quarter:].astype(F32)
        back = act_back[:, e * quarter : (e + 1) * quarter].astype(F32)
        act_silu, slope = silu_parts(gate_pre)
        if e:
            gate_sums.append(jnp.sum(back * act_silu * up_pre, axis=1))
        back = back * mix_all[e][:, None]
        pre_grads.append(
            jnp.concatenate([back * up_pre * slope, back * act_silu], axis=1).astype(BF)
        )
    up_grads = [
        jnp.dot(tokens.T, pre_grads[e], preferred_element_type=F32).astype(BF)
        for e in range(slots)
    ]
    input_part = jnp.zeros((4 * part, D), F32)
    for e in range(slots):
        input_part = input_part + jnp.dot(
            pre_grads[e], w_up[e].T, preferred_element_type=F32
        )
    normed_ffn_grad = collect_tokens(input_part.reshape(4, part, D))
    gate_parts = jnp.stack(gate_sums, axis=0).reshape(E, 4, part)
    recv = swap(jnp.stack([gate_parts[:, 1], gate_parts[:, 3]]), "col")
    gate_grad = gate_parts[:, 0] + recv[0] + swap(gate_parts[:, 2] + recv[1], "row")
    mix_own = mixing[:part].T
    centre = jnp.sum(mix_own * gate_grad, axis=0, keepdims=True)
    logit_grad = (mix_own * (gate_grad - centre)).T.astype(BF)
    normed_ffn_grad = normed_ffn_grad + jnp.dot(logit_grad, w_r.T, preferred_element_type=F32)
    router_grad = jnp.dot(normed_low.T, logit_grad, preferred_element_type=F32)
    hidden_back, gain_ffn_grad = norm_backward(hidden, rstd_ffn, gain_f, normed_ffn_grad)
    hidden_grad = grad_out + hidden_back

    low_own = hidden_grad.astype(BF)
    low_seq = order_pair(c == 0, low_own, swap(low_own, "col"), 0)
    w_out_grad = jnp.dot(context_low.T, low_seq, preferred_element_type=F32).astype(BF)
    context_grad = jnp.dot(low_seq, w_out_full.T, preferred_element_type=F32)
    context_grad = context_grad.astype(BF)
    qkv_grad = jnp.concatenate(
        [
            attend_backward(
                queries, keys_rot, values_low, context_grad, tables, seg_row, seg_col, pair, 1
            )
            for pair in range(heads // 2)
        ],
        axis=2,
    )
    w_qkv_grad = jnp.einsum(
        "td,kte->dke", normed_attn, qkv_grad, preferred_element_type=F32
    ).astype(BF)
    back_part = jnp.einsum("kte,dke->td", qkv_grad, w_qkv_full, preferred_element_type=F32)
    back_halves = back_part.reshape(2, part, D)
    back_keep = lax.dynamic_index_in_dim(back_halves, c, 0, keepdims=False)
    back_send = lax.dynamic_index_in_dim(back_halves, 1 - c, 0, keepdims=False)
    normed_attn_grad = back_keep + swap(back_send.astype(BF), "col").astype(F32)
    input_back, gain_attn_grad = norm_backward(x_own, rstd_attn, gain_a, normed_attn_grad)
    input_grad = hidden_grad + input_back

    owner_f = quarter // n_dp
    owner_d = half // n_dp
    deep = n_dp // 2
    grad_pair = jnp.concatenate(
        [
            w_qkv_grad.reshape(2, n_dp, owner_d, 3, half),
            w_out_grad.reshape(n_dp, owner_d, 2, half).transpose(2, 0, 1, 3)[:, :, :, None],
        ],
        axis=3,
    ).transpose(0, 1, 3, 2, 4)
    up_pair, down_pair, attn_piece = dp_reduce(
        [grad.reshape(2, deep, 2, owner_d, 2 * quarter) for grad in up_grads],
        down_grad.reshape(slots, deep, 2, owner_f, D),
        grad_pair.reshape(2, deep, 2, 4 * owner_d, half),
    )
    attn_piece = attn_piece.reshape(4, owner_d, half)
    down_piece = jnp.where(r == 0, down_pair, down_pair[::-1]).swapaxes(0, 1)
    up_pair = up_pair.reshape(2, slots, owner_d, 2, quarter)
    up_piece = order_pair(r == 0, up_pair[0], up_pair[1], 3)

    plan = [(1, (), owner_d), (3, (0,), owner_f), (3, (1,), owner_f)]
    for e in range(E):
        plan += [(0, (e,), owner_d), (2, (e, 0), owner_f), (2, (e, 1), owner_f)]
    plan += [(4, (), 0)]
    up_full, shared_up_full, down_full, shared_down_full, attn_full = dp_gather(
        (up_piece[1:], up_piece[0], down_piece[1:], down_piece[0], attn_piece),
        (
            (E, half, 2, ff),
            (half, 2, ff),
            (E, 2, quarter, half),
            (2, quarter, half),
            (n_dp, 4, owner_d, half),
        ),
        tuple(plan),
    )
    attn_full = attn_full.swapaxes(0, 1).reshape(4, half, half).astype(F32)

    small = jnp.concatenate([gain_attn_grad[None], gain_ffn_grad[None], router_grad.T], axis=0)
    small = jnp.where(r == 0, small, flip(small))
    small = jnp.concatenate([small.reshape(-1), loss_part[None]])
    small = dp_sum(small)
    loss = small[-1] / (2.0 * count)
    small = small[:-1].reshape(E + 2, D)
    small = lax.dynamic_slice_in_dim(small, r * half, half, 1)
    return (
        from_sequence(output, r, c),
        loss,
        from_sequence(input_grad, r, c),
        small[0],
        small[1],
        attn_full[:3].swapaxes(0, 1),
        attn_full[3],
        small[2:].T,
        shared_up_full.astype(F32),
        shared_down_full.reshape(ff, half).astype(F32),
        up_full.astype(F32),
        down_full.reshape(E, ff, half).astype(F32),
    )


def solution(mesh):
    return jax.shard_map(
        local,
        mesh=mesh,
        in_specs=(
            P(("dp", "col"), "row"),
            P(("dp", "col"), "row"),
            P(("dp", "col")),
            P("dp", None),
            P("dp", None),
            P("row"),
            P("row"),
            P("row", None, "col"),
            P("col", "row"),
            P("row", None),
            P("row", None, "col"),
            P("col", "row"),
            P(None, "row", None, "col"),
            P(None, "col", "row"),
        ),
        out_specs=(
            P(("dp", "col"), "row"),
            P(),
            P(("dp", "col"), "row"),
            P("row"),
            P("row"),
            P("row", None, "col"),
            P("col", "row"),
            P("row", None),
            P("row", None, "col"),
            P("col", "row"),
            P(None, "row", None, "col"),
            P(None, "col", "row"),
        ),
        check_vma=False,
    )
```

time: 1280 us -> 893 us (0.70)
  waiting for transfers between devices: 521 us -> 130 us
  Pallas kernels: 0 us -> 350 us
  other arithmetic: 196 us -> 100 us
  blocking collectives: 82.7 us -> 0 us
  local copies, waits for them, and re-layouts: 166 us -> 91.3 us
  matrix products: 201 us -> 136 us
  loops' own time: 13.5 us -> 0 us
    pallas_call x0 -> x6, Pallas kernels: none -> 350 us  [the longest x1 158 us: dp_reduce(): pl.pallas_call(functools.partial(reduce_kernel, n, slots), out_shape=[jax...]
    ppermute x24 -> x16, waiting for transfers between devices: 377 us -> 36.2 us  [the longest x10 28.7 us: fetch_row(): second = lax.ppermute(first, 'dp', dp_pairs(0))]
    psum x2 -> x0, blocking collectives: 82.7 us -> none  [the longest x1 44 us: local(): small = lax.psum(small, ('dp', 'row', 'col'))]
    dot_general x29 -> x15, matrix products: 151 us -> 92.1 us  [the longest x5 36.8 us: local(): jnp.dot(pre_grads[e], w_up[e].T, preferred_element_type=F32)]
    ppermute x29 -> x37, waiting for transfers between devices: 134 us -> 93.8 us  [swap(): return lax.ppermute(values, axis, [(0, 1), (1, 0)])]
    convert_element_type x22 -> x5, other arithmetic: 47.9 us -> 15.5 us  [the longest x1 6.14 us: local(): up_full.astype(F32)]
    dynamic_update_slice x4 -> x0, local copies, waits for them, and re-layouts: 31.5 us -> none  [attend_forward(): context, log_totals = lax.map(one_block, jnp.arange(length // query_rows))]
    concatenate x6 -> x4, other arithmetic: 30.8 us -> 3.85 us  [the longest x1 2.03 us: local(): jnp.concatenate([keep, fetch_row(send, 0)], axis=0).reshape(D, 2 * quarter)]
  transfers between devices with their start and end apart: 59 -> 59, of which waited for: 20 -> 20; matrix products, arithmetic and copies ran while one was open for 39% -> 32% of each run, Pallas kernels for 0% -> 38%
where the time goes in v2:
time: 893 us; the launch traced here: 882 us
  Pallas kernels  350 us (39%)
  matrix products  136 us (15%)
  waiting for transfers between devices  130 us (15%)
  other arithmetic  100 us (11%)
  local copies, waits for them, and re-layouts  91.3 us (10%)
  starting transfers between devices  69.6 us (8%)
    pallas_call x1, Pallas kernels, dp_reduce(): pl.pallas_call(functools.partial(reduce_kernel, n, slots), out_shape=[jax...  158 us
    pallas_call x1, Pallas kernels, dp_gather(): pl.pallas_call(functools.partial(gather_kernel, n, plan), out_shape=[jax....  156 us
    ppermute x37, waiting for transfers between devices, swap(): return lax.ppermute(values, axis, [(0, 1), (1, 0)])  93.8 us
    ppermute x37, starting transfers between devices, swap(): return lax.ppermute(values, axis, [(0, 1), (1, 0)])  49.2 us
    dot_general x5, matrix products, local(): jnp.dot(pre_grads[e], w_up[e].T, preferred_element_type=F32)  36.8 us
    unnamed x307, local copies, waits for them, and re-layouts  30.3 us
    ppermute x10, waiting for transfers between devices, fetch_row(): second = lax.ppermute(first, 'dp', dp_pairs(0))  28.7 us
    dot_general x5, matrix products, local(): jnp.dot(tokens.T, pre_grads[e], preferred_element_type=F32).astype(BF)  25.3 us
  transfers between devices with their start and end apart: 59, of which 20 were waited for; matrix products, arithmetic and copies ran while one was open for 32% of the time, Pallas kernels for 38%

profile of v2, /device:TPU:27, one launch (start us, length us, event | category | flops | bytes accessed | tf_op | source)
XLA Modules:
  0.0 882.0 jit_solution(232423373518914382)
XLA Ops:
  20.3 7.3 fusion.131
  80.3 6.3 collective-permute-done.17
  88.8 6.3 collective-permute-done.19
  102.4 15.8 %collective-permute-done.23 = bf16[256,384]{1,0:T(8,128)(2,1)S(1)} collective-permute-done((bf16[256,384]{1,0:T(8,128)(2,1)}, bf16[256,384]{1,0:T(8,128)(2,1)S(1)}, u32[]{:S(2)}, u32[]{:S(2)}) %collective-permute-start.23) | collective-permute-done | bytes 196640 | tf_op jit(solution)/shard_map/ppermute | solution.py:182
  134.7 16.3 %shard_map.229 = (bf16[1024,384]{1,0:T(8,128)(2,1)S(1)}, bf16[1024,384]{1,0:T(8,128)(2,1)S(1)}, bf16[1024,384]{1,0:T(8,128)(2,1)S(1)}, bf16[1024,384]{1,0:T(8,128)(2,1)S(1)}) custom-call(f32[3,1024,384]{2,1,0:T(8,128)S(1)} %convolution_bitcast_fusion.pre, f32[1024,128]{1,0:T(8,128)S(1)} %copy.69.cosine, f32[1024,128]{1,0:T(8,128)S(1)} %copy.70.sine, ...), custom_call_target="tpu_custom_call" | custom-call | flops 20000000000 | bytes 8388608 | tf_op jit(solution)/shard_map/pallas_call | solution.py:94
  162.8 28.0 %collective-permute-done.11 = bf16[192,2,512]{2,1,0:T(2,128)(2,1)S(1)} collective-permute-done((bf16[192,2,512]{2,1,0:T(2,128)(2,1)S(1)}, bf16[192,2,512]{2,1,0:T(2,128)(2,1)S(1)}, u32[]{:S(2)}, u32[]{:S(2)}) %collective-permute-start.11) | collective-permute-done | bytes 393248 | tf_op jit(solution)/shard_map/ppermute | solution.py:495
  208.4 6.0 convolution_convert_fusion.6
  225.8 5.9 convolution_convert_fusion.2
  245.5 11.7 %fusion.140 = (bf16[2048,768]{1,0:T(8,128)(2,1)S(1)}, f32[2048,768]{1,0:T(8,128)S(1)}) fusion(bf16[2048,2560]{0,1:T(8,128)(2,1)} %fusion.66, bf16[2560,768]{1,0:T(8,128)(2,1)S(1)} %copy-done.118), kind=kOutput, calls=%fused_computation.339 | convolution fusion | flops 8054636544 | bytes 23855104 | tf_op jit(solution)/shard_map/dot_general | solution.py:632
  265.4 16.7 %collective-permute-done.32 = bf16[512,768]{1,0:T(8,128)(2,1)S(1)} collective-permute-done((bf16[512,768]{1,0:T(8,128)(2,1)S(1)}, bf16[512,768]{1,0:T(8,128)(2,1)S(1)}, u32[]{:S(2)}, u32[]{:S(2)}) %collective-permute-start.32) | collective-permute-done | bytes 786464 | tf_op jit(solution)/shard_map/ppermute | solution.py:182
  296.1 5.8 collective-permute-start.40
  307.2 17.1 %collective-permute-done.44 = bf16[512,768]{1,0:T(8,128)(2,1)} collective-permute-done((bf16[512,768]{1,0:T(8,128)(2,1)S(1)}, bf16[512,768]{1,0:T(8,128)(2,1)}, u32[]{:S(2)}, u32[]{:S(2)}) %collective-permute-start.44) | collective-permute-done | bytes 786464 | tf_op jit(solution)/shard_map/ppermute | solution.py:182
  335.1 12.4 %convolution_convert_fusion.1 = bf16[2560,768]{1,0:T(8,128)(2,1)} fusion(bf16[2048,2560]{0,1:T(8,128)(2,1)} %fusion.66, bf16[2048,768]{1,0:T(8,128)(2,1)S(1)} %bitcast.298), kind=kOutput, calls=%fused_computation.39 | convolution fusion | flops 8055029760 | bytes 17563648 | tf_op jit(solution)/shard_map/dot_general | solution.py:641
  347.5 11.3 %convolution_convert_fusion = bf16[2048,2560]{0,1:T(8,128)(2,1)S(1)} fusion(bf16[2048,768]{1,0:T(8,128)(2,1)} %bitcast.299, bf16[2560,768]{1,0:T(8,128)(2,1)} %copy-done.117), kind=kOutput, calls=%fused_computation | convolution fusion | flops 8058306560 | bytes 17563648 | tf_op jit(solution)/shard_map/dot_general | solution.py:642
  363.8 8.0 fusion.53
  371.9 8.9 %fusion.23 = (bf16[2048,512]{0,1:T(8,128)(2,1)}, bf16[2048,512]{0,1:T(8,128)(2,1)}, bf16[2048,512]{0,1:T(8,128)(2,1)}, bf16[2048,512]{0,1:T(8,128)(2,1)}, bf16[2...) fusion(f32[2048]{0:T(1024)S(1)} %bitcast.358, bf16[2048,1024]{0,1:T(8,128)(2,1)S(1)} %copy-done.29, ...), kind=kLoop, calls=%fused_computation.63 | loop fusion | flops 53477376 | bytes 31481856 | tf_op jit(solution)/shard_map/convert.15
  381.0 6.1 fusion.75
  387.2 5.4 fusion.63
  392.6 5.4 fusion.59
  398.1 5.4 fusion.65
  403.6 5.5 fusion.61
  409.1 15.1 %fusion.141 = (bf16[2048,768]{1,0:T(8,128)(2,1)}, f32[2048,768]{1,0:T(8,128)}) fusion(bf16[384,1024]{1,0:T(8,128)(2,1)S(1)} %copy-done.64, bf16[384,1024]{1,0:T(8,128)(2,1)S(1)} %bitcast.311, bf16[2048,512]{0,1:T(8,128)(2,1)} %copy-done.44, bf16[2048,512]{0,1:T(8,128)(2,1)} %copy-done.43, f32[2048,768]{1,0:T(8,128)} %fusion.59, f32[2048,768]{1,0:T(8,128)} %fusion.61, ...), kind=kOutput, calls=%fused_computation.340 | convolution fusion | flops 3240624128 | bytes 40370176 | tf_op jit(solution)/shard_map/dot_general | solution.py:663
  430.3 6.1 fusion.74
  440.8 6.2 fusion.73
  447.1 10.8 %collective-permute-done.47 = bf16[512,768]{1,0:T(8,128)(2,1)S(1)} collective-permute-done((bf16[512,768]{1,0:T(8,128)(2,1)S(1)}, bf16[512,768]{1,0:T(8,128)(2,1)S(1)}, u32[]{:S(2)}, u32[]{:S(2)}) %collective-permute-start.47) | collective-permute-done | bytes 786464 | tf_op jit(solution)/shard_map/ppermute | solution.py:182
  470.1 6.2 shard_map.232
  477.2 6.4 shard_map.231
  484.5 6.2 shard_map.230
  509.8 158.5 %shard_map.233 = (bf16[2,5,48,1024]{3,2,1,0:T(8,128)(2,1)S(1)}, bf16[2,5,64,384]{3,2,1,0:T(8,128)(2,1)S(1)}, bf16[192,384]{1,0:T(8,128)(2,1)S(1)}) custom-call(bf16[2,4,2,48,1024]{4,3,2,1,0:T(8,128)(2,1)S(1)} %bitcast.273, bf16[2,4,2,48,1024]{4,3,2,1,0:T(8,128)(2,1)S(1)} %bitcast.272, bf16[2,4,2,48,1024]{4,3,2,1,0:T(8,128)(2,1)} %bitcast.319, ...), custom_call_target="tpu_custom_call" | custom-call | tf_op jit(solution)/shard_map/pallas_call | solution.py:352
  692.2 156.1 %shard_map.234 = (bf16[4,384,2,1024]{3,2,1,0:T(2,128)(2,1)}, bf16[384,2,1024]{2,1,0:T(2,128)(2,1)}, bf16[4,2,512,384]{3,2,1,0:T(8,128)(2,1)}, bf16[2,512,384]{2,1,0:T(8,128)(2,1)}, bf16[8,4,48,384]{3,2,1,0:T(8,128)(2,1)}) custom-call(bf16[4,48,2,1024]{3,2,1,0:T(2,128)(2,1)} %slice.421.refs_0_, bf16[48,2,1024]{2,1,0:T(2,128)(2,1)} %slice_bitcast_fusion.12.refs_1_, ...), custom_call_target="tpu_custom_call" | custom-call | tf_op jit(solution)/shard_map/pallas_call | solution.py:472
  848.4 5.1 bitcast_convert_fusion
  869.3 6.1 convert_element_type.269
  (596 shorter events, 282.4 us)
Async XLA Ops:
  0.7 52.6 %collective-permute-start.3 = (f32[384]{0:T(512)}, f32[384]{0:T(512)}, u32[]{:S(2)}, u32[]{:S(2)}) collective-permute-start(f32[384]{0:T(512)} %param.19), channel_id=1, source_target_pairs={{0,2},{2,0},{1,3},{3,1},{4,6},{6,4},{5,7},{7,5},{8,10},{10,8},{9,1... | collective-permute-start | bytes 4616 | tf_op jit(solution)/shard_map/ppermute | solution.py:182
  2.0 55.6 %collective-permute-start.6 = (f32[384]{0:T(512)}, f32[384]{0:T(512)}, u32[]{:S(2)}, u32[]{:S(2)}) collective-permute-start(f32[384]{0:T(512)} %param.20), channel_id=1, source_target_pairs={{0,2},{2,0},{1,3},{3,1},{4,6},{6,4},{5,7},{7,5},{8,10},{10,8},{9,1... | collective-permute-start | bytes 4616 | tf_op jit(solution)/shard_map/ppermute | solution.py:182
  3.9 65.1 %collective-permute-start.21 = (bf16[256,384]{1,0:T(8,128)(2,1)}, bf16[256,384]{1,0:T(8,128)(2,1)}, u32[]{:S(2)}, u32[]{:S(2)}) collective-permute-start(bf16[256,384]{1,0:T(8,128)(2,1)} %constant_dynamic-slice_fusion.1), channel_id=1, source_target_pairs={{0,2},{2,0},{1,3},{3,1},{4,6},{6,4},{5,7},{7,5},{8,10},{10,8},{9,1... | collective-permute-start | bytes 589832 | tf_op jit(solution)/shard_map/ppermute | solution.py:182
  5.1 64.0 %collective-permute-start.4 = (bf16[384,384]{1,0:T(8,128)(2,1)}, bf16[384,384]{1,0:T(8,128)(2,1)}, u32[]{:S(2)}, u32[]{:S(2)}) collective-permute-start(bf16[384,384]{1,0:T(8,128)(2,1)} %param.22), channel_id=1, source_target_pairs={{0,2},{2,0},{1,3},{3,1},{4,6},{6,4},{5,7},{7,5},{8,10},{10,8},{9,1... | collective-permute-start | bytes 884744 | tf_op jit(solution)/shard_map/ppermute | solution.py:182
  5.3 34.3 %collective-permute-start = (bf16[1024,384]{1,0:T(8,128)(2,1)}, bf16[1024,384]{1,0:T(8,128)(2,1)}, u32[]{:S(2)}, u32[]{:S(2)}) collective-permute-start(bf16[1024,384]{1,0:T(8,128)(2,1)} %param.14), channel_id=1, source_target_pairs={{1,3},{2,0},{5,7},{6,4},{9,11},{10,8},{13,15},{14,12},{17,19},{18,... | collective-permute-start | bytes 2359304 | tf_op jit(solution)/shard_map/ppermute | solution.py:519
  42.0 56.4 %collective-permute-start.1 = (bf16[2,1024,384]{2,1,0:T(8,128)(2,1)}, bf16[2,1024,384]{2,1,0:T(8,128)(2,1)}, u32[]{:S(2)}, u32[]{:S(2)}) collective-permute-start(bf16[2,1024,384]{2,1,0:T(8,128)(2,1)} %pad_maximum_fusion.30), channel_id=1, source_target_pairs={{0,1},{3,2},{4,5},{7,6},{8,9},{11,10},{12,13},{15,14},{16,17},{19,... | collective-permute-start | bytes 4718600 | tf_op jit(solution)/shard_map/ppermute | solution.py:521
  69.1 26.0 %collective-permute-start.19 = (bf16[192,2,512]{2,1,0:T(2,128)(2,1)}, bf16[192,2,512]{2,1,0:T(2,128)(2,1)S(1)}, u32[]{:S(2)}, u32[]{:S(2)}) collective-permute-start(bf16[192,2,512]{2,1,0:T(2,128)(2,1)} %dynamic-slice_bitcast_fusion.4), channel_id=1, source_target_pairs={{0,2},{2,0},{1,3},{3,1},{4,6},{6,4},{5,7},{7,5},{8,10},{10,8},{9,1... | collective-permute-start | bytes 1179656 | tf_op jit(solution)/shard_map/ppermute | solution.py:182
  71.8 25.4 %collective-permute-start.22 = (bf16[256,384]{1,0:T(8,128)(2,1)}, bf16[256,384]{1,0:T(8,128)(2,1)S(1)}, u32[]{:S(2)}, u32[]{:S(2)}) collective-permute-start(bf16[256,384]{1,0:T(8,128)(2,1)} %collective-permute-done.21), channel_id=1, source_target_pairs={{0,4},{4,0},{8,12},{12,8},{16,20},{20,16},{24,28},{28,24},{1,5},{5... | collective-permute-start | bytes 589832 | tf_op jit(solution)/shard_map/ppermute | solution.py:495
  78.2 52.9 %collective-permute-start.2 = (bf16[384,3,384]{0,2,1:T(8,128)(2,1)}, bf16[384,3,384]{0,2,1:T(8,128)(2,1)S(1)}, u32[]{:S(2)}, u32[]{:S(2)}) collective-permute-start(bf16[384,3,384]{0,2,1:T(8,128)(2,1)} %copy.67), channel_id=1, source_target_pairs={{0,2},{2,0},{1,3},{3,1},{4,6},{6,4},{5,7},{7,5},{8,10},{10,8},{9,1... | collective-permute-start | bytes 2654216 | tf_op jit(solution)/shard_map/ppermute | solution.py:182
  86.6 31.6 %collective-permute-start.23 = (bf16[256,384]{1,0:T(8,128)(2,1)}, bf16[256,384]{1,0:T(8,128)(2,1)S(1)}, u32[]{:S(2)}, u32[]{:S(2)}) collective-permute-start(bf16[256,384]{1,0:T(8,128)(2,1)} %dynamic-slice_bitcast_fusion.11), channel_id=1, source_target_pairs={{0,2},{2,0},{1,3},{3,1},{4,6},{6,4},{5,7},{7,5},{8,10},{10,8},{9,1... | collective-permute-start | bytes 589832 | tf_op jit(solution)/shard_map/ppermute | solution.py:182
  95.0 27.4 %collective-permute-start.25 = (bf16[256,384]{1,0:T(8,128)(2,1)}, bf16[256,384]{1,0:T(8,128)(2,1)S(1)}, u32[]{:S(2)}, u32[]{:S(2)}) collective-permute-start(bf16[256,384]{1,0:T(8,128)(2,1)} %dynamic-slice_bitcast_fusion.10), channel_id=1, source_target_pairs={{0,2},{2,0},{1,3},{3,1},{4,6},{6,4},{5,7},{7,5},{8,10},{10,8},{9,1... | collective-permute-start | bytes 589832 | tf_op jit(solution)/shard_map/ppermute | solution.py:182
  97.2 29.4 %collective-permute-start.27 = (bf16[256,384]{1,0:T(8,128)(2,1)}, bf16[256,384]{1,0:T(8,128)(2,1)S(1)}, u32[]{:S(2)}, u32[]{:S(2)}) collective-permute-start(bf16[256,384]{1,0:T(8,128)(2,1)} %dynamic-slice_bitcast_fusion.9), channel_id=1, source_target_pairs={{0,2},{2,0},{1,3},{3,1},{4,6},{6,4},{5,7},{7,5},{8,10},{10,8},{9,1... | collective-permute-start | bytes 589832 | tf_op jit(solution)/shard_map/ppermute | solution.py:182
  98.4 32.4 %collective-permute-start.29 = (bf16[256,384]{1,0:T(8,128)(2,1)}, bf16[256,384]{1,0:T(8,128)(2,1)S(1)}, u32[]{:S(2)}, u32[]{:S(2)}) collective-permute-start(bf16[256,384]{1,0:T(8,128)(2,1)} %dynamic-slice_bitcast_fusion.8), channel_id=1, source_target_pairs={{0,2},{2,0},{1,3},{3,1},{4,6},{6,4},{5,7},{7,5},{8,10},{10,8},{9,1... | collective-permute-start | bytes 589832 | tf_op jit(solution)/shard_map/ppermute | solution.py:182
  118.2 39.0 %collective-permute-start.10 = (bf16[192,2,512]{2,1,0:T(2,128)(2,1)S(1)}, bf16[192,2,512]{2,1,0:T(2,128)(2,1)S(1)}, u32[]{:S(2)}, u32[]{:S(2)}) collective-permute-start(bf16[192,2,512]{2,1,0:T(2,128)(2,1)S(1)} %copy-done.112), channel_id=1, source_target_pairs={{0,2},{2,0},{1,3},{3,1},{4,6},{6,4},{5,7},{7,5},{8,10},{10,8},{9,1... | collective-permute-start | bytes 1179656 | tf_op jit(solution)/shard_map/ppermute | solution.py:182
  122.4 29.7 %collective-permute-start.24 = (bf16[256,384]{1,0:T(8,128)(2,1)S(1)}, bf16[256,384]{1,0:T(8,128)(2,1)S(1)}, u32[]{:S(2)}, u32[]{:S(2)}) collective-permute-start(bf16[256,384]{1,0:T(8,128)(2,1)S(1)} %collective-permute-done.23), channel_id=1, source_target_pairs={{0,4},{4,0},{8,12},{12,8},{16,20},{20,16},{24,28},{28,24},{1,5},{5... | collective-permute-start | bytes 589832 | tf_op jit(solution)/shard_map/ppermute | solution.py:495
  126.6 28.2 %collective-permute-start.26 = (bf16[256,384]{1,0:T(8,128)(2,1)S(1)}, bf16[256,384]{1,0:T(8,128)(2,1)S(1)}, u32[]{:S(2)}, u32[]{:S(2)}) collective-permute-start(bf16[256,384]{1,0:T(8,128)(2,1)S(1)} %collective-permute-done.25), channel_id=1, source_target_pairs={{0,4},{4,0},{8,12},{12,8},{16,20},{20,16},{24,28},{28,24},{1,5},{5... | collective-permute-start | bytes 589832 | tf_op jit(solution)/shard_map/ppermute | solution.py:495
  130.8 24.6 %collective-permute-start.28 = (bf16[256,384]{1,0:T(8,128)(2,1)S(1)}, bf16[256,384]{1,0:T(8,128)(2,1)S(1)}, u32[]{:S(2)}, u32[]{:S(2)}) collective-permute-start(bf16[256,384]{1,0:T(8,128)(2,1)S(1)} %collective-permute-done.27), channel_id=1, source_target_pairs={{0,4},{4,0},{8,12},{12,8},{16,20},{20,16},{24,28},{28,24},{1,5},{5... | collective-permute-start | bytes 589832 | tf_op jit(solution)/shard_map/ppermute | solution.py:495
  131.1 28.4 %collective-permute-start.30 = (bf16[256,384]{1,0:T(8,128)(2,1)S(1)}, bf16[256,384]{1,0:T(8,128)(2,1)S(1)}, u32[]{:S(2)}, u32[]{:S(2)}) collective-permute-start(bf16[256,384]{1,0:T(8,128)(2,1)S(1)} %collective-permute-done.29), channel_id=1, source_target_pairs={{0,4},{4,0},{8,12},{12,8},{16,20},{20,16},{24,28},{28,24},{1,5},{5... | collective-permute-start | bytes 589832 | tf_op jit(solution)/shard_map/ppermute | solution.py:495
  154.9 38.0 %collective-permute-start.14 = (bf16[192,2,512]{2,1,0:T(2,128)(2,1)S(1)}, bf16[192,2,512]{2,1,0:T(2,128)(2,1)S(1)}, u32[]{:S(2)}, u32[]{:S(2)}) collective-permute-start(bf16[192,2,512]{2,1,0:T(2,128)(2,1)S(1)} %copy-done.114), channel_id=1, source_target_pairs={{0,4},{4,0},{8,12},{12,8},{16,20},{20,16},{24,28},{28,24},{1,5},{5... | collective-permute-start | bytes 1179656 | tf_op jit(solution)/shard_map/ppermute | solution.py:495
  155.4 42.5 %collective-permute-start.16 = (bf16[192,2,512]{2,1,0:T(2,128)(2,1)S(1)}, bf16[192,2,512]{2,1,0:T(2,128)(2,1)S(1)}, u32[]{:S(2)}, u32[]{:S(2)}) collective-permute-start(bf16[192,2,512]{2,1,0:T(2,128)(2,1)S(1)} %collective-permute-done.15), channel_id=1, source_target_pairs={{0,4},{4,0},{8,12},{12,8},{16,20},{20,16},{24,28},{28,24},{1,5},{5... | collective-permute-start | bytes 1179656 | tf_op jit(solution)/shard_map/ppermute | solution.py:495
  157.2 42.5 %collective-permute-start.18 = (bf16[192,2,512]{2,1,0:T(2,128)(2,1)S(1)}, bf16[192,2,512]{2,1,0:T(2,128)(2,1)S(1)}, u32[]{:S(2)}, u32[]{:S(2)}) collective-permute-start(bf16[192,2,512]{2,1,0:T(2,128)(2,1)S(1)} %collective-permute-done.17), channel_id=1, source_target_pairs={{0,4},{4,0},{8,12},{12,8},{16,20},{20,16},{24,28},{28,24},{1,5},{5... | collective-permute-start | bytes 1179656 | tf_op jit(solution)/shard_map/ppermute | solution.py:495
  157.5 33.3 %collective-permute-start.11 = (bf16[192,2,512]{2,1,0:T(2,128)(2,1)S(1)}, bf16[192,2,512]{2,1,0:T(2,128)(2,1)S(1)}, u32[]{:S(2)}, u32[]{:S(2)}) collective-permute-start(bf16[192,2,512]{2,1,0:T(2,128)(2,1)S(1)} %collective-permute-done.10), channel_id=1, source_target_pairs={{0,4},{4,0},{8,12},{12,8},{16,20},{20,16},{24,28},{28,24},{1,5},{5... | collective-permute-start | bytes 1179656 | tf_op jit(solution)/shard_map/ppermute | solution.py:495
  159.6 34.6 %collective-permute-start.8 = (bf16[512,768]{1,0:T(8,128)(2,1)S(1)}, bf16[512,768]{1,0:T(8,128)(2,1)S(1)}, u32[]{:S(2)}, u32[]{:S(2)}) collective-permute-start(bf16[512,768]{1,0:T(8,128)(2,1)S(1)} %pad_maximum_fusion.51), channel_id=1, source_target_pairs={{0,2},{2,0},{1,3},{3,1},{4,6},{6,4},{5,7},{7,5},{8,10},{10,8},{9,1... | collective-permute-start | bytes 2359304 | tf_op jit(solution)/shard_map/ppermute | solution.py:182
  197.9 61.5 %collective-permute-start.41 = (bf16[1024,384]{1,0:T(8,128)(2,1)S(1)}, bf16[1024,384]{1,0:T(8,128)(2,1)S(1)}, u32[]{:S(2)}, u32[]{:S(2)}) collective-permute-start(bf16[1024,384]{1,0:T(8,128)(2,1)S(1)} %copy-done.58), channel_id=1, source_target_pairs={{1,3},{2,0},{5,7},{6,4},{9,11},{10,8},{13,15},{14,12},{17,19},{18,... | collective-permute-start | bytes 2359304 | tf_op jit(solution)/shard_map/ppermute | solution.py:519
  305.3 19.0 %collective-permute-start.44 = (bf16[512,768]{1,0:T(8,128)(2,1)S(1)}, bf16[512,768]{1,0:T(8,128)(2,1)}, u32[]{:S(2)}, u32[]{:S(2)}) collective-permute-start(bf16[512,768]{1,0:T(8,128)(2,1)S(1)} %pad_maximum_fusion.53), channel_id=1, source_target_pairs={{0,2},{2,0},{1,3},{3,1},{4,6},{6,4},{5,7},{7,5},{8,10},{10,8},{9,1... | collective-permute-start | bytes 2359304 | tf_op jit(solution)/shard_map/ppermute | solution.py:182
  306.6 19.7 %collective-permute-start.33 = (f32[512,384]{1,0:T(8,128)}, f32[512,384]{1,0:T(8,128)}, u32[]{:S(2)}, u32[]{:S(2)}) collective-permute-start(f32[512,384]{1,0:T(8,128)} %get-tuple-element.89), channel_id=1, source_target_pairs={{0,1},{1,0},{2,3},{3,2},{4,5},{5,4},{6,7},{7,6},{8,9},{9,8},{10,11... | collective-permute-start | bytes 2359304 | tf_op jit(solution)/shard_map/ppermute | solution.py:182
  307.2 24.2 %collective-permute-start.43 = (bf16[512,768]{1,0:T(8,128)(2,1)}, bf16[512,768]{1,0:T(8,128)(2,1)}, u32[]{:S(2)}, u32[]{:S(2)}) collective-permute-start(bf16[512,768]{1,0:T(8,128)(2,1)} %multiply_convert_fusion.3), channel_id=1, source_target_pairs={{0,1},{1,0},{2,3},{3,2},{4,5},{5,4},{6,7},{7,6},{8,9},{9,8},{10,11... | collective-permute-start | bytes 2359304 | tf_op jit(solution)/shard_map/ppermute | solution.py:182
  329.5 135.7 %collective-permute-start.34 = (f32[1024,384]{1,0:T(8,128)}, f32[1024,384]{1,0:T(8,128)}, u32[]{:S(2)}, u32[]{:S(2)}) collective-permute-start(f32[1024,384]{1,0:T(8,128)} %maximum_select_fusion), channel_id=1, source_target_pairs={{1,2},{2,1},{5,6},{6,5},{9,10},{10,9},{13,14},{14,13},{17,18},{18,... | collective-permute-start | bytes 4718600 | tf_op jit(solution)/shard_map/ppermute | solution.py:533
  380.9 55.5 %collective-permute-start.48 = (f32[2,4,512]{2,1,0:T(4,128)S(1)}, f32[2,4,512]{2,1,0:T(4,128)S(1)}, u32[]{:S(2)}, u32[]{:S(2)}) collective-permute-start(f32[2,4,512]{2,1,0:T(4,128)S(1)} %pad_maximum_fusion.59), channel_id=1, source_target_pairs={{0,1},{1,0},{2,3},{3,2},{4,5},{5,4},{6,7},{7,6},{8,9},{9,8},{10,11... | collective-permute-start | bytes 49160 | tf_op jit(solution)/shard_map/ppermute | solution.py:182
  506.9 166.8 %collective-permute-start.51 = (bf16[512,768]{1,0:T(8,128)(2,1)}, bf16[512,768]{1,0:T(8,128)(2,1)}, u32[]{:S(2)}, u32[]{:S(2)}) collective-permute-start(bf16[512,768]{1,0:T(8,128)(2,1)} %fusion.90), channel_id=1, source_target_pairs={{0,1},{1,0},{2,3},{3,2},{4,5},{5,4},{6,7},{7,6},{8,9},{9,8},{10,11... | collective-permute-start | bytes 2359304 | tf_op jit(solution)/shard_map/ppermute | solution.py:182
  686.5 191.4 %collective-permute-start.58 = (f32[1024,384]{1,0:T(8,128)S(1)}, f32[1024,384]{1,0:T(8,128)}, u32[]{:S(2)}, u32[]{:S(2)}) collective-permute-start(f32[1024,384]{1,0:T(8,128)S(1)} %maximum_select_fusion.2), channel_id=1, source_target_pairs={{1,2},{2,1},{5,6},{6,5},{9,10},{10,9},{13,14},{14,13},{17,18},{18,... | collective-permute-start | bytes 4718600 | tf_op jit(solution)/shard_map/ppermute | solution.py:533
  689.3 159.0 %collective-permute-start.53 = (f32[4609]{0:T(1024)S(1)}, f32[4609]{0:T(1024)S(1)}, u32[]{:S(2)}, u32[]{:S(2)}) collective-permute-start(f32[4609]{0:T(1024)S(1)} %fusion.173), channel_id=1, source_target_pairs={{0,8},{4,12},{8,0},{12,4},{16,24},{20,28},{24,16},{28,20},{1,9},{5... | collective-permute-start | bytes 55316 | tf_op jit(solution)/shard_map/ppermute | solution.py:197
  (172 other events, 2235.0 us)

commit v3 on v2

--- a/solution.py
+++ b/solution.py
@@ -16,11 +16,6 @@
 F32 = jnp.float32
 
 
-def norm_forward(values, gain_vec):
-    rstd_rows = lax.rsqrt(jnp.mean(values * values, axis=1) + 1e-06)
-    return (rstd_rows, values * rstd_rows[:, None] * gain_vec)
-
-
 def norm_backward(values, rstd_rows, gain_vec, incoming):
     scaled = incoming * gain_vec
     inner_sum = jnp.sum(scaled * values, axis=1)
@@ -61,53 +56,321 @@
     return weight * (1.0 / jnp.sum(weight, axis=0, keepdims=True))
 
 
-def attend_kernel(pre, cosine, sine, seg_row, seg_col, queries, keys, values, context):
-    rows = pre.shape[1]
+def front_kernel(
+    n, x_in, w_qkv, w_out, vectors, shared_up, expert_up, shared_down, expert_down,
+    cosine, sine, seg_row, seg_col,
+    queries, keys, values, context, normed, x_own, hidden, w_qkv_peer, w_out_peer, vec_peer, up_own,
+    tokens, up_peer, down_peer,
+    x_pair, qkv_own, out_own, up_raw, part_raw, up_part, pre, att_send, att_recv, low, low_flip,
+    own_sem, x_send, x_recv, w_send, w_recv, t_send, t_recv,
+):
+    me = lax.axis_index("dp")
+    row, col = lax.axis_index("row"), lax.axis_index("col")
+    z, x = me // 2, me % 2
+    low_z = lax.rem(z, 2)
+    x_peer = {"dp": 2 * z + (1 - x)}
+    z_peer = {"dp": 2 * (z + 1 - 2 * low_z) + x}
+    row_peer, core = {"row": 1 - row}, {"col": 1 - col}
+    mine = 2 * low_z + x
+    of_x, of_z = 2 * low_z + (1 - x), 2 * (1 - low_z) + x
+    rows, half = x_in.shape
+    part = rows // 2
+    quarter = shared_up.shape[2] // 2
+    slots = expert_up.shape[0] + 1
+    greet([row_peer, core, x_peer, z_peer])
+
+    def split(index, size):
+        return pl.ds(pl.multiple_of(index * size, 16), size)
+
+    def source(item, index):
+        if item == 0:
+            return w_qkv.at[:, split(index, half // 4)]
+        if item == 1:
+            return w_out.at[split(index, w_out.shape[0] // 4)]
+        slot, kind = (item - 2) // 2, (item - 2) % 2
+        if kind == 0:
+            return up_part.at[slot]
+        ref = shared_down if slot == 0 else expert_down.at[slot - 1]
+        first = (1 - row) * quarter + index * (quarter // 4)
+        return ref.at[pl.ds(pl.multiple_of(first, 16), quarter // 4)]
+
+    def landing(item, index):
+        if item == 0:
+            return w_qkv_peer.at[:, split(index, half // 4)]
+        if item == 1:
+            return w_out_peer.at[split(index, w_out.shape[0] // 4)]
+        slot, kind = (item - 2) // 2, (item - 2) % 2
+        if kind == 0:
+            return up_peer.at[slot, split(index, half // 4)]
+        return down_peer.at[slot, split(index, quarter // 4)]
+
+    count = 2 + 2 * slots
+    copies = {}
+
+    def start(item, leg, src, device, index):
+        copy = remote(
+            src, landing(item, index), w_send.at[item, leg], w_recv.at[item, leg], device
+        )
+        copy.start()
+        copies[item, leg] = copy
+
+    def fetch(item):
+        start(item, 0, source(item, mine), row_peer, mine)
+
+    def pass_on(item):
+        copies[item, 0].wait_recv()
+        start(item, 1, landing(item, mine), x_peer, mine)
+        start(item, 2, landing(item, mine), z_peer, mine)
+
+    def by_x(item):
+        return (item - item // 4) % 2 == 0
+
+    def pass_far(item):
+        if by_x(item):
+            copies[item, 1].wait_recv()
+            start(item, 3, landing(item, of_x), z_peer, of_x)
+        else:
+            copies[item, 2].wait_recv()
+            start(item, 3, landing(item, of_z), x_peer, of_z)
+
+    def arrive(item):
+        copies[item, 2 if by_x(item) else 1].wait_recv()
+        copies[item, 3].wait_recv()
+
+    progress = [0]
+
+    def pump():
+        at = progress[0]
+        progress[0] += 1
+        if 2 <= at - 1 < count:
+            pass_far(at - 1)
+        if 2 <= at < count:
+            pass_on(at)
+
+    diagonal = row == col
+    over_row = remote(x_in, x_pair.at[1], x_send.at[0], x_recv.at[0], row_peer)
+    across_own = remote(x_in, x_pair.at[0], x_send.at[1], x_recv.at[1], core)
+    across_peer = remote(x_pair.at[1], x_pair.at[1], x_send.at[2], x_recv.at[2], core)
+    own_x = pltpu.make_async_copy(x_in, x_pair.at[0], own_sem.at[0])
+
+    @pl.when(diagonal)
+    def _():
+        own_x.start()
+        across_own.start()
+
+    @pl.when(jnp.logical_not(diagonal))
+    def _():
+        over_row.start()
+
+    def up_slot(slot):
+        return shared_up if slot == 0 else expert_up.at[slot - 1]
+
+    keep_lanes = pl.ds(pl.multiple_of(row * quarter, 128), quarter)
+    send_lanes = pl.ds(pl.multiple_of((1 - row) * quarter, 128), quarter)
+    part_loads, up_loads = [], []
+    for slot in range(slots):
+        piece = up_slot(slot).at[pl.ds(mine * (half // 4), half // 4), :, send_lanes]
+        part_loads.append(pltpu.make_async_copy(piece, part_raw.at[slot], own_sem.at[4 + slot]))
+        part_loads[slot].start()
+
+    def split_own(slot):
+        up_loads[slot].wait()
+        for k in range(2):
+            up_own[slot, :, k * quarter : (k + 1) * quarter] = up_raw[slot, :, k]
+
+    give_vectors = remote(vectors, vec_peer, x_send.at[3], x_recv.at[3], row_peer)
+    give_vectors.start()
+    fetch(0)
+    fetch(1)
+    own_qkv = pltpu.make_async_copy(w_qkv, qkv_own, own_sem.at[1])
+    own_qkv.start()
+    own_out = pltpu.make_async_copy(w_out, out_own, own_sem.at[2])
+    own_out.start()
+
+    for slot in range(slots):
+        piece = up_slot(slot).at[:, :, keep_lanes]
+        up_loads.append(
+            pltpu.make_async_copy(piece, up_raw.at[slot], own_sem.at[4 + slots + slot])
+        )
+        up_loads[slot].start()
+    for slot in range(slots):
+        part_loads[slot].wait()
+        for k in range(2):
+            up_part[slot, :, k * quarter : (k + 1) * quarter] = part_raw[slot, :, k]
+
+    @pl.when(diagonal)
+    def _():
+        over_row.wait_recv()
+        across_peer.start()
+        own_x.wait()
+
+    @pl.when(jnp.logical_not(diagonal))
+    def _():
+        over_row.wait_send()
+
+    for item in range(2, count):
+        fetch(item)
+    pass_on(0)
+    pass_on(1)
+    split_own(0)
+
+    @pl.when(jnp.logical_not(diagonal))
+    def _():
+        across_own.wait_recv()
+        across_peer.wait_recv()
+
+    give_vectors.wait_recv()
+    progress[0] = 2
+    x_first, x_second = x_pair[0].astype(F32), x_pair[1].astype(F32)
+    squares = jnp.sum(x_first * x_first, axis=1, keepdims=True)
+    squares = squares + jnp.sum(x_second * x_second, axis=1, keepdims=True)
+    rstd = lax.rsqrt(squares / (2 * half) + 1e-06)
+    normed[0] = (x_first * rstd * vectors[0:1]).astype(BF)
+    normed[1] = (x_second * rstd * vec_peer[0:1]).astype(BF)
+    pass_far(0)
+    pass_far(1)
+    for slot in range(1, slots):
+        split_own(slot)
+    arrive(0)
+    own_qkv.wait()
+    for j in range(3):
+        pre[j] = jnp.dot(normed[0], qkv_own[j], preferred_element_type=F32) + jnp.dot(
+            normed[1], w_qkv_peer[j], preferred_element_type=F32
+        )
+        pump()
+
     first = lanes_of((rows, PAIR)) % HEAD_DIM < HEAD_DIM // 2
+    lower = lanes_of((ABLOCK, PAIR)) < HEAD_DIM
     cos, sin = cosine[...], sine[...]
-    query = pre[0]
-    queries[...] = ((query * cos + turn(query, first) * sin) * HEAD_DIM**-0.5).astype(BF)
-    key = pre[1]
-    keys[...] = (key * cos + turn(key, first) * sin).astype(BF)
-    value = pre[2]
-    values[...] = value.astype(BF)
-    value_t = value.T.astype(BF)
-    lower = lanes_of((ABLOCK, PAIR)) < HEAD_DIM
-    for block in range(rows // ABLOCK):
-        start, stop = block * ABLOCK, (block + 1) * ABLOCK
-        query = queries[start:stop]
-        parts = []
-        for head in range(2):
-            query_head = jnp.where(lower == (head == 0), query, jnp.zeros_like(query))
-            shares = shares_of(
-                keys[:stop], query_head, seg_col[:stop], seg_row[:, start:stop]
-            ).astype(BF)
-            parts.append(jnp.dot(value_t[:, :stop], shares, preferred_element_type=F32))
-        both = jnp.concatenate([parts[0][:HEAD_DIM], parts[1][HEAD_DIM:]], axis=0)
-        context[start:stop] = both.T.astype(BF)
-
-
-def attend_forward(pre, tables, seg_row, seg_col):
-    _, rows, width = pre.shape
-    block = pl.BlockSpec((rows, PAIR), lambda i: (0, i))
-    whole = pl.BlockSpec((rows, PAIR), lambda i: (0, 0))
+    for pair in range(half // PAIR):
+        lanes = slice(pair * PAIR, (pair + 1) * PAIR)
+        query = pre[0, :, lanes]
+        queries[:, lanes] = ((query * cos + turn(query, first) * sin) * HEAD_DIM**-0.5).astype(BF)
+        key = pre[1, :, lanes]
+        keys[:, lanes] = (key * cos + turn(key, first) * sin).astype(BF)
+        value = pre[2, :, lanes]
+        values[:, lanes] = value.astype(BF)
+        value_t = value.T.astype(BF)
+        for block in range(rows // ABLOCK):
+            begin, stop = block * ABLOCK, (block + 1) * ABLOCK
+            query = queries[begin:stop, lanes]
+            parts = []
+            for head in range(2):
+                query_head = jnp.where(lower == (head == 0), query, jnp.zeros_like(query))
+                shares = shares_of(
+                    keys[:stop, lanes], query_head, seg_col[:stop], seg_row[:, begin:stop]
+                ).astype(BF)
+                parts.append(jnp.dot(value_t[:, :stop], shares, preferred_element_type=F32))
+            both = jnp.concatenate([parts[0][:HEAD_DIM], parts[1][HEAD_DIM:]], axis=0)
+            context[begin:stop, lanes] = both.T.astype(BF)
+            if block % 2 == 1:
+                pump()
+
+    arrive(1)
+    own_out.wait()
+    there, here = split(1 - col, part), split(col, part)
+    for at, weight in enumerate((out_own, w_out_peer)):
+        att_send[:, at * half : (at + 1) * half] = jnp.dot(
+            context[there], weight[...], preferred_element_type=F32
+        ).astype(BF)
+    swap_att = remote(att_send, att_recv, t_send.at[0], t_recv.at[0], core)
+    swap_att.start()
+    pump()
+    for at, weight in enumerate((out_own, w_out_peer)):
+        lanes = slice(at * half, (at + 1) * half)
+        x_own[at] = x_pair[at, here]
+        hidden[:, lanes] = x_own[at].astype(F32) + jnp.dot(
+            context[here], weight[...], preferred_element_type=F32
+        )
+    swap_att.wait_recv()
+    total = hidden[...] + att_recv[...].astype(F32)
+    hidden[...] = total
+    rstd = lax.rsqrt(jnp.mean(total * total, axis=1, keepdims=True) + 1e-06)
+    gains = jnp.concatenate([vectors[1:2], vec_peer[1:2]], axis=1)
+    total = (total * rstd * gains).astype(BF)
+    low[...] = total
+    low_flip[:, :half] = total[:, half:]
+    low_flip[:, half:] = total[:, :half]
+    own_tokens = pltpu.make_async_copy(low, tokens.at[0], own_sem.at[3])
+    own_tokens.start()
+    far = remote(low_flip, tokens.at[2], t_send.at[1], t_recv.at[1], row_peer)
+    far.start()
+    near = remote(low, tokens.at[1], t_send.at[2], t_recv.at[2], core)
+    near.start()
+    while progress[0] <= count:
+        pump()
+    far.wait_recv()
+    far_near = remote(tokens.at[2], tokens.at[3], t_send.at[3], t_recv.at[3], core)
+    far_near.start()
+    for item in range(2, count):
+        arrive(item)
+    near.wait_recv()
+    far_near.wait_recv()
+    own_tokens.wait()
+    for copy in (give_vectors, swap_att, far, near, far_near, *copies.values()):
+        copy.wait_send()
+
+    @pl.when(diagonal)
+    def _():
+        across_own.wait_send()
+        across_peer.wait_send()
+
+
+def front(x_in, w_qkv, w_out, vectors, shared_up, expert_up, shared_down, expert_down, tables, seg):
+    n = lax.axis_size("dp")
+    rows, half = x_in.shape
+    quarter = shared_up.shape[2] // 2
+    slots = expert_up.shape[0] + 1
+    count = 2 + 2 * slots
+    sems = pltpu.SemaphoreType.DMA
+    any_spec = pl.BlockSpec(memory_space=pl.ANY)
+    vmem_spec = pl.BlockSpec(memory_space=pltpu.VMEM)
+    shape = jax.ShapeDtypeStruct
+    wide = w_out.shape[0]
     return pl.pallas_call(
-        attend_kernel,
-        grid=(width // PAIR,),
-        out_shape=[jax.ShapeDtypeStruct((rows, width), BF)] * 4,
-        in_specs=[
-            pl.BlockSpec((3, rows, PAIR), lambda i: (0, 0, i)),
-            whole,
-            whole,
-            pl.BlockSpec((1, rows), lambda i: (0, 0)),
-            pl.BlockSpec((rows, 1), lambda i: (0, 0)),
-        ],
-        out_specs=[block] * 4,
-        compiler_params=pltpu.CompilerParams(vmem_limit_bytes=40 << 20),
-        cost_estimate=pl.CostEstimate(
-            flops=20_000_000_000, bytes_accessed=8 << 20, transcendentals=4 << 20
+        functools.partial(front_kernel, n),
+        out_shape=[shape((rows, wide), BF)] * 4
+        + [
+            shape((2, rows, half), BF),
+            shape((2, rows // 2, half), BF),
+            shape((rows // 2, 2 * half), F32),
+            shape(w_qkv.shape, BF),
+            shape(w_out.shape, BF),
+            shape(vectors.shape, F32),
+            shape((slots, half, 2 * quarter), BF),
+            shape((4, rows // 2, 2 * half), BF),
+            shape((slots, half, 2 * quarter), BF),
+            shape((slots, quarter, half), BF),
+        ],
+        in_specs=[any_spec] * 3 + [vmem_spec] + [any_spec] * 4 + [vmem_spec] * 4,
+        out_specs=[vmem_spec] * 11 + [any_spec] * 3,
+        scratch_shapes=[
+            pltpu.VMEM((2, rows, half), BF),
+            pltpu.VMEM(w_qkv.shape, BF),
+            pltpu.VMEM(w_out.shape, BF),
+            pltpu.VMEM((slots, half, 2, quarter), BF),
+            pltpu.VMEM((slots, half // 4, 2, quarter), BF),
+            pltpu.VMEM((slots, half // 4, 2 * quarter), BF),
+            pltpu.VMEM((3, rows, wide), F32),
+            pltpu.VMEM((rows // 2, 2 * half), BF),
+            pltpu.VMEM((rows // 2, 2 * half), BF),
+            pltpu.VMEM((rows // 2, 2 * half), BF),
+            pltpu.VMEM((rows // 2, 2 * half), BF),
+            sems((4 + 2 * slots,)),
+            sems((4,)),
+            sems((4,)),
+            sems((count, 4)),
+            sems((count, 4)),
+            sems((4,)),
+            sems((4,)),
+        ],
+        compiler_params=pltpu.CompilerParams(
+            collective_id=2, has_side_effects=True, vmem_limit_bytes=48 << 20
         ),
-    )(pre, tables[0], tables[1], seg_row, seg_col)
+    )(
+        x_in, w_qkv, w_out, vectors, shared_up, expert_up, shared_down, expert_down,
+        tables[0], tables[1], seg[None, :], seg[:, None],
+    )
 
 
 def attend_back_kernel(
@@ -224,13 +487,12 @@
 
 
 def reduce_kernel(n, slots, *refs):
-    ups, (down, attn) = refs[:slots], refs[slots : slots + 2]
-    up_out, down_out, attn_out = refs[slots + 2 : slots + 5]
+    ups, down, attn, up_out, down_out, attn_out = refs[:6]
     (
         up_keep, down_keep, attn_keep, up_x, down_x, attn_x, up_z, down_z, attn_z,
         up_done, down_done, attn_done, attn_y,
         keep_sem, x_send, x_recv, z_send, z_recv, out_sem, y_send, y_recv,
-    ) = refs[slots + 5 :]
+    ) = refs[6:]
     me = lax.axis_index("dp")
     row = lax.axis_index("row")
     deep = n // 2
@@ -251,7 +513,7 @@
         if kind == "down":
             return down.at[at], down_keep.at[at], down_x.at[at], down_z.at[at], down_done.at[at]
         if kind == "up":
-            return ups[at // 2].at[at % 2], up_keep.at[at], up_x.at[at], up_z.at[at], up_done.at[at]
+            return ups.at[at // 2, at % 2], up_keep.at[at], up_x.at[at], up_z.at[at], up_done.at[at]
         return None, attn_keep.at[:, x], attn_x, attn_z, attn_done
 
     y_first = remote(attn.at[1], attn_y, y_send.at[last], y_recv.at[last], peer)
@@ -342,8 +604,8 @@
 def dp_reduce(up_grads, down_grad, attn_grad):
     n = lax.axis_size("dp")
     deep = n // 2
-    slots = len(up_grads)
-    up_tail, down_tail, attn_tail = up_grads[0].shape[3:], down_grad.shape[3:], attn_grad.shape[3:]
+    slots = up_grads.shape[0]
+    up_tail, down_tail, attn_tail = up_grads.shape[4:], down_grad.shape[3:], attn_grad.shape[3:]
     sems = pltpu.SemaphoreType.DMA
     count = 3 * slots + 1
     vmem = lambda *shape: pltpu.VMEM(shape, BF)
@@ -356,7 +618,7 @@
             jax.ShapeDtypeStruct((2, slots, down_tail[0], half), BF),
             jax.ShapeDtypeStruct(attn_tail, BF),
         ],
-        in_specs=[any_spec] * (slots + 2),
+        in_specs=[any_spec] * 3,
         out_specs=[any_spec] * 3,
         scratch_shapes=[
             vmem(2 * slots, deep, *up_tail),
@@ -384,7 +646,7 @@
         compiler_params=pltpu.CompilerParams(
             collective_id=1, has_side_effects=True, vmem_limit_bytes=48 << 20
         ),
-    )(*up_grads, down_grad, attn_grad)
+    )(up_grads, down_grad, attn_grad)
 
 
 def order_pair(first_is_own, own, other, axis):
@@ -485,20 +747,175 @@
     )(*pieces)
 
 
-def half_by_x(values, axis):
-    size = values.shape[axis] // 2
-    return lax.dynamic_slice_in_dim(values, (lax.axis_index("dp") % 2) * size, size, axis)
-
-
-def fetch_row(values, axis):
-    first = swap(half_by_x(values, axis), "row")
-    second = lax.ppermute(first, "dp", dp_pairs(0))
-    return order_pair(lax.axis_index("dp") % 2 == 0, first, second, axis)
-
-
-def silu_parts(values):
-    sigma = jax.nn.sigmoid(values)
-    return (values * sigma, sigma * (1.0 + values * (1.0 - sigma)))
+TN = (((0,), (0,)), ((), ()))
+TILE = 512
+
+
+def column(values, index):
+    return jnp.sum(jnp.where(lanes_of(values.shape) == index, values, 0.0), axis=1, keepdims=True)
+
+
+def ffn_kernel(tokens, up_own, up_peer, down_own, down_peer, mix, pre, act, out):
+    slot = pl.program_id(0)
+    quarter = down_own.shape[1]
+    w_up = jnp.concatenate([up_own[0], up_peer[0]], axis=0)
+    w_down = jnp.concatenate([down_own[0], down_peer[0]], axis=1)
+    for tile in range(tokens.shape[0] // TILE):
+        rows = pl.ds(tile * TILE, TILE)
+        both = jnp.dot(tokens[rows], w_up, preferred_element_type=F32)
+        pre[0, rows] = both.astype(BF)
+        gate, up = both[:, :quarter], both[:, quarter:]
+        hidden = gate / (1.0 + jnp.exp(-gate)) * up * column(mix[rows], slot)
+        act[0, rows] = hidden.astype(BF)
+        part = jnp.dot(hidden.astype(BF), w_down, preferred_element_type=F32)
+
+        @pl.when(slot == 0)
+        def _():
+            out[rows] = part
+
+        @pl.when(slot > 0)
+        def _():
+            out[rows] += part
+
+
+def ffn_forward(tokens, up_own, up_peer, down_own, down_peer, mix):
+    slots, half, width = up_own.shape
+    rows, depth = tokens.shape
+    per_slot = lambda *shape: pl.BlockSpec((1,) + shape, lambda e: (e, 0, 0))
+    whole = lambda *shape: pl.BlockSpec(shape, lambda e: (0, 0))
+    return pl.pallas_call(
+        ffn_kernel,
+        grid=(slots,),
+        out_shape=[
+            jax.ShapeDtypeStruct((slots, rows, width), BF),
+            jax.ShapeDtypeStruct((slots, rows, width // 2), BF),
+            jax.ShapeDtypeStruct((rows, depth), F32),
+        ],
+        in_specs=[
+            whole(rows, depth),
+            per_slot(half, width),
+            per_slot(half, width),
+            per_slot(width // 2, half),
+            per_slot(width // 2, half),
+            whole(rows, 8),
+        ],
+        out_specs=[per_slot(rows, width), per_slot(rows, width // 2), whole(rows, depth)],
+        compiler_params=pltpu.CompilerParams(vmem_limit_bytes=56 << 20),
+        cost_estimate=pl.CostEstimate(
+            flops=3 * slots * rows * depth * width,
+            bytes_accessed=40 << 20,
+            transcendentals=slots * rows * width // 2,
+        ),
+    )(tokens, up_own, up_peer, down_own, down_peer, mix)
+
+
+def ffn_back_kernel(
+    grads, tokens, pre, act, down_own, down_peer, mix, down_grad, up_grad, pre_grad, gate_sum
+):
+    slot = pl.program_id(0)
+    quarter = down_own.shape[1]
+    w_down = jnp.concatenate([down_own[0], down_peer[0]], axis=1)
+    depth = tokens.shape[1]
+    for tile in range(tokens.shape[0] // TILE):
+        rows = pl.ds(tile * TILE, TILE)
+        back = lax.dot_general(grads[rows], w_down, NT, preferred_element_type=F32)
+        gate = pre[0, rows, :quarter].astype(F32)
+        up = pre[0, rows, quarter:].astype(F32)
+        sigma = 1.0 / (1.0 + jnp.exp(-gate))
+        act_silu = gate * sigma
+        sums = jnp.sum(back * act_silu * up, axis=1, keepdims=True)
+        mine = lanes_of((TILE, 8)) == slot
+
+        @pl.when(slot == 0)
+        def _():
+            gate_sum[rows] = jnp.zeros((TILE, 8), F32)
+
+        gate_sum[rows] += jnp.where(mine, sums, 0.0)
+        back = back * column(mix[rows], slot)
+        pre_grad[0, rows, :quarter] = (back * up * (sigma * (1.0 + gate * (1.0 - sigma)))).astype(BF)
+        pre_grad[0, rows, quarter:] = (back * act_silu).astype(BF)
+    down_grad[0] = lax.dot_general(act[0], grads[...], TN, preferred_element_type=F32).astype(BF)
+    for tile in range(depth // 256):
+        columns = slice(tile * 256, (tile + 1) * 256)
+        up_grad[0, columns] = lax.dot_general(
+            tokens[:, columns], pre_grad[0], TN, preferred_element_type=F32
+        ).astype(BF)
+
+
+def ffn_backward(grads, tokens, pre, act, down_own, down_peer, mix):
+    slots, rows, width = pre.shape
+    depth = tokens.shape[1]
+    per_slot = lambda *shape: pl.BlockSpec((1,) + shape, lambda e: (e, 0, 0))
+    whole = lambda *shape: pl.BlockSpec(shape, lambda e: (0, 0), pipeline_mode=pl.Buffered(1))
+    return pl.pallas_call(
+        ffn_back_kernel,
+        grid=(slots,),
+        out_shape=[
+            jax.ShapeDtypeStruct((slots, width // 2, depth), BF),
+            jax.ShapeDtypeStruct((slots, depth, width), BF),
+            jax.ShapeDtypeStruct((slots, rows, width), BF),
+            jax.ShapeDtypeStruct((rows, 8), F32),
+        ],
+        in_specs=[
+            whole(rows, depth),
+            whole(rows, depth),
+            per_slot(rows, width),
+            per_slot(rows, width // 2),
+            per_slot(width // 2, depth // 2),
+            per_slot(width // 2, depth // 2),
+            whole(rows, 8),
+        ],
+        out_specs=[
+            per_slot(width // 2, depth),
+            per_slot(depth, width),
+            per_slot(rows, width),
+            pl.BlockSpec((rows, 8), lambda e: (0, 0)),
+        ],
+        compiler_params=pltpu.CompilerParams(vmem_limit_bytes=58 << 20),
+        cost_estimate=pl.CostEstimate(
+            flops=4 * slots * rows * depth * width,
+            bytes_accessed=70 << 20,
+            transcendentals=slots * rows * width // 2,
+        ),
+    )(grads, tokens, pre, act, down_own, down_peer, mix)
+
+
+def ffn_input_kernel(pre_grad, up_own, up_peer, out):
+    slot = pl.program_id(0)
+    w_up = jnp.concatenate([up_own[0], up_peer[0]], axis=0)
+    for tile in range(out.shape[0] // TILE):
+        rows = pl.ds(tile * TILE, TILE)
+        part = lax.dot_general(pre_grad[0, rows], w_up, NT, preferred_element_type=F32)
+
+        @pl.when(slot == 0)
+        def _():
+            out[rows] = part
+
+        @pl.when(slot > 0)
+        def _():
+            out[rows] += part
+
+
+def ffn_input(pre_grad, up_own, up_peer, part, parts):
+    slots, rows, width = pre_grad.shape
+    half = up_own.shape[1]
+    depth = 2 * half
+    rows = rows // parts
+    return pl.pallas_call(
+        ffn_input_kernel,
+        grid=(slots,),
+        out_shape=jax.ShapeDtypeStruct((rows, depth), F32),
+        in_specs=[
+            pl.BlockSpec((1, rows, width), lambda e: (e, part, 0)),
+            pl.BlockSpec((1, half, width), lambda e: (e, 0, 0)),
+            pl.BlockSpec((1, half, width), lambda e: (e, 0, 0)),
+        ],
+        out_specs=pl.BlockSpec((rows, depth), lambda e: (0, 0)),
+        compiler_params=pltpu.CompilerParams(vmem_limit_bytes=40 << 20),
+        cost_estimate=pl.CostEstimate(
+            flops=2 * slots * rows * depth * width, bytes_accessed=20 << 20, transcendentals=0
+        ),
+    )(pre_grad, up_own, up_peer)
 
 
 def spread_tokens(own):
@@ -509,10 +926,10 @@
 
 
 def collect_tokens(parts):
-    recv = swap(jnp.stack([parts[1], parts[3]]).astype(BF), "col").astype(F32)
-    own = parts[0] + recv[0]
-    far = parts[2] + recv[1]
-    return own + swap(flip(far.astype(BF)), "row").astype(F32)
+    far = parts[2] + swap(parts[3].astype(BF), "col").astype(F32)
+    far = swap(flip(far.astype(BF)), "row").astype(F32)
+    own = parts[0] + swap(parts[1].astype(BF), "col").astype(F32)
+    return own + far
 
 
 def to_sequence(values, r, c):
@@ -561,13 +978,23 @@
     quarter = ff // 2
     slots = E + 1
 
-    x_pair = to_sequence(layer_input, r, c)
-    x_seq = jnp.concatenate([x_pair[0], x_pair[1]], axis=1).astype(F32)
-    w_qkv_full = jnp.concatenate([w_qkv, swap(w_qkv, "row")], axis=0)
-    w_out_full = jnp.concatenate([w_out, swap(w_out, "row")], axis=1)
-    gain_a = jnp.concatenate([gain_attn, swap(gain_attn, "row")])
-    gain_f = jnp.concatenate([gain_ffn, swap(gain_ffn, "row")])
-    w_r = jnp.concatenate([w_router, swap(w_router, "row")])
+    seg = lax.dynamic_slice_in_dim(segments, r, 1, 0)[0]
+    seg_row, seg_col = seg[None, :], seg[:, None]
+    tables = rope_tables(rows)
+    w_qkv = w_qkv.swapaxes(0, 1)
+    vectors = jnp.concatenate(
+        [gain_attn[None], gain_ffn[None], w_router.T.astype(F32), jnp.zeros((6 - E, half), F32)]
+    )
+    (
+        queries, keys_rot, values_low, context_low, normed_attn, x_own, hidden,
+        w_qkv_peer, w_out_peer, vec_peer, up_own, tokens, up_peer, down_peer,
+    ) = front(
+        layer_input, w_qkv, w_out, vectors, w_shared_up, w_expert_up, w_shared_down, w_expert_down,
+        tables, seg,
+    )
+
+    vectors = jnp.concatenate([vectors, vec_peer], axis=1)
+    gain_a, gain_f, w_r = vectors[0], vectors[1], vectors[2 : 2 + E].astype(BF).T
     t_pair = to_sequence(teacher, r, c)
     t_seq = jnp.concatenate([t_pair[0], t_pair[1]], axis=1)
     teacher_own = lax.dynamic_slice_in_dim(t_seq, c * part, part, 0).astype(F32)
@@ -575,61 +1002,30 @@
     valid_seq = jnp.where(r == c, valid_mask, valid_other).astype(F32)
     valid_own = lax.dynamic_slice_in_dim(valid_seq, c * part, part, 0)
     count = dp_sum(jnp.full((128,), jnp.sum(valid_own), F32))[0]
-    seg = lax.dynamic_slice_in_dim(segments, r, 1, 0)[0]
     route_blocks = routes.reshape(2, 2, part, 2)
     route_blocks = jnp.where(r == 0, route_blocks, route_blocks[::-1])
     route_blocks = jnp.where(c == 0, route_blocks, route_blocks[:, ::-1]).reshape(4 * part, 2)
     picks = (route_blocks[:, :, None] == jnp.arange(E, dtype=jnp.int32)[None, None, :]).astype(F32)
 
-    up_parts = [w_shared_up] + [w_expert_up[e] for e in range(E)]
-    down_parts = [w_shared_down] + [w_expert_down[e] for e in range(E)]
-    w_up, w_down = [], []
-    for e in range(slots):
-        keep = lax.dynamic_slice_in_dim(up_parts[e], r * quarter, quarter, 2)
-        send = lax.dynamic_slice_in_dim(up_parts[e], (1 - r) * quarter, quarter, 2)
-        w_up.append(
-            jnp.concatenate([keep, fetch_row(send, 0)], axis=0).reshape(D, 2 * quarter)
-        )
-        keep = lax.dynamic_slice_in_dim(down_parts[e], r * quarter, quarter, 0)
-        send = lax.dynamic_slice_in_dim(down_parts[e], (1 - r) * quarter, quarter, 0)
-        w_down.append(jnp.concatenate([keep, fetch_row(send, 0)], axis=1))
-    w_down = jnp.concatenate(w_down, axis=0)
-
-    rstd_seq, normed = norm_forward(x_seq, gain_a)
-    normed_attn = normed.astype(BF)
-    qkv_pre = jnp.einsum("td,dke->kte", normed_attn, w_qkv_full, preferred_element_type=F32)
-    tables = rope_tables(rows)
-    seg_row, seg_col = seg[None, :], seg[:, None]
-    queries, keys_rot, values_low, context_low = attend_forward(qkv_pre, tables, seg_row, seg_col)
-    attention = jnp.dot(context_low, w_out_full, preferred_element_type=F32)
-    att_halves = attention.reshape(2, part, D)
-    att_keep = lax.dynamic_index_in_dim(att_halves, c, 0, keepdims=False)
-    att_send = lax.dynamic_index_in_dim(att_halves, 1 - c, 0, keepdims=False)
-    x_own = lax.dynamic_slice_in_dim(x_seq, c * part, part, 0)
-    rstd_attn = lax.dynamic_slice_in_dim(rstd_seq, c * part, part, 0)
-    hidden = x_own + att_keep + swap(att_send.astype(BF), "col").astype(F32)
-
-    rstd_ffn, normed = norm_forward(hidden, gain_f)
-    normed_low = normed.astype(BF)
-    tokens = spread_tokens(normed_low).reshape(4 * part, D)
+    down_own = jnp.concatenate([w_shared_down[None], w_expert_down])
+    down_own = lax.dynamic_slice_in_dim(down_own, r * quarter, quarter, 1)
+
+    x_own = jnp.concatenate([x_own[0], x_own[1]], axis=1).astype(F32)
+    rstd_attn = lax.rsqrt(jnp.mean(x_own * x_own, axis=1) + 1e-06)
+
+    rstd_ffn = lax.rsqrt(jnp.mean(hidden * hidden, axis=1) + 1e-06)
+    normed_low = tokens[0]
+    tokens = tokens.reshape(4 * part, D)
     logits = jnp.dot(tokens, w_r, preferred_element_type=F32)
     chosen = jnp.sum(picks * logits[:, None, :], axis=2)
     chosen = chosen - jnp.max(chosen, axis=1, keepdims=True)
     gates = jnp.exp(chosen)
     gates = gates / jnp.sum(gates, axis=1, keepdims=True)
     mixing = jnp.sum(picks * gates[:, :, None], axis=1)
-    mix_all = jnp.concatenate([jnp.ones((4 * part, 1), F32), mixing], axis=1).T
-    pre = [
-        jnp.dot(tokens, w_up[e], preferred_element_type=F32).astype(BF)
-        for e in range(slots)
-    ]
-    acts = []
-    for e in range(slots):
-        gate_pre, up_pre = pre[e][:, :quarter].astype(F32), pre[e][:, quarter:].astype(F32)
-        act = gate_pre * jax.nn.sigmoid(gate_pre) * up_pre
-        acts.append((act * mix_all[e][:, None]).astype(BF))
-    act_all = jnp.concatenate(acts, axis=1)
-    branch = jnp.dot(act_all, w_down, preferred_element_type=F32)
+    mix = jnp.concatenate(
+        [jnp.ones((4 * part, 1), F32), mixing, jnp.zeros((4 * part, 7 - E), F32)], axis=1
+    )
+    pre, act, branch = ffn_forward(tokens, up_own, up_peer, down_own, down_peer, mix)
     output = hidden + collect_tokens(branch.reshape(4, part, D))
 
     error = output - teacher_own
@@ -638,33 +1034,13 @@
     grad_out = total_tokens / count * valid_own[:, None] * error
 
     grads = spread_tokens(grad_out.astype(BF)).reshape(4 * part, D)
-    down_grad = jnp.dot(act_all.T, grads, preferred_element_type=F32).astype(BF)
-    act_back = jnp.dot(
-        grads, w_down.T, preferred_element_type=F32
-    ).astype(BF)
-    pre_grads = []
-    gate_sums = []
-    for e in range(slots):
-        gate_pre, up_pre = pre[e][:, :quarter].astype(F32), pre[e][:, quarter:].astype(F32)
-        back = act_back[:, e * quarter : (e + 1) * quarter].astype(F32)
-        act_silu, slope = silu_parts(gate_pre)
-        if e:
-            gate_sums.append(jnp.sum(back * act_silu * up_pre, axis=1))
-        back = back * mix_all[e][:, None]
-        pre_grads.append(
-            jnp.concatenate([back * up_pre * slope, back * act_silu], axis=1).astype(BF)
-        )
-    up_grads = [
-        jnp.dot(tokens.T, pre_grads[e], preferred_element_type=F32).astype(BF)
-        for e in range(slots)
-    ]
-    input_part = jnp.zeros((4 * part, D), F32)
-    for e in range(slots):
-        input_part = input_part + jnp.dot(
-            pre_grads[e], w_up[e].T, preferred_element_type=F32
-        )
-    normed_ffn_grad = collect_tokens(input_part.reshape(4, part, D))
-    gate_parts = jnp.stack(gate_sums, axis=0).reshape(E, 4, part)
+    down_grad, up_grad, pre_grad, gate_sums = ffn_backward(
+        grads, tokens, pre, act, down_own, down_peer, mix
+    )
+    far_part = ffn_input(pre_grad, up_own, up_peer, 1, 2).reshape(2, part, D)
+    near_part = ffn_input(pre_grad, up_own, up_peer, 0, 2).reshape(2, part, D)
+    normed_ffn_grad = collect_tokens([near_part[0], near_part[1], far_part[0], far_part[1]])
+    gate_parts = gate_sums[:, 1 : E + 1].T.reshape(E, 4, part)
     recv = swap(jnp.stack([gate_parts[:, 1], gate_parts[:, 3]]), "col")
     gate_grad = gate_parts[:, 0] + recv[0] + swap(gate_parts[:, 2] + recv[1], "row")
     mix_own = mixing[:part].T
@@ -678,6 +1054,9 @@
     low_own = hidden_grad.astype(BF)
     low_seq = order_pair(c == 0, low_own, swap(low_own, "col"), 0)
     w_out_grad = jnp.dot(context_low.T, low_seq, preferred_element_type=F32).astype(BF)
+    w_out_full = jnp.concatenate([w_out, w_out_peer], axis=1)
+    w_qkv_full = jnp.concatenate([w_qkv, w_qkv_peer], axis=1)
+    normed_attn = jnp.concatenate([normed_attn[0], normed_attn[1]], axis=1)
     context_grad = jnp.dot(low_seq, w_out_full.T, preferred_element_type=F32)
     context_grad = context_grad.astype(BF)
     qkv_grad = jnp.concatenate(
@@ -692,7 +1071,7 @@
     w_qkv_grad = jnp.einsum(
         "td,kte->dke", normed_attn, qkv_grad, preferred_element_type=F32
     ).astype(BF)
-    back_part = jnp.einsum("kte,dke->td", qkv_grad, w_qkv_full, preferred_element_type=F32)
+    back_part = jnp.einsum("kte,kde->td", qkv_grad, w_qkv_full, preferred_element_type=F32)
     back_halves = back_part.reshape(2, part, D)
     back_keep = lax.dynamic_index_in_dim(back_halves, c, 0, keepdims=False)
     back_send = lax.dynamic_index_in_dim(back_halves, 1 - c, 0, keepdims=False)
@@ -711,7 +1090,7 @@
         axis=3,
     ).transpose(0, 1, 3, 2, 4)
     up_pair, down_pair, attn_piece = dp_reduce(
-        [grad.reshape(2, deep, 2, owner_d, 2 * quarter) for grad in up_grads],
+        up_grad.reshape(slots, 2, deep, 2, owner_d, 2 * quarter),
         down_grad.reshape(slots, deep, 2, owner_f, D),
         grad_pair.reshape(2, deep, 2, 4 * owner_d, half),
     )

time: 893 us -> 835 us (0.935)
  Pallas kernels: 350 us -> 601 us
  matrix products: 136 us -> 16.8 us
  waiting for transfers between devices: 130 us -> 64.6 us
  local copies, waits for them, and re-layouts: 91.3 us -> 37.1 us
  other arithmetic: 100 us -> 64.2 us
  starting transfers between devices: 69.6 us -> 34.1 us
    pallas_call x1 -> x5, Pallas kernels: 16.3 us -> 253 us  [the longest x1 121 us: front(): pl.pallas_call(functools.partial(front_kernel, n), out_shape=[shape((rows...]
    dot_general x21 -> x1, matrix products: 126 us -> 3.67 us  [local(): jnp.einsum('kte,kde->td', qkv_grad, w_qkv_full, preferred_element_type=F32)]
    ppermute x37 -> x20, waiting for transfers between devices: 93.8 us -> 49.3 us  [swap(): return lax.ppermute(values, axis, [(0, 1), (1, 0)])]
    ppermute x37 -> x20, starting transfers between devices: 49.2 us -> 18 us  [swap(): return lax.ppermute(values, axis, [(0, 1), (1, 0)])]
    ppermute x10 -> x0, waiting for transfers between devices: 28.7 us -> none  [fetch_row(): second = lax.ppermute(first, 'dp', dp_pairs(0))]
    dynamic_slice x18 -> x0, local copies, waits for them, and re-layouts: 28.6 us -> none  [the longest x10 15.2 us: half_by_x(): lax.dynamic_slice_in_dim(values, lax.axis_index('dp') % 2 * size, size, a...]
    another operation x6 -> x1, other arithmetic: 21 us -> 3.09 us
    unnamed x307 -> x100, local copies, waits for them, and re-layouts: 30.3 us -> 12.8 us
  transfers between devices with their start and end apart: 59 -> 30, of which waited for: 20 -> 11; matrix products, arithmetic and copies ran while one was open for 32% -> 10% of each run, Pallas kernels for 38% -> 71%
where the time goes in v3:
time: 835 us; the launch traced here: 822 us
  Pallas kernels  601 us (72%)
  waiting for transfers between devices  64.6 us (8%)
  other arithmetic  64.2 us (8%)
  local copies, waits for them, and re-layouts  37.1 us (4%)
  starting transfers between devices  34.1 us (4%)
  matrix products  16.8 us (2%)
    pallas_call x1, Pallas kernels, dp_gather(): pl.pallas_call(functools.partial(gather_kernel, n, plan), out_shape=[jax....  168 us
    pallas_call x1, Pallas kernels, dp_reduce(): pl.pallas_call(functools.partial(reduce_kernel, n, slots), out_shape=[jax...  161 us
    pallas_call x1, Pallas kernels, front(): pl.pallas_call(functools.partial(front_kernel, n), out_shape=[shape((rows...  121 us
    pallas_call x1, Pallas kernels, ffn_backward(): pl.pallas_call(ffn_back_kernel, grid=(slots,), out_shape=[jax.ShapeDtypeS...  56.9 us
    ppermute x20, waiting for transfers between devices, swap(): return lax.ppermute(values, axis, [(0, 1), (1, 0)])  49.3 us
    pallas_call x1, Pallas kernels, ffn_forward(): pl.pallas_call(ffn_kernel, grid=(slots,), out_shape=[jax.ShapeDtypeStruct...  42.5 us
    pallas_call x2, Pallas kernels, ffn_input(): pl.pallas_call(ffn_input_kernel, grid=(slots,), out_shape=jax.ShapeDtypeS...  32.5 us
    pallas_call x3, Pallas kernels, attend_backward(): pl.pallas_call(attend_back_kernel, grid=(pairs,), out_shape=jax.ShapeDtyp...  19 us
  transfers between devices with their start and end apart: 30, of which 11 were waited for; matrix products, arithmetic and copies ran while one was open for 10% of the time, Pallas kernels for 71%

profile of v3, /device:TPU:27, one launch (start us, length us, event | category | flops | bytes accessed | tf_op | source)
XLA Modules:
  0.0 821.9 jit_solution(347819441572472769)
XLA Ops:
  0.7 3.2 collective-permute-start.11
  8.7 121.0 %shard_map.229 = (bf16[1024,384]{1,0:T(8,128)(2,1)S(1)}, bf16[1024,384]{1,0:T(8,128)(2,1)S(1)}, bf16[1024,384]{1,0:T(8,128)(2,1)S(1)}, bf16[1024,384]{1,0:T(8,12...) custom-call(bf16[1024,384]{1,0:T(8,128)(2,1)} %x_in.1, ...), custom_call_target="tpu_custom_call" | custom-call | tf_op jit(solution)/shard_map/pallas_call | solution.py:330
  129.8 4.0 fusion.37
  135.4 3.0 fusion.down_own
  138.4 42.5 %shard_map.230 = (bf16[5,2048,1024]{2,1,0:T(8,128)(2,1)}, bf16[5,2048,512]{2,1,0:T(8,128)(2,1)}, f32[2048,768]{1,0:T(8,128)}) custom-call(bf16[2048,768]{1,0:T(8,128)(2,1)} %bitcast.134, bf16[5,384,1024]{2,1,0:T(8,128)(2,1)} %get-tuple-element.43.up_own, bf16[5,384,1024]{2,1,0:T(8,128)(2,1)} %get-tuple-element.44.up_peer, ...), custom_call_target="tpu_custom_call" | custom-call | flops 24159191040 | bytes 41943040 | tf_op jit(solution)/shard_map/pallas_call | solution.py:786
  180.9 3.1 convert.18
  194.3 16.6 %collective-permute-done.2 = bf16[512,768]{1,0:T(8,128)(2,1)S(1)} collective-permute-done((bf16[512,768]{1,0:T(8,128)(2,1)S(1)}, bf16[512,768]{1,0:T(8,128)(2,1)S(1)}, u32[]{:S(2)}, u32[]{:S(2)}) %collective-permute-start.2) | collective-permute-done | bytes 786464 | tf_op jit(solution)/shard_map/ppermute | solution.py:445
  210.9 3.2 multiply_reduce_fusion
  215.6 3.4 collective-permute-start.6
  220.5 3.4 collective-permute-start.7
  225.7 3.2 collective-permute-done.8
  231.3 5.4 collective-permute-start.10
  240.8 17.4 %collective-permute-done.14 = bf16[512,768]{1,0:T(8,128)(2,1)} collective-permute-done((bf16[512,768]{1,0:T(8,128)(2,1)}, bf16[512,768]{1,0:T(8,128)(2,1)}, u32[]{:S(2)}, u32[]{:S(2)}) %collective-permute-start.14) | collective-permute-done | bytes 786464 | tf_op jit(solution)/shard_map/ppermute | solution.py:445
  262.7 3.3 pad_maximum_fusion
  266.0 56.9 %shard_map.231 = (bf16[5,512,768]{2,1,0:T(8,128)(2,1)}, bf16[5,768,1024]{2,1,0:T(8,128)(2,1)}, bf16[5,2048,1024]{2,1,0:T(8,128)(2,1)}, f32[2048,8]{1,0:T(8,128)}) custom-call(bf16[2048,768]{1,0:T(8,128)(2,1)} %bitcast.145, bf16[2048,768]{1,0:T(8,128)(2,1)} %bitcast.135, bf16[5,2048,1024]{2,1,0:T(8,128)(2,1)} %get-tuple-element.51.pre, ...), custom_call_target="tpu_custom_call" | custom-call | flops 32212254720 | bytes 73400320 | tf_op jit(solution)/shard_map/pallas_call | solution.py:850
  329.8 16.2 %shard_map.233 = f32[1024,768]{1,0:T(8,128)S(1)} custom-call(bf16[5,2048,1024]{2,1,0:T(8,128)(2,1)} %get-tuple-element.53.pre_grad, bf16[5,384,1024]{2,1,0:T(8,128)(2,1)S(1)} %copy-done.2, bf16[5,384,1024]{2,1,0:T(8,128)(2,1)S(1)} %copy-done.3), custom_call_target="tpu_custom_call" | custom-call | flops 8053063680 | bytes 20971520 | tf_op jit(solution)/shard_map/pallas_call | solution.py:904
  347.3 16.2 %shard_map.232 = f32[1024,768]{1,0:T(8,128)S(1)} custom-call(bf16[5,2048,1024]{2,1,0:T(8,128)(2,1)} %get-tuple-element.53.pre_grad, bf16[5,384,1024]{2,1,0:T(8,128)(2,1)S(1)} %copy-done.2, bf16[5,384,1024]{2,1,0:T(8,128)(2,1)S(1)} %copy-done.3), custom_call_target="tpu_custom_call" | custom-call | flops 8053063680 | bytes 20971520 | tf_op jit(solution)/shard_map/pallas_call | solution.py:904
  369.4 3.2 maximum_select_fusion
  376.2 9.7 %collective-permute-done.20 = f32[4,512]{1,0:T(4,128)S(1)} collective-permute-done((f32[4,512]{1,0:T(4,128)}, f32[4,512]{1,0:T(4,128)S(1)}, u32[]{:S(2)}, u32[]{:S(2)}) %collective-permute-start.20) | collective-permute-done | bytes 8224 | tf_op jit(solution)/shard_map/ppermute | solution.py:445
  385.9 2.9 multiply_reduce_fusion.2
  392.6 10.3 %collective-permute-done.4 = f32[1024,384]{1,0:T(8,128)} collective-permute-done((f32[1024,384]{1,0:T(8,128)}, f32[1024,384]{1,0:T(8,128)}, u32[]{:S(2)}, u32[]{:S(2)}) %collective-permute-start.4) | collective-permute-done | bytes 1572896 | tf_op jit(solution)/shard_map/ppermute | solution.py:950
  407.6 6.3 shard_map.236
  413.9 6.5 shard_map.235
  420.4 6.3 shard_map.234
  430.7 3.7 fusion.1
  439.5 160.9 %shard_map.237 = (bf16[2,5,48,1024]{3,2,1,0:T(8,128)(2,1)S(1)}, bf16[2,5,64,384]{3,2,1,0:T(8,128)(2,1)S(1)}, bf16[192,384]{1,0:T(8,128)(2,1)S(1)}) custom-call(bf16[5,2,4,2,48,1024]{5,4,3,2,1,0:T(8,128)(2,1)} %bitcast.136, bf16[5,4,2,64,768]{4,3,2,1,0:T(8,128)(2,1)} %bitcast.143, bf16[2,4,2,192,384]{4,3,2,1,0:T(8,128)(2,1)S(1)} %bitcast.131), custom_call_target="tpu_custom_call" | custom-call | tf_op jit(solution)/shard_map/pallas_call | solution.py:614
  602.7 3.4 broadcast_select_fusion
  622.0 168.4 %shard_map.238 = (bf16[4,384,2,1024]{3,2,1,0:T(2,128)(2,1)}, bf16[384,2,1024]{2,1,0:T(2,128)(2,1)}, bf16[4,2,512,384]{3,2,1,0:T(8,128)(2,1)}, bf16[2,512,384]{2,1,0:T(8,128)(2,1)}, bf16[8,4,48,384]{3,2,1,0:T(8,128)(2,1)}) custom-call(bf16[4,48,2,1024]{3,2,1,0:T(2,128)(2,1)} %slice.258.refs_0_, bf16[48,2,1024]{2,1,0:T(2,128)(2,1)} %slice_bitcast_fusion.6.refs_1_, ...), custom_call_target="tpu_custom_call" | custom-call | tf_op jit(solution)/shard_map/pallas_call | solution.py:734
  790.6 5.1 bitcast_convert_fusion
  798.4 4.0 collective-permute-start.27
  806.4 2.7 convert_element_type.122
  809.2 6.1 convert_element_type.125
  (267 shorter events, 96.7 us)
Async XLA Ops:
  0.7 184.7 %collective-permute-start.11 = (bf16[1024,384]{1,0:T(8,128)(2,1)}, bf16[1024,384]{1,0:T(8,128)(2,1)S(1)}, u32[]{:S(2)}, u32[]{:S(2)}) collective-permute-start(bf16[1024,384]{1,0:T(8,128)(2,1)} %param.15), channel_id=1, source_target_pairs={{1,3},{2,0},{5,7},{6,4},{9,11},{10,8},{13,15},{14,12},{17,19},{18,... | collective-permute-start | bytes 2359304 | tf_op jit(solution)/shard_map/ppermute | solution.py:936
  7.9 121.8 %copy-start.4 = (f32[1024,128]{1,0:T(8,128)}, f32[1024,128]{1,0:T(8,128)S(1)}, u32[]{:S(2)}) copy-start(f32[1024,128]{1,0:T(8,128)S(1)} %copy.80.sine) | copy-start | bytes 1572868
  8.1 121.5 %copy-start.6 = (s32[1024,1]{1,0:T(8,128)}, s32[1024,1]{1,0:T(8,128)S(1)}, u32[]{:S(2)}) copy-start(s32[1024,1]{1,0:T(8,128)S(1)} %copy.81.seg_col) | copy-start | bytes 12292
  185.2 5.0 collective-permute-start.1
  186.7 5.7 collective-permute-start.12
  188.0 4.4 collective-permute-start.5
  190.3 4.0 collective-permute-start
  192.2 18.7 %collective-permute-start.2 = (bf16[512,768]{1,0:T(8,128)(2,1)S(1)}, bf16[512,768]{1,0:T(8,128)(2,1)S(1)}, u32[]{:S(2)}, u32[]{:S(2)}) collective-permute-start(bf16[512,768]{1,0:T(8,128)(2,1)S(1)} %pad_maximum_fusion.6), channel_id=1, source_target_pairs={{0,2},{2,0},{1,3},{3,1},{4,6},{6,4},{5,7},{7,5},{8,10},{10,8},{9,1... | collective-permute-start | bytes 2359304 | tf_op jit(solution)/shard_map/ppermute | solution.py:445
  215.6 4.3 collective-permute-start.6
  220.5 4.4 collective-permute-start.7
  225.5 3.4 collective-permute-start.8
  228.9 2.4 collective-permute-start.9
  231.3 6.2 collective-permute-start.10
  239.0 19.1 %collective-permute-start.14 = (bf16[512,768]{1,0:T(8,128)(2,1)}, bf16[512,768]{1,0:T(8,128)(2,1)}, u32[]{:S(2)}, u32[]{:S(2)}) collective-permute-start(bf16[512,768]{1,0:T(8,128)(2,1)} %pad_maximum_fusion.7), channel_id=1, source_target_pairs={{0,2},{2,0},{1,3},{3,1},{4,6},{6,4},{5,7},{7,5},{8,10},{10,8},{9,1... | collective-permute-start | bytes 2359304 | tf_op jit(solution)/shard_map/ppermute | solution.py:445
  240.1 22.5 %collective-permute-start.13 = (bf16[512,768]{1,0:T(8,128)(2,1)S(1)}, bf16[512,768]{1,0:T(8,128)(2,1)S(1)}, u32[]{:S(2)}, u32[]{:S(2)}) collective-permute-start(bf16[512,768]{1,0:T(8,128)(2,1)S(1)} %multiply_convert_fusion), channel_id=1, source_target_pairs={{0,1},{1,0},{2,3},{3,2},{4,5},{5,4},{6,7},{7,6},{8,9},{9,8},{10,11... | collective-permute-start | bytes 2359304 | tf_op jit(solution)/shard_map/ppermute | solution.py:445
  258.1 4.5 collective-permute-start.15
  262.5 106.9 %collective-permute-start.3 = (f32[512,384]{1,0:T(8,128)}, f32[512,384]{1,0:T(8,128)}, u32[]{:S(2)}, u32[]{:S(2)}) collective-permute-start(f32[512,384]{1,0:T(8,128)} %get-tuple-element.93), channel_id=1, source_target_pairs={{0,1},{1,0},{2,3},{3,2},{4,5},{5,4},{6,7},{7,6},{8,9},{9,8},{10,11... | collective-permute-start | bytes 2359304 | tf_op jit(solution)/shard_map/ppermute | solution.py:445
  346.1 18.9 %collective-permute-start.17 = (bf16[512,768]{1,0:T(8,128)(2,1)S(1)}, bf16[512,768]{1,0:T(8,128)(2,1)S(1)}, u32[]{:S(2)}, u32[]{:S(2)}) collective-permute-start(bf16[512,768]{1,0:T(8,128)(2,1)S(1)} %slice.318), channel_id=1, source_target_pairs={{0,1},{1,0},{2,3},{3,2},{4,5},{5,4},{6,7},{7,6},{8,9},{9,8},{10,11... | collective-permute-start | bytes 2359304 | tf_op jit(solution)/shard_map/ppermute | solution.py:445
  347.3 20.0 %collective-permute-start.19 = (f32[2,4,512]{2,1,0:T(4,128)}, f32[2,4,512]{2,1,0:T(4,128)S(1)}, u32[]{:S(2)}, u32[]{:S(2)}) collective-permute-start(f32[2,4,512]{2,1,0:T(4,128)} %pad_maximum_fusion.14), channel_id=1, source_target_pairs={{0,1},{1,0},{2,3},{3,2},{4,5},{5,4},{6,7},{7,6},{8,9},{9,8},{10,11... | collective-permute-start | bytes 49160 | tf_op jit(solution)/shard_map/ppermute | solution.py:445
  364.5 21.4 %collective-permute-start.16 = (bf16[512,768]{1,0:T(8,128)(2,1)}, bf16[512,768]{1,0:T(8,128)(2,1)}, u32[]{:S(2)}, u32[]{:S(2)}) collective-permute-start(bf16[512,768]{1,0:T(8,128)(2,1)} %slice.319), channel_id=1, source_target_pairs={{0,1},{1,0},{2,3},{3,2},{4,5},{5,4},{6,7},{7,6},{8,9},{9,8},{10,11... | collective-permute-start | bytes 2359304 | tf_op jit(solution)/shard_map/ppermute | solution.py:445
  366.2 19.7 %collective-permute-start.18 = (bf16[512,768]{1,0:T(8,128)(2,1)}, bf16[512,768]{1,0:T(8,128)(2,1)}, u32[]{:S(2)}, u32[]{:S(2)}) collective-permute-start(bf16[512,768]{1,0:T(8,128)(2,1)} %pad_maximum_fusion.8), channel_id=1, source_target_pairs={{0,2},{2,0},{1,3},{3,1},{4,6},{6,4},{5,7},{7,5},{8,10},{10,8},{9,1... | collective-permute-start | bytes 2359304 | tf_op jit(solution)/shard_map/ppermute | solution.py:445
  367.9 17.9 %collective-permute-start.20 = (f32[4,512]{1,0:T(4,128)}, f32[4,512]{1,0:T(4,128)S(1)}, u32[]{:S(2)}, u32[]{:S(2)}) collective-permute-start(f32[4,512]{1,0:T(4,128)} %fusion.30), channel_id=1, source_target_pairs={{0,2},{2,0},{1,3},{3,1},{4,6},{6,4},{5,7},{7,5},{8,10},{10,8},{9,1... | collective-permute-start | bytes 24584 | tf_op jit(solution)/shard_map/ppermute | solution.py:445
  372.5 30.3 %collective-permute-start.4 = (f32[1024,384]{1,0:T(8,128)}, f32[1024,384]{1,0:T(8,128)}, u32[]{:S(2)}, u32[]{:S(2)}) collective-permute-start(f32[1024,384]{1,0:T(8,128)} %maximum_select_fusion), channel_id=1, source_target_pairs={{1,2},{2,1},{5,6},{6,5},{9,10},{10,9},{13,14},{14,13},{17,18},{18,... | collective-permute-start | bytes 4718600 | tf_op jit(solution)/shard_map/ppermute | solution.py:950
  390.5 15.1 %collective-permute-start.21 = (bf16[512,768]{1,0:T(8,128)(2,1)S(1)}, bf16[512,768]{1,0:T(8,128)(2,1)S(1)}, u32[]{:S(2)}, u32[]{:S(2)}) collective-permute-start(bf16[512,768]{1,0:T(8,128)(2,1)S(1)} %get-tuple-element.80), channel_id=1, source_target_pairs={{0,1},{1,0},{2,3},{3,2},{4,5},{5,4},{6,7},{7,6},{8,9},{9,8},{10,11... | collective-permute-start | bytes 2359304 | tf_op jit(solution)/shard_map/ppermute | solution.py:445
  435.3 170.7 %collective-permute-start.22 = (bf16[512,768]{1,0:T(8,128)(2,1)}, bf16[512,768]{1,0:T(8,128)(2,1)}, u32[]{:S(2)}, u32[]{:S(2)}) collective-permute-start(bf16[512,768]{1,0:T(8,128)(2,1)} %fusion.16), channel_id=1, source_target_pairs={{0,1},{1,0},{2,3},{3,2},{4,5},{5,4},{6,7},{7,6},{8,9},{9,8},{10,11... | collective-permute-start | bytes 2359304 | tf_op jit(solution)/shard_map/ppermute | solution.py:445
  610.6 2.6 collective-permute-start.28
  612.8 5.6 collective-permute-start.23
  616.5 201.4 %collective-permute-start.29 = (f32[1024,384]{1,0:T(8,128)S(1)}, f32[1024,384]{1,0:T(8,128)}, u32[]{:S(2)}, u32[]{:S(2)}) collective-permute-start(f32[1024,384]{1,0:T(8,128)S(1)} %maximum_select_fusion.2), channel_id=1, source_target_pairs={{1,2},{2,1},{5,6},{6,5},{9,10},{10,9},{13,14},{14,13},{17,18},{18,... | collective-permute-start | bytes 4718600 | tf_op jit(solution)/shard_map/ppermute | solution.py:950
  619.1 171.4 %collective-permute-start.24 = (f32[4609]{0:T(1024)S(1)}, f32[4609]{0:T(1024)S(1)}, u32[]{:S(2)}, u32[]{:S(2)}) collective-permute-start(f32[4609]{0:T(1024)S(1)} %fusion.56), channel_id=1, source_target_pairs={{0,8},{4,12},{8,0},{12,4},{16,24},{20,28},{24,16},{28,20},{1,9},{5... | collective-permute-start | bytes 55316 | tf_op jit(solution)/shard_map/ppermute | solution.py:460
  790.5 5.2 collective-permute-start.25
  795.7 2.7 collective-permute-start.26
  798.4 16.9 %collective-permute-start.27 = (f32[4609]{0:T(1024)S(1)}, f32[4609]{0:T(1024)S(1)}, u32[]{:S(2)}, u32[]{:S(2)}) collective-permute-start(f32[4609]{0:T(1024)S(1)} %add.141), channel_id=1, source_target_pairs={{0,1},{1,0},{2,3},{3,2},{4,5},{5,4},{6,7},{7,6},{8,9},{9,8},{10,11... | collective-permute-start | bytes 55316 | tf_op jit(solution)/shard_map/ppermute | solution.py:445
  (46 other events, 331.1 us)

commit v4 on v3

--- a/solution.py
+++ b/solution.py
@@ -56,12 +56,15 @@
     return weight * (1.0 / jnp.sum(weight, axis=0, keepdims=True))
 
 
+LAG = 3
+
+
 def front_kernel(
-    n, x_in, w_qkv, w_out, vectors, shared_up, expert_up, shared_down, expert_down,
+    n, x_in, teacher, w_qkv, w_out, vectors, shared_up, expert_up, shared_down, expert_down,
     cosine, sine, seg_row, seg_col,
     queries, keys, values, context, normed, x_own, hidden, w_qkv_peer, w_out_peer, vec_peer, up_own,
-    tokens, up_peer, down_peer,
-    x_pair, qkv_own, out_own, up_raw, part_raw, up_part, pre, att_send, att_recv, low, low_flip,
+    tokens, up_peer, down_peer, teacher_pair,
+    x_pair, teacher_in, qkv_own, out_own, up_raw, part_raw, up_part, pre, att_send, att_recv, low, low_flip,
     own_sem, x_send, x_recv, w_send, w_recv, t_send, t_recv,
 ):
     me = lax.axis_index("dp")
@@ -142,16 +145,18 @@
     def pump():
         at = progress[0]
         progress[0] += 1
-        if 2 <= at - 1 < count:
-            pass_far(at - 1)
         if 2 <= at < count:
             pass_on(at)
+        if 2 <= at - LAG < count:
+            pass_far(at - LAG)
 
     diagonal = row == col
     over_row = remote(x_in, x_pair.at[1], x_send.at[0], x_recv.at[0], row_peer)
     across_own = remote(x_in, x_pair.at[0], x_send.at[1], x_recv.at[1], core)
     across_peer = remote(x_pair.at[1], x_pair.at[1], x_send.at[2], x_recv.at[2], core)
     own_x = pltpu.make_async_copy(x_in, x_pair.at[0], own_sem.at[0])
+
+    fetch(0)
 
     @pl.when(diagonal)
     def _():
@@ -180,12 +185,25 @@
 
     give_vectors = remote(vectors, vec_peer, x_send.at[3], x_recv.at[3], row_peer)
     give_vectors.start()
-    fetch(0)
     fetch(1)
     own_qkv = pltpu.make_async_copy(w_qkv, qkv_own, own_sem.at[1])
     own_qkv.start()
     own_out = pltpu.make_async_copy(w_out, out_own, own_sem.at[2])
     own_out.start()
+
+    goal_row = remote(teacher, teacher_in, x_send.at[4], x_recv.at[4], row_peer)
+    goal_own = remote(
+        teacher.at[split(1 - col, part)], teacher_pair.at[0], x_send.at[5], x_recv.at[5], core
+    )
+    goal_peer = remote(
+        teacher_in.at[split(1 - col, part)], teacher_pair.at[1], x_send.at[6], x_recv.at[6], core
+    )
+    keep_own = pltpu.make_async_copy(
+        teacher.at[split(col, part)], teacher_pair.at[0], own_sem.at[4 + 2 * slots]
+    )
+    keep_peer = pltpu.make_async_copy(
+        teacher_in.at[split(col, part)], teacher_pair.at[1], own_sem.at[5 + 2 * slots]
+    )
 
     for slot in range(slots):
         piece = up_slot(slot).at[:, :, keep_lanes]
@@ -210,6 +228,16 @@
 
     for item in range(2, count):
         fetch(item)
+
+    @pl.when(diagonal)
+    def _():
+        goal_own.start()
+        keep_own.start()
+
+    @pl.when(jnp.logical_not(diagonal))
+    def _():
+        goal_row.start()
+
     pass_on(0)
     pass_on(1)
     split_own(0)
@@ -297,8 +325,15 @@
     far.start()
     near = remote(low, tokens.at[1], t_send.at[2], t_recv.at[2], core)
     near.start()
-    while progress[0] <= count:
+    while progress[0] < count + LAG:
         pump()
+
+    @pl.when(diagonal)
+    def _():
+        goal_row.wait_recv()
+        goal_peer.start()
+        keep_peer.start()
+
     far.wait_recv()
     far_near = remote(tokens.at[2], tokens.at[3], t_send.at[3], t_recv.at[3], core)
     far_near.start()
@@ -314,9 +349,19 @@
     def _():
         across_own.wait_send()
         across_peer.wait_send()
-
-
-def front(x_in, w_qkv, w_out, vectors, shared_up, expert_up, shared_down, expert_down, tables, seg):
+        goal_own.wait_send()
+        goal_peer.wait_send()
+        keep_own.wait()
+        keep_peer.wait()
+
+    @pl.when(jnp.logical_not(diagonal))
+    def _():
+        goal_row.wait_send()
+        goal_own.wait_recv()
+        goal_peer.wait_recv()
+
+
+def front(x_in, teacher, w_qkv, w_out, vectors, shared_up, expert_up, shared_down, expert_down, tables, seg):
     n = lax.axis_size("dp")
     rows, half = x_in.shape
     quarter = shared_up.shape[2] // 2
@@ -341,11 +386,13 @@
             shape((4, rows // 2, 2 * half), BF),
             shape((slots, half, 2 * quarter), BF),
             shape((slots, quarter, half), BF),
-        ],
-        in_specs=[any_spec] * 3 + [vmem_spec] + [any_spec] * 4 + [vmem_spec] * 4,
-        out_specs=[vmem_spec] * 11 + [any_spec] * 3,
+            shape((2, rows // 2, half), BF),
+        ],
+        in_specs=[any_spec] * 4 + [vmem_spec] + [any_spec] * 4 + [vmem_spec] * 4,
+        out_specs=[vmem_spec] * 11 + [any_spec] * 4,
         scratch_shapes=[
             pltpu.VMEM((2, rows, half), BF),
+            pltpu.VMEM((rows, half), BF),
             pltpu.VMEM(w_qkv.shape, BF),
             pltpu.VMEM(w_out.shape, BF),
             pltpu.VMEM((slots, half, 2, quarter), BF),
@@ -356,9 +403,9 @@
             pltpu.VMEM((rows // 2, 2 * half), BF),
             pltpu.VMEM((rows // 2, 2 * half), BF),
             pltpu.VMEM((rows // 2, 2 * half), BF),
-            sems((4 + 2 * slots,)),
-            sems((4,)),
-            sems((4,)),
+            sems((6 + 2 * slots,)),
+            sems((7,)),
+            sems((7,)),
             sems((count, 4)),
             sems((count, 4)),
             sems((4,)),
@@ -368,7 +415,7 @@
             collective_id=2, has_side_effects=True, vmem_limit_bytes=48 << 20
         ),
     )(
-        x_in, w_qkv, w_out, vectors, shared_up, expert_up, shared_down, expert_down,
+        x_in, teacher, w_qkv, w_out, vectors, shared_up, expert_up, shared_down, expert_down,
         tables[0], tables[1], seg[None, :], seg[:, None],
     )
 
@@ -450,18 +497,6 @@
     return jnp.concatenate([values[..., half:], values[..., :half]], axis=-1)
 
 
-def dp_pairs(bit):
-    n = lax.axis_size("dp")
-    return [(i, i ^ (1 << bit)) for i in range(n)]
-
-
-def dp_sum(values):
-    for bit in range(lax.axis_size("dp").bit_length() - 1):
-        values = values + lax.ppermute(values, "dp", dp_pairs(bit))
-    values = values + swap(values, "row")
-    return values + swap(values, "col")
-
-
 def remote(src, dst, send, recv, device):
     return pltpu.make_async_remote_copy(
         src_ref=src,
@@ -733,7 +768,9 @@
     sems = pltpu.SemaphoreType.DMA
     return pl.pallas_call(
         functools.partial(gather_kernel, n, plan),
-        out_shape=[jax.ShapeDtypeStruct(shape, BF) for shape in fulls],
+        out_shape=[
+            jax.ShapeDtypeStruct(shape, piece.dtype) for shape, piece in zip(fulls, pieces)
+        ],
         in_specs=[pl.BlockSpec(memory_space=pl.ANY)] * len(pieces),
         out_specs=[pl.BlockSpec(memory_space=pl.ANY)] * len(fulls),
         scratch_shapes=[
@@ -930,13 +967,6 @@
     far = swap(flip(far.astype(BF)), "row").astype(F32)
     own = parts[0] + swap(parts[1].astype(BF), "col").astype(F32)
     return own + far
-
-
-def to_sequence(values, r, c):
-    other = lax.ppermute(values, ("row", "col"), [(1, 3), (2, 0)])
-    pair = jnp.stack([values, other])
-    copied = lax.ppermute(pair, ("row", "col"), [(0, 1), (3, 2)])
-    return jnp.where(r == c, pair, copied)
 
 
 def from_sequence(values, r, c):
@@ -987,21 +1017,18 @@
     )
     (
         queries, keys_rot, values_low, context_low, normed_attn, x_own, hidden,
-        w_qkv_peer, w_out_peer, vec_peer, up_own, tokens, up_peer, down_peer,
+        w_qkv_peer, w_out_peer, vec_peer, up_own, tokens, up_peer, down_peer, teacher_pair,
     ) = front(
-        layer_input, w_qkv, w_out, vectors, w_shared_up, w_expert_up, w_shared_down, w_expert_down,
+        layer_input, teacher, w_qkv, w_out, vectors, w_shared_up, w_expert_up, w_shared_down, w_expert_down,
         tables, seg,
     )
 
     vectors = jnp.concatenate([vectors, vec_peer], axis=1)
     gain_a, gain_f, w_r = vectors[0], vectors[1], vectors[2 : 2 + E].astype(BF).T
-    t_pair = to_sequence(teacher, r, c)
-    t_seq = jnp.concatenate([t_pair[0], t_pair[1]], axis=1)
-    teacher_own = lax.dynamic_slice_in_dim(t_seq, c * part, part, 0).astype(F32)
+    teacher_own = jnp.concatenate([teacher_pair[0], teacher_pair[1]], axis=1).astype(F32)
     valid_other = swap(valid_mask, "col")
     valid_seq = jnp.where(r == c, valid_mask, valid_other).astype(F32)
     valid_own = lax.dynamic_slice_in_dim(valid_seq, c * part, part, 0)
-    count = dp_sum(jnp.full((128,), jnp.sum(valid_own), F32))[0]
     route_blocks = routes.reshape(2, 2, part, 2)
     route_blocks = jnp.where(r == 0, route_blocks, route_blocks[::-1])
     route_blocks = jnp.where(c == 0, route_blocks, route_blocks[:, ::-1]).reshape(4 * part, 2)
@@ -1030,8 +1057,7 @@
 
     error = output - teacher_own
     loss_part = jnp.sum(valid_own * jnp.sum(error * error, axis=1))
-    total_tokens = part * 4 * n_dp
-    grad_out = total_tokens / count * valid_own[:, None] * error
+    grad_out = valid_own[:, None] * error
 
     grads = spread_tokens(grad_out.astype(BF)).reshape(4 * part, D)
     down_grad, up_grad, pre_grad, gate_sums = ffn_backward(
@@ -1099,43 +1125,48 @@
     up_pair = up_pair.reshape(2, slots, owner_d, 2, quarter)
     up_piece = order_pair(r == 0, up_pair[0], up_pair[1], 3)
 
+    small = jnp.concatenate([gain_attn_grad[None], gain_ffn_grad[None], router_grad.T], axis=0)
+    small = jnp.where(r == 0, small, flip(small))
+    loss_row = jnp.full((1, D), loss_part).at[0, half:].set(jnp.sum(valid_own))
+    small = jnp.concatenate([small, loss_row, jnp.zeros((1, D), F32)])
+    small = small + swap(small, "row")
+    small = small + swap(small, "col")
     plan = [(1, (), owner_d), (3, (0,), owner_f), (3, (1,), owner_f)]
     for e in range(E):
         plan += [(0, (e,), owner_d), (2, (e, 0), owner_f), (2, (e, 1), owner_f)]
-    plan += [(4, (), 0)]
-    up_full, shared_up_full, down_full, shared_down_full, attn_full = dp_gather(
-        (up_piece[1:], up_piece[0], down_piece[1:], down_piece[0], attn_piece),
+    plan += [(4, (), 0), (5, (), 0)]
+    up_full, shared_up_full, down_full, shared_down_full, attn_full, small_full = dp_gather(
+        (up_piece[1:], up_piece[0], down_piece[1:], down_piece[0], attn_piece, small),
         (
             (E, half, 2, ff),
             (half, 2, ff),
             (E, 2, quarter, half),
             (2, quarter, half),
             (n_dp, 4, owner_d, half),
+            (n_dp, E + 4, D),
         ),
         tuple(plan),
     )
-    attn_full = attn_full.swapaxes(0, 1).reshape(4, half, half).astype(F32)
-
-    small = jnp.concatenate([gain_attn_grad[None], gain_ffn_grad[None], router_grad.T], axis=0)
-    small = jnp.where(r == 0, small, flip(small))
-    small = jnp.concatenate([small.reshape(-1), loss_part[None]])
-    small = dp_sum(small)
-    loss = small[-1] / (2.0 * count)
-    small = small[:-1].reshape(E + 2, D)
+    small = jnp.sum(small_full, axis=0)
+    count = small[E + 2, half]
+    loss = small[E + 2, 0] / (2.0 * count)
+    scale = part * 4 * n_dp / count
+    small = small[: E + 2] * scale
+    attn_full = attn_full.swapaxes(0, 1).reshape(4, half, half).astype(F32) * scale
     small = lax.dynamic_slice_in_dim(small, r * half, half, 1)
     return (
         from_sequence(output, r, c),
         loss,
-        from_sequence(input_grad, r, c),
+        from_sequence(input_grad, r, c) * scale,
         small[0],
         small[1],
         attn_full[:3].swapaxes(0, 1),
         attn_full[3],
         small[2:].T,
-        shared_up_full.astype(F32),
-        shared_down_full.reshape(ff, half).astype(F32),
-        up_full.astype(F32),
-        down_full.reshape(E, ff, half).astype(F32),
+        shared_up_full.astype(F32) * scale,
+        shared_down_full.reshape(ff, half).astype(F32) * scale,
+        up_full.astype(F32) * scale,
+        down_full.reshape(E, ff, half).astype(F32) * scale,
     )
 
 

time: 835 us -> 775 us (0.928)
  Pallas kernels: 601 us -> 565 us
  other arithmetic: 64.2 us -> 52.5 us
  starting transfers between devices: 34.1 us -> 23.7 us
    pallas_call x1, Pallas kernels: 121 us -> 91.2 us  [front(): pl.pallas_call(functools.partial(front_kernel, n), out_shape=[shape((rows...]
    mul x1 -> x7, other arithmetic: 0.08 us -> 15.9 us  [the longest x1 6.59 us: local(): up_full.astype(F32) * scale]
    convert_element_type x5 -> x0, other arithmetic: 15.5 us -> none  [the longest x1 6.13 us: local(): up_full.astype(F32)]
    ppermute x8 -> x0, starting transfers between devices: 11.6 us -> none  [the longest x6 7.14 us: dp_sum(): values = values + lax.ppermute(values, 'dp', dp_pairs(bit))]
    ppermute x2, starting transfers between devices: 4.47 us -> 14.1 us  [from_sequence(): moved = lax.ppermute(whole, ('row', 'col'), [(1, 2), (2, 1)])]
    ppermute x20 -> x18, starting transfers between devices: 18 us -> 9.6 us  [swap(): return lax.ppermute(values, axis, [(0, 1), (1, 0)])]
    ppermute x20 -> x18, waiting for transfers between devices: 49.3 us -> 48 us  [swap(): return lax.ppermute(values, axis, [(0, 1), (1, 0)])]
  transfers between devices with their start and end apart: 30 -> 20, of which waited for: 11 -> 9; matrix products, arithmetic and copies ran while one was open for 10% -> 8% of each run, Pallas kernels for 71% -> 33%
where the time goes in v4:
time: 775 us; the launch traced here: 764 us
  Pallas kernels  565 us (73%)
  waiting for transfers between devices  59.2 us (8%)
  other arithmetic  52.5 us (7%)
  local copies, waits for them, and re-layouts  37.8 us (5%)
  starting transfers between devices  23.7 us (3%)
  matrix products  18.6 us (2%)
    pallas_call x1, Pallas kernels, dp_gather(): pl.pallas_call(functools.partial(gather_kernel, n, plan), out_shape=[jax....  163 us
    pallas_call x1, Pallas kernels, dp_reduce(): pl.pallas_call(functools.partial(reduce_kernel, n, slots), out_shape=[jax...  159 us
    pallas_call x1, Pallas kernels, front(): pl.pallas_call(functools.partial(front_kernel, n), out_shape=[shape((rows...  91.2 us
    pallas_call x1, Pallas kernels, ffn_backward(): pl.pallas_call(ffn_back_kernel, grid=(slots,), out_shape=[jax.ShapeDtypeS...  57.4 us
    ppermute x18, waiting for transfers between devices, swap(): return lax.ppermute(values, axis, [(0, 1), (1, 0)])  48 us
    pallas_call x1, Pallas kernels, ffn_forward(): pl.pallas_call(ffn_kernel, grid=(slots,), out_shape=[jax.ShapeDtypeStruct...  42.5 us
    pallas_call x2, Pallas kernels, ffn_input(): pl.pallas_call(ffn_input_kernel, grid=(slots,), out_shape=jax.ShapeDtypeS...  32.5 us
    pallas_call x3, Pallas kernels, attend_backward(): pl.pallas_call(attend_back_kernel, grid=(pairs,), out_shape=jax.ShapeDtyp...  19 us
  transfers between devices with their start and end apart: 20, of which 9 were waited for; matrix products, arithmetic and copies ran while one was open for 8% of the time, Pallas kernels for 33%

profile of v4, /device:TPU:27, one launch (start us, length us, event | category | flops | bytes accessed | tf_op | source)
XLA Modules:
  0.0 764.1 jit_solution(8787212629818045979)
XLA Ops:
  6.1 91.2 %shard_map.229 = (bf16[1024,384]{1,0:T(8,128)(2,1)S(1)}, bf16[1024,384]{1,0:T(8,128)(2,1)S(1)}, bf16[1024,384]{1,0:T(8,128)(2,1)S(1)}, bf16[1024,384]{1,0:T(8,12...) custom-call(bf16[1024,384]{1,0:T(8,128)(2,1)} %x_in.1, ...), custom_call_target="tpu_custom_call" | custom-call | tf_op jit(solution)/shard_map/pallas_call | solution.py:375
  97.4 4.0 fusion.36
  103.0 2.9 fusion.down_own
  106.0 42.5 %shard_map.230 = (bf16[5,2048,1024]{2,1,0:T(8,128)(2,1)}, bf16[5,2048,512]{2,1,0:T(8,128)(2,1)}, f32[2048,768]{1,0:T(8,128)}) custom-call(bf16[2048,768]{1,0:T(8,128)(2,1)} %bitcast.131, bf16[5,384,1024]{2,1,0:T(8,128)(2,1)} %get-tuple-element.57.up_own, bf16[5,384,1024]{2,1,0:T(8,128)(2,1)} %get-tuple-element.58.up_peer, ...), custom_call_target="tpu_custom_call" | custom-call | flops 24159191040 | bytes 41943040 | tf_op jit(solution)/shard_map/pallas_call | solution.py:823
  148.5 3.1 convert.15
  159.0 17.8 %collective-permute-done.2 = bf16[512,768]{1,0:T(8,128)(2,1)S(1)} collective-permute-done((bf16[512,768]{1,0:T(8,128)(2,1)}, bf16[512,768]{1,0:T(8,128)(2,1)S(1)}, u32[]{:S(2)}, u32[]{:S(2)}) %collective-permute-start.2) | collective-permute-done | bytes 786464 | tf_op jit(solution)/shard_map/ppermute | solution.py:492
  177.6 3.0 multiply_reduce_fusion
  186.8 15.6 %collective-permute-done.7 = bf16[512,768]{1,0:T(8,128)(2,1)} collective-permute-done((bf16[512,768]{1,0:T(8,128)(2,1)}, bf16[512,768]{1,0:T(8,128)(2,1)}, u32[]{:S(2)}, u32[]{:S(2)}) %collective-permute-start.7) | collective-permute-done | bytes 786464 | tf_op jit(solution)/shard_map/ppermute | solution.py:492
  207.9 2.9 pad_maximum_fusion
  210.8 57.4 %shard_map.231 = (bf16[5,512,768]{2,1,0:T(8,128)(2,1)}, bf16[5,768,1024]{2,1,0:T(8,128)(2,1)}, bf16[5,2048,1024]{2,1,0:T(8,128)(2,1)}, f32[2048,8]{1,0:T(8,128)}) custom-call(bf16[2048,768]{1,0:T(8,128)(2,1)} %bitcast.147, bf16[2048,768]{1,0:T(8,128)(2,1)} %bitcast.132, bf16[5,2048,1024]{2,1,0:T(8,128)(2,1)} %get-tuple-element.63.pre, ...), custom_call_target="tpu_custom_call" | custom-call | flops 32212254720 | bytes 73400320 | tf_op jit(solution)/shard_map/pallas_call | solution.py:887
  270.8 2.1 copy-done.2
  272.9 2.1 copy-done.3
  275.0 16.2 %shard_map.233 = f32[1024,768]{1,0:T(8,128)S(1)} custom-call(bf16[5,2048,1024]{2,1,0:T(8,128)(2,1)} %get-tuple-element.71.pre_grad, bf16[5,384,1024]{2,1,0:T(8,128)(2,1)S(1)} %copy-done.2, bf16[5,384,1024]{2,1,0:T(8,128)(2,1)S(1)} %copy-done.3), custom_call_target="tpu_custom_call" | custom-call | flops 8053063680 | bytes 20971520 | tf_op jit(solution)/shard_map/pallas_call | solution.py:941
  292.6 16.2 %shard_map.232 = f32[1024,768]{1,0:T(8,128)S(1)} custom-call(bf16[5,2048,1024]{2,1,0:T(8,128)(2,1)} %get-tuple-element.71.pre_grad, bf16[5,384,1024]{2,1,0:T(8,128)(2,1)S(1)} %copy-done.2, bf16[5,384,1024]{2,1,0:T(8,128)(2,1)S(1)} %copy-done.3), custom_call_target="tpu_custom_call" | custom-call | flops 8053063680 | bytes 20971520 | tf_op jit(solution)/shard_map/pallas_call | solution.py:941
  314.6 3.2 maximum_select_fusion
  317.8 2.5 collective-permute-start.4
  321.4 9.8 %collective-permute-done.13 = f32[4,512]{1,0:T(4,128)S(1)} collective-permute-done((f32[4,512]{1,0:T(4,128)}, f32[4,512]{1,0:T(4,128)S(1)}, u32[]{:S(2)}, u32[]{:S(2)}) %collective-permute-start.13) | collective-permute-done | bytes 8224 | tf_op jit(solution)/shard_map/ppermute | solution.py:492
  331.2 2.9 multiply_reduce_fusion.1
  341.5 6.6 collective-permute-done.4
  348.1 2.7 broadcast_select_fusion.1
  353.2 6.3 shard_map.236
  359.5 6.5 shard_map.235
  366.0 6.3 shard_map.234
  373.9 2.2 reshape.236
  376.3 5.5 fusion.1
  381.7 2.3 convolution_convert_fusion
  384.3 159.5 %shard_map.237 = (bf16[2,5,48,1024]{3,2,1,0:T(8,128)(2,1)S(1)}, bf16[2,5,64,384]{3,2,1,0:T(8,128)(2,1)S(1)}, bf16[192,384]{1,0:T(8,128)(2,1)S(1)}) custom-call(bf16[5,2,4,2,48,1024]{5,4,3,2,1,0:T(8,128)(2,1)} %bitcast.134, bf16[5,4,2,64,768]{4,3,2,1,0:T(8,128)(2,1)} %bitcast.144, bf16[2,4,2,192,384]{4,3,2,1,0:T(8,128)(2,1)S(1)} %bitcast.128), custom_call_target="tpu_custom_call" | custom-call | tf_op jit(solution)/shard_map/pallas_call | solution.py:649
  559.1 163.4 %shard_map.238 = (bf16[4,384,2,1024]{3,2,1,0:T(2,128)(2,1)}, bf16[384,2,1024]{2,1,0:T(2,128)(2,1)}, bf16[4,2,512,384]{3,2,1,0:T(8,128)(2,1)}, bf16[2,512,384]{2,...) custom-call(bf16[4,48,2,1024]{3,2,1,0:T(2,128)(2,1)} %slice.271.refs_0_, ...), custom_call_target="tpu_custom_call" | custom-call | tf_op jit(solution)/shard_map/pallas_call | solution.py:769
  731.8 11.6 %collective-permute-start.19 = (f32[1024,384]{1,0:T(8,128)S(1)}, f32[1024,384]{1,0:T(8,128)S(1)}, u32[]{:S(2)}, u32[]{:S(2)}) collective-permute-start(f32[1024,384]{1,0:T(8,128)S(1)} %maximum_select_fusion.2), channel_id=1, source_target_pairs={{1,2},{2,1},{5,6},{6,5},{9,10},{10,9},{13,14},{14,13},{17,18},{18,... | collective-permute-start | bytes 4718600 | tf_op jit(solution)/shard_map/ppermute | solution.py:980
  747.0 3.2 convert_multiply_fusion.1
  750.3 6.6 convert_multiply_fusion
  756.9 4.6 collective-permute-done.19
  (245 shorter events, 74.7 us)
Async XLA Ops:
  5.4 92.0 %copy-start.4 = (f32[1024,128]{1,0:T(8,128)}, f32[1024,128]{1,0:T(8,128)S(1)}, u32[]{:S(2)}) copy-start(f32[1024,128]{1,0:T(8,128)S(1)} %copy.80.sine) | copy-start | bytes 1572868
  5.6 91.7 %copy-start.6 = (s32[1024,1]{1,0:T(8,128)}, s32[1024,1]{1,0:T(8,128)S(1)}, u32[]{:S(2)}) copy-start(s32[1024,1]{1,0:T(8,128)S(1)} %copy.81.seg_col) | copy-start | bytes 12292
  5.9 91.5 %copy-start.8 = (f32[1024,128]{1,0:T(8,128)}, f32[1024,128]{1,0:T(8,128)S(1)}, u32[]{:S(2)}) copy-start(f32[1024,128]{1,0:T(8,128)S(1)} %copy.79.cosine) | copy-start | bytes 1572868
  152.6 2.3 collective-permute-start.1
  152.7 6.3 collective-permute-start
  157.5 19.2 %collective-permute-start.2 = (bf16[512,768]{1,0:T(8,128)(2,1)}, bf16[512,768]{1,0:T(8,128)(2,1)S(1)}, u32[]{:S(2)}, u32[]{:S(2)}) collective-permute-start(bf16[512,768]{1,0:T(8,128)(2,1)} %pad_maximum_fusion.5), channel_id=1, source_target_pairs={{0,2},{2,0},{1,3},{3,1},{4,6},{6,4},{5,7},{7,5},{8,10},{10,8},{9,1... | collective-permute-start | bytes 2359304 | tf_op jit(solution)/shard_map/ppermute | solution.py:492
  157.7 1.3 collective-permute-start.5
  158.2 22.4 %copy-start.25 = (bf16[512,384]{1,0:T(8,128)(2,1)}, bf16[512,384]{1,0:T(8,128)(2,1)S(1)}, u32[]{:S(2)}) copy-start(bf16[512,384]{1,0:T(8,128)(2,1)S(1)} %get-tuple-element.124) | copy-start | bytes 1179652
  158.2 22.4 %copy-start.27 = (bf16[512,384]{1,0:T(8,128)(2,1)}, bf16[512,384]{1,0:T(8,128)(2,1)S(1)}, u32[]{:S(2)}) copy-start(bf16[512,384]{1,0:T(8,128)(2,1)S(1)} %get-tuple-element.125) | copy-start | bytes 1179652
  159.0 17.8 %copy-start.39 = (bf16[512,768]{1,0:T(8,128)(2,1)}, bf16[512,768]{1,0:T(8,128)(2,1)S(1)}, u32[]{:S(2)}) copy-start(bf16[512,768]{1,0:T(8,128)(2,1)S(1)} %collective-permute-done) | copy-start | bytes 2359300
  180.7 25.9 %copy-start.22 = (f32[512,768]{1,0:T(8,128)}, f32[512,768]{1,0:T(8,128)S(1)}, u32[]{:S(2)}) copy-start(f32[512,768]{1,0:T(8,128)S(1)} %get-tuple-element.98) | copy-start | bytes 4718596
  183.9 18.4 %collective-permute-start.7 = (bf16[512,768]{1,0:T(8,128)(2,1)}, bf16[512,768]{1,0:T(8,128)(2,1)}, u32[]{:S(2)}, u32[]{:S(2)}) collective-permute-start(bf16[512,768]{1,0:T(8,128)(2,1)} %pad_maximum_fusion.6), channel_id=1, source_target_pairs={{0,2},{2,0},{1,3},{3,1},{4,6},{6,4},{5,7},{7,5},{8,10},{10,8},{9,1... | collective-permute-start | bytes 2359304 | tf_op jit(solution)/shard_map/ppermute | solution.py:492
  184.8 20.5 %copy-start.38 = (bf16[2,1024,384]{2,1,0:T(8,128)(2,1)S(1)}, bf16[2,1024,384]{2,1,0:T(8,128)(2,1)}, u32[]{:S(2)}) copy-start(bf16[2,1024,384]{2,1,0:T(8,128)(2,1)} %get-tuple-element.67) | copy-start | bytes 4718596
  185.5 22.4 %collective-permute-start.6 = (bf16[512,768]{1,0:T(8,128)(2,1)S(1)}, bf16[512,768]{1,0:T(8,128)(2,1)S(1)}, u32[]{:S(2)}, u32[]{:S(2)}) collective-permute-start(bf16[512,768]{1,0:T(8,128)(2,1)S(1)} %multiply_convert_fusion), channel_id=1, source_target_pairs={{0,1},{1,0},{2,3},{3,2},{4,5},{5,4},{6,7},{7,6},{8,9},{9,8},{10,11... | collective-permute-start | bytes 2359304 | tf_op jit(solution)/shard_map/ppermute | solution.py:492
  202.4 5.6 collective-permute-start.8
  207.9 106.7 %collective-permute-start.3 = (f32[512,384]{1,0:T(8,128)}, f32[512,384]{1,0:T(8,128)}, u32[]{:S(2)}, u32[]{:S(2)}) collective-permute-start(f32[512,384]{1,0:T(8,128)} %get-tuple-element.109), channel_id=1, source_target_pairs={{0,1},{1,0},{2,3},{3,2},{4,5},{5,4},{6,7},{7,6},{8,9},{9,8},{10,11... | collective-permute-start | bytes 2359304 | tf_op jit(solution)/shard_map/ppermute | solution.py:492
  291.4 18.9 %collective-permute-start.10 = (bf16[512,768]{1,0:T(8,128)(2,1)S(1)}, bf16[512,768]{1,0:T(8,128)(2,1)S(1)}, u32[]{:S(2)}, u32[]{:S(2)}) collective-permute-start(bf16[512,768]{1,0:T(8,128)(2,1)S(1)} %slice.344), channel_id=1, source_target_pairs={{0,1},{1,0},{2,3},{3,2},{4,5},{5,4},{6,7},{7,6},{8,9},{9,8},{10,11... | collective-permute-start | bytes 2359304 | tf_op jit(solution)/shard_map/ppermute | solution.py:492
  292.5 20.2 %collective-permute-start.12 = (f32[2,4,512]{2,1,0:T(4,128)}, f32[2,4,512]{2,1,0:T(4,128)S(1)}, u32[]{:S(2)}, u32[]{:S(2)}) collective-permute-start(f32[2,4,512]{2,1,0:T(4,128)} %pad_maximum_fusion.12), channel_id=1, source_target_pairs={{0,1},{1,0},{2,3},{3,2},{4,5},{5,4},{6,7},{7,6},{8,9},{9,8},{10,11... | collective-permute-start | bytes 49160 | tf_op jit(solution)/shard_map/ppermute | solution.py:492
  309.8 21.4 %collective-permute-start.9 = (bf16[512,768]{1,0:T(8,128)(2,1)}, bf16[512,768]{1,0:T(8,128)(2,1)}, u32[]{:S(2)}, u32[]{:S(2)}) collective-permute-start(bf16[512,768]{1,0:T(8,128)(2,1)} %slice.345), channel_id=1, source_target_pairs={{0,1},{1,0},{2,3},{3,2},{4,5},{5,4},{6,7},{7,6},{8,9},{9,8},{10,11... | collective-permute-start | bytes 2359304 | tf_op jit(solution)/shard_map/ppermute | solution.py:492
  311.5 19.7 %collective-permute-start.11 = (bf16[512,768]{1,0:T(8,128)(2,1)}, bf16[512,768]{1,0:T(8,128)(2,1)}, u32[]{:S(2)}, u32[]{:S(2)}) collective-permute-start(bf16[512,768]{1,0:T(8,128)(2,1)} %pad_maximum_fusion.7), channel_id=1, source_target_pairs={{0,2},{2,0},{1,3},{3,1},{4,6},{6,4},{5,7},{7,5},{8,10},{10,8},{9,1... | collective-permute-start | bytes 2359304 | tf_op jit(solution)/shard_map/ppermute | solution.py:492
  313.3 17.8 %collective-permute-start.13 = (f32[4,512]{1,0:T(4,128)}, f32[4,512]{1,0:T(4,128)S(1)}, u32[]{:S(2)}, u32[]{:S(2)}) collective-permute-start(f32[4,512]{1,0:T(4,128)} %fusion.29), channel_id=1, source_target_pairs={{0,2},{2,0},{1,3},{3,1},{4,6},{6,4},{5,7},{7,5},{8,10},{10,8},{9,1... | collective-permute-start | bytes 24584 | tf_op jit(solution)/shard_map/ppermute | solution.py:492
  317.8 30.3 %collective-permute-start.4 = (f32[1024,384]{1,0:T(8,128)}, f32[1024,384]{1,0:T(8,128)}, u32[]{:S(2)}, u32[]{:S(2)}) collective-permute-start(f32[1024,384]{1,0:T(8,128)} %maximum_select_fusion), channel_id=1, source_target_pairs={{1,2},{2,1},{5,6},{6,5},{9,10},{10,9},{13,14},{14,13},{17,18},{18,... | collective-permute-start | bytes 4718600 | tf_op jit(solution)/shard_map/ppermute | solution.py:980
  335.9 14.9 %collective-permute-start.14 = (bf16[512,768]{1,0:T(8,128)(2,1)S(1)}, bf16[512,768]{1,0:T(8,128)(2,1)S(1)}, u32[]{:S(2)}, u32[]{:S(2)}) collective-permute-start(bf16[512,768]{1,0:T(8,128)(2,1)S(1)} %get-tuple-element.99), channel_id=1, source_target_pairs={{0,1},{1,0},{2,3},{3,2},{4,5},{5,4},{6,7},{7,6},{8,9},{9,8},{10,11... | collective-permute-start | bytes 2359304 | tf_op jit(solution)/shard_map/ppermute | solution.py:492
  341.5 9.3 %copy-start.21 = (bf16[384,384]{1,0:T(8,128)(2,1)S(1)}, bf16[384,384]{1,0:T(8,128)(2,1)}, u32[]{:S(2)}) copy-start(bf16[384,384]{1,0:T(8,128)(2,1)} %copy-done.20) | copy-start | bytes 884740
  366.0 6.3 copy-start.13
  546.7 6.0 collective-permute-start.15
  553.6 2.7 collective-permute-start.16
  556.4 2.2 collective-permute-start.17
  557.8 173.9 %collective-permute-start.18 = (f32[512,384]{1,0:T(8,128)S(1)}, f32[512,384]{1,0:T(8,128)S(1)}, u32[]{:S(2)}, u32[]{:S(2)}) collective-permute-start(f32[512,384]{1,0:T(8,128)S(1)} %get-tuple-element.104), channel_id=1, source_target_pairs={{0,1},{1,0},{2,3},{3,2},{4,5},{5,4},{6,7},{7,6},{8,9},{9,8},{10,11... | collective-permute-start | bytes 2359304 | tf_op jit(solution)/shard_map/ppermute | solution.py:492
  731.7 12.3 %copy-start.37 = (bf16[384,2,1024]{2,1,0:T(2,128)(2,1)S(1)}, bf16[384,2,1024]{2,1,0:T(2,128)(2,1)}, u32[]{:S(2)}) copy-start(bf16[384,2,1024]{2,1,0:T(2,128)(2,1)} %get-tuple-element.82) | copy-start | bytes 4718596
  731.8 29.7 %collective-permute-start.19 = (f32[1024,384]{1,0:T(8,128)S(1)}, f32[1024,384]{1,0:T(8,128)S(1)}, u32[]{:S(2)}, u32[]{:S(2)}) collective-permute-start(f32[1024,384]{1,0:T(8,128)S(1)} %maximum_select_fusion.2), channel_id=1, source_target_pairs={{1,2},{2,1},{5,6},{6,5},{9,10},{10,9},{13,14},{14,13},{17,18},{18,... | collective-permute-start | bytes 4718600 | tf_op jit(solution)/shard_map/ppermute | solution.py:980
  750.3 12.5 %copy-start.1 = (s32[2,1024]{1,0:T(2,128)S(1)}, s32[2,1024]{1,0:T(2,128)}, u32[]{:S(2)}) copy-start(s32[2,1024]{1,0:T(2,128)} %param.20) | copy-start | bytes 24580
  (38 other events, 100.0 us)

commit v5 on v4

--- a/solution.py
+++ b/solution.py
@@ -792,9 +792,17 @@
     return jnp.sum(jnp.where(lanes_of(values.shape) == index, values, 0.0), axis=1, keepdims=True)
 
 
-def ffn_kernel(tokens, up_own, up_peer, down_own, down_peer, mix, pre, act, out):
+def clear(first, ref):
+    @pl.when(first)
+    def _():
+        ref[...] = jnp.zeros(ref.shape, ref.dtype)
+
+
+def ffn_kernel(tokens, up_own, up_peer, down_own, down_peer, mix, *refs):
+    pre, act, out = refs[-3:]
     slot = pl.program_id(0)
     quarter = down_own.shape[1]
+    clear(slot == 0, out)
     w_up = jnp.concatenate([up_own[0], up_peer[0]], axis=0)
     w_down = jnp.concatenate([down_own[0], down_peer[0]], axis=1)
     for tile in range(tokens.shape[0] // TILE):
@@ -804,56 +812,55 @@
         gate, up = both[:, :quarter], both[:, quarter:]
         hidden = gate / (1.0 + jnp.exp(-gate)) * up * column(mix[rows], slot)
         act[0, rows] = hidden.astype(BF)
-        part = jnp.dot(hidden.astype(BF), w_down, preferred_element_type=F32)
-
-        @pl.when(slot == 0)
-        def _():
-            out[rows] = part
-
-        @pl.when(slot > 0)
-        def _():
-            out[rows] += part
-
-
-def ffn_forward(tokens, up_own, up_peer, down_own, down_peer, mix):
+        out[rows] += jnp.dot(hidden.astype(BF), w_down, preferred_element_type=F32)
+
+
+def ffn_forward(tokens, up_own, up_peer, down_own, down_peer, mix, part, parts, filled=()):
     slots, half, width = up_own.shape
     rows, depth = tokens.shape
+    size = rows // parts
     per_slot = lambda *shape: pl.BlockSpec((1,) + shape, lambda e: (e, 0, 0))
-    whole = lambda *shape: pl.BlockSpec(shape, lambda e: (0, 0))
+    of_part = lambda *shape: pl.BlockSpec((1,) + shape, lambda e: (e, part, 0))
+    whole = lambda *shape: pl.BlockSpec(shape, lambda e: (part, 0))
     return pl.pallas_call(
         ffn_kernel,
         grid=(slots,),
         out_shape=[
             jax.ShapeDtypeStruct((slots, rows, width), BF),
             jax.ShapeDtypeStruct((slots, rows, width // 2), BF),
-            jax.ShapeDtypeStruct((rows, depth), F32),
+            jax.ShapeDtypeStruct((size, depth), F32),
         ],
         in_specs=[
-            whole(rows, depth),
+            whole(size, depth),
             per_slot(half, width),
             per_slot(half, width),
             per_slot(width // 2, half),
             per_slot(width // 2, half),
-            whole(rows, 8),
-        ],
-        out_specs=[per_slot(rows, width), per_slot(rows, width // 2), whole(rows, depth)],
+            whole(size, 8),
+        ]
+        + [pl.BlockSpec(memory_space=pl.ANY)] * len(filled),
+        out_specs=[
+            of_part(size, width),
+            of_part(size, width // 2),
+            pl.BlockSpec((size, depth), lambda e: (0, 0)),
+        ],
+        input_output_aliases={6: 0, 7: 1} if filled else {},
         compiler_params=pltpu.CompilerParams(vmem_limit_bytes=56 << 20),
         cost_estimate=pl.CostEstimate(
-            flops=3 * slots * rows * depth * width,
-            bytes_accessed=40 << 20,
-            transcendentals=slots * rows * width // 2,
+            flops=3 * slots * size * depth * width,
+            bytes_accessed=20 << 20,
+            transcendentals=slots * size * width // 2,
         ),
-    )(tokens, up_own, up_peer, down_own, down_peer, mix)
-
-
-def ffn_back_kernel(
-    grads, tokens, pre, act, down_own, down_peer, mix, down_grad, up_grad, pre_grad, gate_sum
-):
+    )(tokens, up_own, up_peer, down_own, down_peer, mix, *filled)
+
+
+def ffn_back_kernel(grads, pre, down_own, down_peer, mix, *refs):
+    pre_grad, gate_sum = refs[-2:]
     slot = pl.program_id(0)
     quarter = down_own.shape[1]
+    clear(slot == 0, gate_sum)
     w_down = jnp.concatenate([down_own[0], down_peer[0]], axis=1)
-    depth = tokens.shape[1]
-    for tile in range(tokens.shape[0] // TILE):
+    for tile in range(grads.shape[0] // TILE):
         rows = pl.ds(tile * TILE, TILE)
         back = lax.dot_general(grads[rows], w_down, NT, preferred_element_type=F32)
         gate = pre[0, rows, :quarter].astype(F32)
@@ -861,76 +868,88 @@
         sigma = 1.0 / (1.0 + jnp.exp(-gate))
         act_silu = gate * sigma
         sums = jnp.sum(back * act_silu * up, axis=1, keepdims=True)
-        mine = lanes_of((TILE, 8)) == slot
-
-        @pl.when(slot == 0)
-        def _():
-            gate_sum[rows] = jnp.zeros((TILE, 8), F32)
-
-        gate_sum[rows] += jnp.where(mine, sums, 0.0)
+        gate_sum[rows] += jnp.where(lanes_of((TILE, 8)) == slot, sums, 0.0)
         back = back * column(mix[rows], slot)
         pre_grad[0, rows, :quarter] = (back * up * (sigma * (1.0 + gate * (1.0 - sigma)))).astype(BF)
         pre_grad[0, rows, quarter:] = (back * act_silu).astype(BF)
-    down_grad[0] = lax.dot_general(act[0], grads[...], TN, preferred_element_type=F32).astype(BF)
-    for tile in range(depth // 256):
+
+
+def ffn_backward(grads, pre, down_own, down_peer, mix, part, parts, filled=()):
+    slots, rows, width = pre.shape
+    size, depth = grads.shape
+    per_slot = lambda *shape: pl.BlockSpec((1,) + shape, lambda e: (e, 0, 0))
+    of_part = lambda *shape: pl.BlockSpec((1,) + shape, lambda e: (e, part, 0))
+    return pl.pallas_call(
+        ffn_back_kernel,
+        grid=(slots,),
+        out_shape=[
+            jax.ShapeDtypeStruct((slots, rows, width), BF),
+            jax.ShapeDtypeStruct((size, 8), F32),
+        ],
+        in_specs=[
+            pl.BlockSpec((size, depth), lambda e: (0, 0)),
+            of_part(size, width),
+            per_slot(width // 2, depth // 2),
+            per_slot(width // 2, depth // 2),
+            pl.BlockSpec((size, 8), lambda e: (part, 0)),
+        ]
+        + [pl.BlockSpec(memory_space=pl.ANY)] * len(filled),
+        out_specs=[of_part(size, width), pl.BlockSpec((size, 8), lambda e: (0, 0))],
+        input_output_aliases={5: 0} if filled else {},
+        compiler_params=pltpu.CompilerParams(vmem_limit_bytes=56 << 20),
+        cost_estimate=pl.CostEstimate(
+            flops=2 * slots * size * depth * width,
+            bytes_accessed=25 << 20,
+            transcendentals=slots * size * width // 2,
+        ),
+    )(grads, pre, down_own, down_peer, mix, *filled)
+
+
+def ffn_weights_kernel(near, far, tokens, act, pre_grad, down_grad, up_grad):
+    size = near.shape[0]
+    total = lax.dot_general(act[0, :size], near[...], TN, preferred_element_type=F32)
+    total = total + lax.dot_general(act[0, size:], far[...], TN, preferred_element_type=F32)
+    down_grad[0] = total.astype(BF)
+    for tile in range(tokens.shape[1] // 256):
         columns = slice(tile * 256, (tile + 1) * 256)
         up_grad[0, columns] = lax.dot_general(
             tokens[:, columns], pre_grad[0], TN, preferred_element_type=F32
         ).astype(BF)
 
 
-def ffn_backward(grads, tokens, pre, act, down_own, down_peer, mix):
-    slots, rows, width = pre.shape
+def ffn_weights(near, far, tokens, act, pre_grad):
+    slots, rows, width = pre_grad.shape
     depth = tokens.shape[1]
     per_slot = lambda *shape: pl.BlockSpec((1,) + shape, lambda e: (e, 0, 0))
     whole = lambda *shape: pl.BlockSpec(shape, lambda e: (0, 0), pipeline_mode=pl.Buffered(1))
     return pl.pallas_call(
-        ffn_back_kernel,
+        ffn_weights_kernel,
         grid=(slots,),
         out_shape=[
             jax.ShapeDtypeStruct((slots, width // 2, depth), BF),
             jax.ShapeDtypeStruct((slots, depth, width), BF),
-            jax.ShapeDtypeStruct((slots, rows, width), BF),
-            jax.ShapeDtypeStruct((rows, 8), F32),
         ],
         in_specs=[
+            whole(rows // 2, depth),
+            whole(rows // 2, depth),
             whole(rows, depth),
-            whole(rows, depth),
+            per_slot(rows, width // 2),
             per_slot(rows, width),
-            per_slot(rows, width // 2),
-            per_slot(width // 2, depth // 2),
-            per_slot(width // 2, depth // 2),
-            whole(rows, 8),
-        ],
-        out_specs=[
-            per_slot(width // 2, depth),
-            per_slot(depth, width),
-            per_slot(rows, width),
-            pl.BlockSpec((rows, 8), lambda e: (0, 0)),
-        ],
-        compiler_params=pltpu.CompilerParams(vmem_limit_bytes=58 << 20),
+        ],
+        out_specs=[per_slot(width // 2, depth), per_slot(depth, width)],
+        compiler_params=pltpu.CompilerParams(vmem_limit_bytes=56 << 20),
         cost_estimate=pl.CostEstimate(
-            flops=4 * slots * rows * depth * width,
-            bytes_accessed=70 << 20,
-            transcendentals=slots * rows * width // 2,
+            flops=3 * slots * rows * depth * width, bytes_accessed=50 << 20, transcendentals=0
         ),
-    )(grads, tokens, pre, act, down_own, down_peer, mix)
+    )(near, far, tokens, act, pre_grad)
 
 
 def ffn_input_kernel(pre_grad, up_own, up_peer, out):
-    slot = pl.program_id(0)
+    clear(pl.program_id(0) == 0, out)
     w_up = jnp.concatenate([up_own[0], up_peer[0]], axis=0)
     for tile in range(out.shape[0] // TILE):
         rows = pl.ds(tile * TILE, TILE)
-        part = lax.dot_general(pre_grad[0, rows], w_up, NT, preferred_element_type=F32)
-
-        @pl.when(slot == 0)
-        def _():
-            out[rows] = part
-
-        @pl.when(slot > 0)
-        def _():
-            out[rows] += part
+        out[rows] += lax.dot_general(pre_grad[0, rows], w_up, NT, preferred_element_type=F32)
 
 
 def ffn_input(pre_grad, up_own, up_peer, part, parts):
@@ -955,18 +974,18 @@
     )(pre_grad, up_own, up_peer)
 
 
-def spread_tokens(own):
-    near = swap(own, "col")
-    far = swap(flip(own), "row")
-    far_near = swap(far, "col")
-    return jnp.stack([own, near, far, far_near])
-
-
-def collect_tokens(parts):
-    far = parts[2] + swap(parts[3].astype(BF), "col").astype(F32)
-    far = swap(flip(far.astype(BF)), "row").astype(F32)
-    own = parts[0] + swap(parts[1].astype(BF), "col").astype(F32)
-    return own + far
+def join_core(parts):
+    size = parts.shape[0] // 2
+    return parts[:size] + swap(parts[size:].astype(BF), "col").astype(F32)
+
+
+def collect_tokens(far, near_of, operand):
+    send = flip(join_core(far).astype(BF))
+    send, operand = lax.optimization_barrier((send, operand))
+    recv = swap(send, "row")
+    near, *rest = near_of(operand)
+    near, recv = lax.optimization_barrier((near, recv))
+    return (join_core(near) + recv.astype(F32), *rest)
 
 
 def from_sequence(values, r, c):
@@ -1052,23 +1071,36 @@
     mix = jnp.concatenate(
         [jnp.ones((4 * part, 1), F32), mixing, jnp.zeros((4 * part, 7 - E), F32)], axis=1
     )
-    pre, act, branch = ffn_forward(tokens, up_own, up_peer, down_own, down_peer, mix)
-    output = hidden + collect_tokens(branch.reshape(4, part, D))
+    weights = (up_own, up_peer, down_own, down_peer)
+    pre, act, far = ffn_forward(tokens, *weights, mix, 1, 2)
+
+    def near_forward(operand):
+        pre, act, near = ffn_forward(operand[0], *weights, mix, 0, 2, operand[1:])
+        return near, pre, act
+
+    branch, pre, act = collect_tokens(far, near_forward, (tokens, pre, act))
+    output = hidden + branch
 
     error = output - teacher_own
     loss_part = jnp.sum(valid_own * jnp.sum(error * error, axis=1))
     grad_out = valid_own[:, None] * error
 
-    grads = spread_tokens(grad_out.astype(BF)).reshape(4 * part, D)
-    down_grad, up_grad, pre_grad, gate_sums = ffn_backward(
-        grads, tokens, pre, act, down_own, down_peer, mix
-    )
-    far_part = ffn_input(pre_grad, up_own, up_peer, 1, 2).reshape(2, part, D)
-    near_part = ffn_input(pre_grad, up_own, up_peer, 0, 2).reshape(2, part, D)
-    normed_ffn_grad = collect_tokens([near_part[0], near_part[1], far_part[0], far_part[1]])
-    gate_parts = gate_sums[:, 1 : E + 1].T.reshape(E, 4, part)
+    low_own = grad_out.astype(BF)
+    far = swap(flip(low_own), "row")
+    near = jnp.concatenate([low_own, swap(low_own, "col")])
+    pre_grad, near_sums = ffn_backward(near, pre, down_own, down_peer, mix, 0, 2)
+    pre_grad, far = lax.optimization_barrier((pre_grad, far))
+    far = jnp.concatenate([far, swap(far, "col")])
+    pre_grad, far_sums = ffn_backward(far, pre, down_own, down_peer, mix, 1, 2, (pre_grad,))
+    gate_parts = jnp.concatenate([near_sums, far_sums])[:, 1 : E + 1].T.reshape(E, 4, part)
     recv = swap(jnp.stack([gate_parts[:, 1], gate_parts[:, 3]]), "col")
     gate_grad = gate_parts[:, 0] + recv[0] + swap(gate_parts[:, 2] + recv[1], "row")
+    down_grad, up_grad = ffn_weights(near, far, tokens, act, pre_grad)
+    pre_grad, gate_grad, up_grad = lax.optimization_barrier((pre_grad, gate_grad, up_grad))
+    far = ffn_input(pre_grad, up_own, up_peer, 1, 2)
+    (normed_ffn_grad,) = collect_tokens(
+        far, lambda operand: (ffn_input(operand, up_own, up_peer, 0, 2),), pre_grad
+    )
     mix_own = mixing[:part].T
     centre = jnp.sum(mix_own * gate_grad, axis=0, keepdims=True)
     logit_grad = (mix_own * (gate_grad - centre)).T.astype(BF)

time: 775 us -> 733 us (0.946)
  waiting for transfers between devices: 59.2 us -> 29.2 us
  other arithmetic: 52.5 us -> 41.9 us
  local copies, waits for them, and re-layouts: 37.8 us -> 46.5 us
    ppermute x18, waiting for transfers between devices: 48 us -> 13.8 us  [swap(): return lax.ppermute(values, axis, [(0, 1), (1, 0)])]
    pallas_call x0 -> x1, Pallas kernels: none -> 31.6 us  [ffn_weights(): pl.pallas_call(ffn_weights_kernel, grid=(slots,), out_shape=[jax.ShapeDty...]
    pallas_call x1 -> x2, Pallas kernels: 57.4 us -> 30.7 us  [ffn_backward(): pl.pallas_call(ffn_back_kernel, grid=(slots,), out_shape=[jax.ShapeDtypeS...]
    pallas_call x2, Pallas kernels: 32.5 us -> 22.1 us  [ffn_input(): pl.pallas_call(ffn_input_kernel, grid=(slots,), out_shape=jax.ShapeDtypeS...]
    pallas_call x1 -> x2, Pallas kernels: 42.5 us -> 39 us  [ffn_forward(): pl.pallas_call(ffn_kernel, grid=(slots,), out_shape=[jax.ShapeDtypeStruct...]
  transfers between devices with their start and end apart: 20 -> 20, of which waited for: 9 -> 12; matrix products, arithmetic and copies ran while one was open for 8% -> 8% of each run, Pallas kernels for 33% -> 56%
where the time goes in v5:
time: 733 us; the launch traced here: 721 us
  Pallas kernels  558 us (76%)
  local copies, waits for them, and re-layouts  46.5 us (6%)
  other arithmetic  41.9 us (6%)
  waiting for transfers between devices  29.2 us (4%)
  starting transfers between devices  22 us (3%)
  matrix products  16 us (2%)
    pallas_call x1, Pallas kernels, dp_gather(): pl.pallas_call(functools.partial(gather_kernel, n, plan), out_shape=[jax....  166 us
    pallas_call x1, Pallas kernels, dp_reduce(): pl.pallas_call(functools.partial(reduce_kernel, n, slots), out_shape=[jax...  158 us
    pallas_call x1, Pallas kernels, front(): pl.pallas_call(functools.partial(front_kernel, n), out_shape=[shape((rows...  90.9 us
    pallas_call x2, Pallas kernels, ffn_forward(): pl.pallas_call(ffn_kernel, grid=(slots,), out_shape=[jax.ShapeDtypeStruct...  39 us
    pallas_call x1, Pallas kernels, ffn_weights(): pl.pallas_call(ffn_weights_kernel, grid=(slots,), out_shape=[jax.ShapeDty...  31.6 us
    pallas_call x2, Pallas kernels, ffn_backward(): pl.pallas_call(ffn_back_kernel, grid=(slots,), out_shape=[jax.ShapeDtypeS...  30.7 us
    pallas_call x2, Pallas kernels, ffn_input(): pl.pallas_call(ffn_input_kernel, grid=(slots,), out_shape=jax.ShapeDtypeS...  22.1 us
    pallas_call x3, Pallas kernels, attend_backward(): pl.pallas_call(attend_back_kernel, grid=(pairs,), out_shape=jax.ShapeDtyp...  19 us
  transfers between devices with their start and end apart: 20, of which 12 were waited for; matrix products, arithmetic and copies ran while one was open for 8% of the time, Pallas kernels for 56%

profile of v5, /device:TPU:27, one launch (start us, length us, event | category | flops | bytes accessed | tf_op | source)
XLA Modules:
  0.0 720.6 jit_solution(17320230838121994219)
XLA Ops:
  5.3 90.9 %shard_map.229 = (bf16[1024,384]{1,0:T(8,128)(2,1)S(1)}, bf16[1024,384]{1,0:T(8,128)(2,1)S(1)}, bf16[1024,384]{1,0:T(8,128)(2,1)S(1)}, bf16[1024,384]{1,0:T(8,12...) custom-call(bf16[1024,384]{1,0:T(8,128)(2,1)} %x_in.1, ...), custom_call_target="tpu_custom_call" | custom-call | tf_op jit(solution)/shard_map/pallas_call | solution.py:375
  101.7 2.8 fusion.34
  106.2 2.9 fusion.down_own
  109.1 19.4 %shard_map.230 = (bf16[5,2048,1024]{2,1,0:T(8,128)(2,1)}, bf16[5,2048,512]{2,1,0:T(8,128)(2,1)}, f32[1024,768]{1,0:T(8,128)}) custom-call(bf16[2048,768]{1,0:T(8,128)(2,1)} %bitcast.124, bf16[5,384,1024]{2,1,0:T(8,128)(2,1)} %get-tuple-element.77.up_own, bf16[5,384,1024]{2,1,0:T(8,128)(2,1)} %get-tuple-element.78.up_peer, ...), custom_call_target="tpu_custom_call" | custom-call | flops 12079595520 | bytes 20971520 | tf_op jit(solution)/shard_map/pallas_call | solution.py:825
  134.3 19.6 %shard_map.231 = (bf16[5,2048,1024]{2,1,0:T(8,128)(2,1)}, bf16[5,2048,512]{2,1,0:T(8,128)(2,1)}, f32[1024,768]{1,0:T(8,128)}) custom-call(bf16[2048,768]{1,0:T(8,128)(2,1)} %bitcast.125, bf16[5,384,1024]{2,1,0:T(8,128)(2,1)} %get-tuple-element.77.up_own, ...), custom_call_target="tpu_custom_call", output_to_operand_aliasing={{0}: (6, {}), {1}: (7, {})} | custom-call | flops 12079595520 | bytes 20971520 | tf_op jit(solution)/shard_map/pallas_call | solution.py:825
  154.0 2.7 slice.337
  159.4 2.5 multiply_reduce_fusion
  166.6 15.4 %shard_map.232 = (bf16[5,2048,1024]{2,1,0:T(8,128)(2,1)}, f32[1024,8]{1,0:T(8,128)}) custom-call(bf16[1024,768]{1,0:T(8,128)(2,1)} %pad_maximum_fusion.2.grads.near, bf16[5,2048,1024]{2,1,0:T(8,128)(2,1)} %get-tuple-element.92.pre, bf16[5,512,384]{2,1,0:T(8,128)(2,1)} %fusion.down_own, bf16[5,512,384]{2,1,0:T(8,128)(2,1)} %get-tuple-element.79.down_peer, ...), custom_call_target="tpu_custom_call" | custom-call | flops 8053063680 | bytes 26214400 | tf_op jit(solution)/shard_map/pallas_call | solution.py:882
  186.8 15.4 %shard_map.233 = (bf16[5,2048,1024]{2,1,0:T(8,128)(2,1)}, f32[1024,8]{1,0:T(8,128)}) custom-call(bf16[1024,768]{1,0:T(8,128)(2,1)} %copy-done.41, bf16[5,2048,1024]{2,1,0:T(8,128)(2,1)} %get-tuple-element.92.pre, bf16[5,512,384]{2,1,0:T(8,128)(2,1)} %fusion.down_own, ...), custom_call_target="tpu_custom_call", output_to_operand_aliasing={{0}: (5, {})} | custom-call | flops 8053063680 | bytes 26214400 | tf_op jit(solution)/shard_map/pallas_call | solution.py:882
  206.0 31.6 %shard_map.234 = (bf16[5,512,768]{2,1,0:T(8,128)(2,1)}, bf16[5,768,1024]{2,1,0:T(8,128)(2,1)}) custom-call(bf16[1024,768]{1,0:T(8,128)(2,1)} %pad_maximum_fusion.2.grads.near, bf16[1024,768]{1,0:T(8,128)(2,1)} %copy-done.41, bf16[2048,768]{1,0:T(8,128)(2,1)} %bitcast.126, bf16[5,2048,512]{2,1,0:T(8,128)(2,1)} %get-tuple-element.99.act, ...), custom_call_target="tpu_custom_call" | custom-call | flops 24159191040 | bytes 52428800 | tf_op jit(solution)/shard_map/pallas_call | solution.py:925
  237.6 11.0 %shard_map.235 = f32[1024,768]{1,0:T(8,128)S(1)} custom-call(bf16[5,2048,1024]{2,1,0:T(8,128)(2,1)} %get-tuple-element.108.pre_grad, bf16[5,384,1024]{2,1,0:T(8,128)(2,1)S(1)} %copy-done.2, bf16[5,384,1024]{2,1,0:T(8,128)(2,1)S(1)} %copy-done.4), custom_call_target="tpu_custom_call" | custom-call | flops 8053063680 | bytes 20971520 | tf_op jit(solution)/shard_map/pallas_call | solution.py:960
  253.3 2.8 slice_bitcast_fusion.1
  260.4 11.0 %shard_map.236 = f32[1024,768]{1,0:T(8,128)S(1)} custom-call(bf16[5,2048,1024]{2,1,0:T(8,128)(2,1)} %get-tuple-element.108.pre_grad, bf16[5,384,1024]{2,1,0:T(8,128)(2,1)S(1)} %copy-done.3, bf16[5,384,1024]{2,1,0:T(8,128)(2,1)S(1)} %copy-done.5), custom_call_target="tpu_custom_call" | custom-call | flops 8053063680 | bytes 20971520 | tf_op jit(solution)/shard_map/pallas_call | solution.py:960
  271.5 5.6 collective-permute-done.12
  289.3 10.8 %collective-permute-done.4 = f32[1024,384]{1,0:T(8,128)} collective-permute-done((f32[1024,384]{1,0:T(8,128)S(1)}, f32[1024,384]{1,0:T(8,128)}, u32[]{:S(2)}, u32[]{:S(2)}) %collective-permute-start.4) | collective-permute-done | bytes 1572896 | tf_op jit(solution)/shard_map/ppermute | solution.py:999
  300.1 2.7 broadcast_select_fusion.1
  303.5 2.5 convolution_convert_fusion.1.context_grad
  306.1 6.3 shard_map.237
  312.3 6.5 shard_map.238
  318.8 6.3 shard_map.239
  325.1 2.2 fusion.1
  330.0 3.1 convolution_convert_fusion.2
  333.0 2.7 reshape.213
  336.9 3.6 convolution_convert_fusion
  340.8 158.0 %shard_map.240 = (bf16[2,5,48,1024]{3,2,1,0:T(8,128)(2,1)S(1)}, bf16[2,5,64,384]{3,2,1,0:T(8,128)(2,1)S(1)}, bf16[192,384]{1,0:T(8,128)(2,1)S(1)}) custom-call(bf16[5,2,4,2,48,1024]{5,4,3,2,1,0:T(8,128)(2,1)} %bitcast.128, bf16[5,4,2,64,768]{4,3,2,1,0:T(8,128)(2,1)} %bitcast.136, bf16[2,4,2,192,384]{4,3,2,1,0:T(8,128)(2,1)S(1)} %bitcast.121), custom_call_target="tpu_custom_call" | custom-call | tf_op jit(solution)/shard_map/pallas_call | solution.py:649
  501.0 2.9 broadcast_select_fusion
  511.7 3.3 collective-permute-start.17
  516.4 166.4 %shard_map.241 = (bf16[4,384,2,1024]{3,2,1,0:T(2,128)(2,1)}, bf16[384,2,1024]{2,1,0:T(2,128)(2,1)}, bf16[4,2,512,384]{3,2,1,0:T(8,128)(2,1)}, bf16[2,512,384]{2,...) custom-call(bf16[4,48,2,1024]{3,2,1,0:T(2,128)(2,1)} %slice.262.refs_0_, ...), custom_call_target="tpu_custom_call" | custom-call | tf_op jit(solution)/shard_map/pallas_call | solution.py:769
  692.0 7.6 %collective-permute-start.19 = (f32[1024,384]{1,0:T(8,128)S(1)}, f32[1024,384]{1,0:T(8,128)S(1)}, u32[]{:S(2)}, u32[]{:S(2)}) collective-permute-start(f32[1024,384]{1,0:T(8,128)S(1)} %maximum_select_fusion.2), channel_id=1, source_target_pairs={{1,2},{2,1},{5,6},{6,5},{9,10},{10,9},{13,14},{14,13},{17,18},{18,... | collective-permute-start | bytes 4718600 | tf_op jit(solution)/shard_map/ppermute | solution.py:999
  703.3 3.2 convert_multiply_fusion.1
  706.5 6.6 convert_multiply_fusion
  713.1 4.6 collective-permute-done.19
  (276 shorter events, 80.5 us)
Async XLA Ops:
  4.6 91.6 %copy-start.10 = (f32[1024,128]{1,0:T(8,128)}, f32[1024,128]{1,0:T(8,128)S(1)}, u32[]{:S(2)}) copy-start(f32[1024,128]{1,0:T(8,128)S(1)} %copy.83.sine) | copy-start | bytes 1572868
  4.8 91.4 %copy-start.12 = (f32[1024,128]{1,0:T(8,128)}, f32[1024,128]{1,0:T(8,128)S(1)}, u32[]{:S(2)}) copy-start(f32[1024,128]{1,0:T(8,128)S(1)} %copy.82.cosine) | copy-start | bytes 1572868
  5.3 96.1 %copy-start.57 = (s32[2048,2]{0,1:T(2,128)S(1)}, s32[2048,2]{0,1:T(2,128)}, u32[]{:S(2)}) copy-start(s32[2048,2]{0,1:T(2,128)} %param.19) | copy-start | bytes 49156
  130.0 2.4 collective-permute-start
  134.1 19.9 %collective-permute-start.1 = (bf16[512,768]{1,0:T(8,128)(2,1)S(1)}, bf16[512,768]{1,0:T(8,128)(2,1)S(1)}, u32[]{:S(2)}, u32[]{:S(2)}) collective-permute-start(bf16[512,768]{1,0:T(8,128)(2,1)S(1)} %pad_maximum_fusion.5), channel_id=1, source_target_pairs={{0,2},{2,0},{1,3},{3,1},{4,6},{6,4},{5,7},{7,5},{8,10},{10,8},{9,1... | collective-permute-start | bytes 2359304 | tf_op jit(solution)/shard_map/ppermute | solution.py:492
  156.7 2.7 collective-permute-start.2
  157.1 1.9 collective-permute-start.5
  163.1 2.3 collective-permute-start.6
  163.6 19.1 %collective-permute-start.7 = (bf16[512,768]{1,0:T(8,128)(2,1)S(1)}, bf16[512,768]{1,0:T(8,128)(2,1)S(1)}, u32[]{:S(2)}, u32[]{:S(2)}) collective-permute-start(bf16[512,768]{1,0:T(8,128)(2,1)S(1)} %pad_maximum_fusion.6), channel_id=1, source_target_pairs={{0,2},{2,0},{1,3},{3,1},{4,6},{6,4},{5,7},{7,5},{8,10},{10,8},{9,1... | collective-permute-start | bytes 2359304 | tf_op jit(solution)/shard_map/ppermute | solution.py:492
  182.7 2.9 collective-permute-start.8
  203.4 1.3 collective-permute-start.9
  204.7 32.9 %collective-permute-start.10 = (f32[4,512]{1,0:T(4,128)S(1)}, f32[4,512]{1,0:T(4,128)S(1)}, u32[]{:S(2)}, u32[]{:S(2)}) collective-permute-start(f32[4,512]{1,0:T(4,128)S(1)} %fusion.27), channel_id=1, source_target_pairs={{0,2},{2,0},{1,3},{3,1},{4,6},{6,4},{5,7},{7,5},{8,10},{10,8},{9,1... | collective-permute-start | bytes 24584 | tf_op jit(solution)/shard_map/ppermute | solution.py:492
  205.9 31.6 %copy-start.2 = (bf16[5,384,1024]{2,1,0:T(8,128)(2,1)S(1)}, bf16[5,384,1024]{2,1,0:T(8,128)(2,1)}, u32[]{:S(2)}) copy-start(bf16[5,384,1024]{2,1,0:T(8,128)(2,1)} %get-tuple-element.77.up_own) | copy-start | bytes 11796484
  206.0 31.6 %copy-start.4 = (bf16[5,384,1024]{2,1,0:T(8,128)(2,1)S(1)}, bf16[5,384,1024]{2,1,0:T(8,128)(2,1)}, u32[]{:S(2)}) copy-start(bf16[5,384,1024]{2,1,0:T(8,128)(2,1)} %get-tuple-element.78.up_peer) | copy-start | bytes 11796484
  250.4 5.7 collective-permute-start.11
  253.3 30.2 %copy-start.55 = (f32[512]{0:T(512)}, f32[512]{0:T(512)S(1)}, u32[]{:S(2)}) copy-start(f32[512]{0:T(512)S(1)} %fusion.7) | copy-start | bytes 6148
  257.8 19.2 %collective-permute-start.12 = (bf16[512,768]{1,0:T(8,128)(2,1)S(1)}, bf16[512,768]{1,0:T(8,128)(2,1)S(1)}, u32[]{:S(2)}, u32[]{:S(2)}) collective-permute-start(bf16[512,768]{1,0:T(8,128)(2,1)S(1)} %pad_maximum_fusion.7), channel_id=1, source_target_pairs={{0,2},{2,0},{1,3},{3,1},{4,6},{6,4},{5,7},{7,5},{8,10},{10,8},{9,1... | collective-permute-start | bytes 2359304 | tf_op jit(solution)/shard_map/ppermute | solution.py:492
  259.2 18.8 %collective-permute-start.3 = (f32[512,384]{1,0:T(8,128)S(1)}, f32[512,384]{1,0:T(8,128)S(1)}, u32[]{:S(2)}, u32[]{:S(2)}) collective-permute-start(f32[512,384]{1,0:T(8,128)S(1)} %get-tuple-element.148), channel_id=1, source_target_pairs={{0,1},{1,0},{2,3},{3,2},{4,5},{5,4},{6,7},{7,6},{8,9},{9,8},{10,11... | collective-permute-start | bytes 2359304 | tf_op jit(solution)/shard_map/ppermute | solution.py:492
  277.1 3.6 collective-permute-start.13
  278.1 22.0 %collective-permute-start.4 = (f32[1024,384]{1,0:T(8,128)S(1)}, f32[1024,384]{1,0:T(8,128)}, u32[]{:S(2)}, u32[]{:S(2)}) collective-permute-start(f32[1024,384]{1,0:T(8,128)S(1)} %maximum_select_fusion), channel_id=1, source_target_pairs={{1,2},{2,1},{5,6},{6,5},{9,10},{10,9},{13,14},{14,13},{17,18},{18,... | collective-permute-start | bytes 4718600 | tf_op jit(solution)/shard_map/ppermute | solution.py:999
  283.5 19.9 %copy-start.46 = (bf16[512,768]{1,0:T(8,128)(2,1)}, bf16[512,768]{1,0:T(8,128)(2,1)S(1)}, u32[]{:S(2)}) copy-start(bf16[512,768]{1,0:T(8,128)(2,1)S(1)} %get-tuple-element.139) | copy-start | bytes 2359300
  283.5 19.9 %collective-permute-start.14 = (bf16[512,768]{1,0:T(8,128)(2,1)S(1)}, bf16[512,768]{1,0:T(8,128)(2,1)}, u32[]{:S(2)}, u32[]{:S(2)}) collective-permute-start(bf16[512,768]{1,0:T(8,128)(2,1)S(1)} %get-tuple-element.139), channel_id=1, source_target_pairs={{0,1},{1,0},{2,3},{3,2},{4,5},{5,4},{6,7},{7,6},{8,9},{9,8},{10,11... | collective-permute-start | bytes 2359304 | tf_op jit(solution)/shard_map/ppermute | solution.py:492
  288.0 14.8 %copy-start.51 = (f32[1,768]{1,0:T(1,128)}, f32[1,768]{1,0:T(1,128)S(1)}, u32[]{:S(2)}) copy-start(f32[1,768]{1,0:T(1,128)S(1)} %scatter.4) | copy-start | bytes 9220
  289.3 14.1 %copy-start.27 = (bf16[384,384]{1,0:T(8,128)(2,1)S(1)}, bf16[384,384]{1,0:T(8,128)(2,1)}, u32[]{:S(2)}) copy-start(bf16[384,384]{1,0:T(8,128)(2,1)} %copy-done.26) | copy-start | bytes 884740
  318.8 6.3 copy-start.45
  330.0 177.8 %collective-permute-start.15 = (bf16[512,768]{1,0:T(8,128)(2,1)}, bf16[512,768]{1,0:T(8,128)(2,1)S(1)}, u32[]{:S(2)}, u32[]{:S(2)}) collective-permute-start(bf16[512,768]{1,0:T(8,128)(2,1)} %fusion.14), channel_id=1, source_target_pairs={{0,1},{1,0},{2,3},{3,2},{4,5},{5,4},{6,7},{7,6},{8,9},{9,8},{10,11... | collective-permute-start | bytes 2359304 | tf_op jit(solution)/shard_map/ppermute | solution.py:492
  508.7 2.8 collective-permute-start.16
  511.7 4.1 collective-permute-start.17
  515.1 176.9 %collective-permute-start.18 = (f32[512,384]{1,0:T(8,128)S(1)}, f32[512,384]{1,0:T(8,128)S(1)}, u32[]{:S(2)}, u32[]{:S(2)}) collective-permute-start(f32[512,384]{1,0:T(8,128)S(1)} %get-tuple-element.143), channel_id=1, source_target_pairs={{0,1},{1,0},{2,3},{3,2},{4,5},{5,4},{6,7},{7,6},{8,9},{9,8},{10,11... | collective-permute-start | bytes 2359304 | tf_op jit(solution)/shard_map/ppermute | solution.py:492
  691.9 8.3 %copy-start.44 = (bf16[384,2,1024]{2,1,0:T(2,128)(2,1)S(1)}, bf16[384,2,1024]{2,1,0:T(2,128)(2,1)}, u32[]{:S(2)}) copy-start(bf16[384,2,1024]{2,1,0:T(2,128)(2,1)} %get-tuple-element.122) | copy-start | bytes 4718596
  692.0 25.7 %collective-permute-start.19 = (f32[1024,384]{1,0:T(8,128)S(1)}, f32[1024,384]{1,0:T(8,128)S(1)}, u32[]{:S(2)}, u32[]{:S(2)}) collective-permute-start(f32[1024,384]{1,0:T(8,128)S(1)} %maximum_select_fusion.2), channel_id=1, source_target_pairs={{1,2},{2,1},{5,6},{6,5},{9,10},{10,9},{13,14},{14,13},{17,18},{18,... | collective-permute-start | bytes 4718600 | tf_op jit(solution)/shard_map/ppermute | solution.py:999
  706.5 12.5 %copy-start.1 = (s32[2,1024]{1,0:T(2,128)S(1)}, s32[2,1024]{1,0:T(2,128)}, u32[]{:S(2)}) copy-start(s32[2,1024]{1,0:T(2,128)} %param.20) | copy-start | bytes 24580
  (51 other events, 123.6 us)

commit v6 on v5

--- a/solution.py
+++ b/solution.py
@@ -517,17 +517,17 @@
     pl.semaphore_wait(barrier, len(devices))
 
 
+BESIDE = 2
 AHEAD = 3
 BEHIND = 3
 
 
 def reduce_kernel(n, slots, *refs):
-    ups, down, attn, up_out, down_out, attn_out = refs[:6]
+    ups, attn, up_out, attn_out = refs[:4]
     (
-        up_keep, down_keep, attn_keep, up_x, down_x, attn_x, up_z, down_z, attn_z,
-        up_done, down_done, attn_done, attn_y,
+        up_keep, attn_keep, up_x, attn_x, up_z, attn_z, up_done, attn_done, attn_y,
         keep_sem, x_send, x_recv, z_send, z_recv, out_sem, y_send, y_recv,
-    ) = refs[6:]
+    ) = refs[4:]
     me = lax.axis_index("dp")
     row = lax.axis_index("row")
     deep = n // 2
@@ -537,18 +537,15 @@
     ahead = [lax.rem(z + k, deep) for k in range(deep)]
     greet([partner, peer] + [{"dp": 2 * ahead[k] + x} for k in range(1, deep)])
 
-    items = [("down", e) for e in range(slots)]
-    items += [("up", 2 * e + h) for e in range(slots) for h in (1, 0)]
+    items = [("up", 2 * e + h) for e in range(slots) for h in (1, 0)]
     items += [("attn", 0)]
     count = len(items)
     last = count - 1
 
     def buffers(item):
         kind, at = items[item]
-        if kind == "down":
-            return down.at[at], down_keep.at[at], down_x.at[at], down_z.at[at], down_done.at[at]
         if kind == "up":
-            return ups.at[at // 2, at % 2], up_keep.at[at], up_x.at[at], up_z.at[at], up_done.at[at]
+            return ups.at[BESIDE + at // 2, at % 2], up_keep.at[at], up_x.at[at], up_z.at[at], up_done.at[at]
         return None, attn_keep.at[:, x], attn_x, attn_z, attn_done
 
     y_first = remote(attn.at[1], attn_y, y_send.at[last], y_recv.at[last], peer)
@@ -598,7 +595,6 @@
             z_copies[item, k].wait_recv()
             total = total + arrivals[k - 1].astype(F32)
         done[...] = total.astype(BF)
-        half = down.shape[4] // 2
 
         def keep_own(source, target):
             copy = pltpu.make_async_copy(source, target, out_sem.at[item])
@@ -610,10 +606,7 @@
             copy.start()
             y_copies.append(copy)
 
-        if kind == "down":
-            keep_own(done.at[:, :half], down_out.at[0, at])
-            give_peer(done.at[:, half:], down_out.at[1, at])
-        elif kind == "attn":
+        if kind == "attn":
             keep_own(done, attn_out)
         elif at % 2 == 0:
             keep_own(done, up_out.at[0, at // 2])
@@ -636,37 +629,31 @@
         copy.wait_send()
 
 
-def dp_reduce(up_grads, down_grad, attn_grad):
+def dp_reduce(up_grads, attn_grad):
     n = lax.axis_size("dp")
     deep = n // 2
-    slots = up_grads.shape[0]
-    up_tail, down_tail, attn_tail = up_grads.shape[4:], down_grad.shape[3:], attn_grad.shape[3:]
+    slots = up_grads.shape[0] - BESIDE
+    up_tail, attn_tail = up_grads.shape[4:], attn_grad.shape[3:]
     sems = pltpu.SemaphoreType.DMA
-    count = 3 * slots + 1
+    count = 2 * slots + 1
     vmem = lambda *shape: pltpu.VMEM(shape, BF)
-    half = down_tail[1] // 2
     any_spec = pl.BlockSpec(memory_space=pl.ANY)
     return pl.pallas_call(
         functools.partial(reduce_kernel, n, slots),
         out_shape=[
             jax.ShapeDtypeStruct((2, slots) + up_tail, BF),
-            jax.ShapeDtypeStruct((2, slots, down_tail[0], half), BF),
             jax.ShapeDtypeStruct(attn_tail, BF),
         ],
-        in_specs=[any_spec] * 3,
-        out_specs=[any_spec] * 3,
+        in_specs=[any_spec] * 2,
+        out_specs=[any_spec] * 2,
         scratch_shapes=[
             vmem(2 * slots, deep, *up_tail),
-            vmem(slots, deep, *down_tail),
             vmem(deep, 2, *attn_tail),
             vmem(2 * slots, deep, *up_tail),
-            vmem(slots, deep, *down_tail),
             vmem(deep, *attn_tail),
             vmem(2 * slots, deep - 1, *up_tail),
-            vmem(slots, deep - 1, *down_tail),
             vmem(deep - 1, *attn_tail),
             vmem(2 * slots, *up_tail),
-            vmem(slots, *down_tail),
             vmem(*attn_tail),
             vmem(deep, 2, *attn_tail),
             sems((count,)),
@@ -681,7 +668,30 @@
         compiler_params=pltpu.CompilerParams(
             collective_id=1, has_side_effects=True, vmem_limit_bytes=48 << 20
         ),
-    )(up_grads, down_grad, attn_grad)
+    )(up_grads, attn_grad)
+
+
+def pick(values, index, axis):
+    return lax.dynamic_index_in_dim(values, index, axis, keepdims=False)
+
+
+def x_halves(values, axis):
+    shape, x = values.shape, lax.axis_index("dp") % 2
+    values = values.reshape(shape[:axis] + (shape[axis] // 2, 2) + shape[axis + 1 :])
+    return pick(values, x, axis + 1), pick(values, 1 - x, axis + 1)
+
+
+def along_dp(values, step):
+    return lax.ppermute(values, "dp", [(i, i ^ step) for i in range(lax.axis_size("dp"))])
+
+
+def add_low(*terms):
+    return sum(term.astype(F32) for term in terms).astype(BF)
+
+
+def z_blocks(values, axis):
+    z = lax.axis_index("dp") // 2
+    return [pick(values, z ^ k, axis) for k in range(values.shape[axis])]
 
 
 def order_pair(first_is_own, own, other, axis):
@@ -905,11 +915,32 @@
     )(grads, pre, down_own, down_peer, mix, *filled)
 
 
-def ffn_weights_kernel(near, far, tokens, act, pre_grad, down_grad, up_grad):
+def ffn_down_kernel(near, far, act, down_grad):
     size = near.shape[0]
     total = lax.dot_general(act[0, :size], near[...], TN, preferred_element_type=F32)
     total = total + lax.dot_general(act[0, size:], far[...], TN, preferred_element_type=F32)
     down_grad[0] = total.astype(BF)
+
+
+def ffn_down(near, far, act):
+    slots, rows, width = act.shape
+    depth = near.shape[1]
+    per_slot = lambda *shape: pl.BlockSpec((1,) + shape, lambda e: (e, 0, 0))
+    whole = lambda *shape: pl.BlockSpec(shape, lambda e: (0, 0), pipeline_mode=pl.Buffered(1))
+    return pl.pallas_call(
+        ffn_down_kernel,
+        grid=(slots,),
+        out_shape=jax.ShapeDtypeStruct((slots, width, depth), BF),
+        in_specs=[whole(rows // 2, depth), whole(rows // 2, depth), per_slot(rows, width)],
+        out_specs=per_slot(width, depth),
+        compiler_params=pltpu.CompilerParams(vmem_limit_bytes=40 << 20),
+        cost_estimate=pl.CostEstimate(
+            flops=2 * slots * rows * depth * width, bytes_accessed=20 << 20, transcendentals=0
+        ),
+    )(near, far, act)
+
+
+def ffn_up_kernel(tokens, pre_grad, up_grad):
     for tile in range(tokens.shape[1] // 256):
         columns = slice(tile * 256, (tile + 1) * 256)
         up_grad[0, columns] = lax.dot_general(
@@ -917,31 +948,24 @@
         ).astype(BF)
 
 
-def ffn_weights(near, far, tokens, act, pre_grad):
+def ffn_up(tokens, pre_grad):
     slots, rows, width = pre_grad.shape
     depth = tokens.shape[1]
     per_slot = lambda *shape: pl.BlockSpec((1,) + shape, lambda e: (e, 0, 0))
-    whole = lambda *shape: pl.BlockSpec(shape, lambda e: (0, 0), pipeline_mode=pl.Buffered(1))
     return pl.pallas_call(
-        ffn_weights_kernel,
+        ffn_up_kernel,
         grid=(slots,),
-        out_shape=[
-            jax.ShapeDtypeStruct((slots, width // 2, depth), BF),
-            jax.ShapeDtypeStruct((slots, depth, width), BF),
-        ],
+        out_shape=jax.ShapeDtypeStruct((slots, depth, width), BF),
         in_specs=[
-            whole(rows // 2, depth),
-            whole(rows // 2, depth),
-            whole(rows, depth),
-            per_slot(rows, width // 2),
+            pl.BlockSpec((rows, depth), lambda e: (0, 0), pipeline_mode=pl.Buffered(1)),
             per_slot(rows, width),
         ],
-        out_specs=[per_slot(width // 2, depth), per_slot(depth, width)],
-        compiler_params=pltpu.CompilerParams(vmem_limit_bytes=56 << 20),
+        out_specs=per_slot(depth, width),
+        compiler_params=pltpu.CompilerParams(vmem_limit_bytes=40 << 20),
         cost_estimate=pl.CostEstimate(
-            flops=3 * slots * rows * depth * width, bytes_accessed=50 << 20, transcendentals=0
+            flops=2 * slots * rows * depth * width, bytes_accessed=35 << 20, transcendentals=0
         ),
-    )(near, far, tokens, act, pre_grad)
+    )(tokens, pre_grad)
 
 
 def ffn_input_kernel(pre_grad, up_own, up_peer, out):
@@ -1091,16 +1115,36 @@
     pre_grad, near_sums = ffn_backward(near, pre, down_own, down_peer, mix, 0, 2)
     pre_grad, far = lax.optimization_barrier((pre_grad, far))
     far = jnp.concatenate([far, swap(far, "col")])
+    owner_f = quarter // n_dp
+    owner_d = half // n_dp
+    deep = n_dp // 2
+    down_grad = ffn_down(near, far, act)
+    down_keep, down_send = x_halves(down_grad.reshape(slots, n_dp, owner_f, D), 1)
+    pre_grad, far, down_send = lax.optimization_barrier((pre_grad, far, down_send))
+    first_recv = along_dp(down_send[:3], 1)
+    second_recv = along_dp(down_send[3:], 1)
     pre_grad, far_sums = ffn_backward(far, pre, down_own, down_peer, mix, 1, 2, (pre_grad,))
     gate_parts = jnp.concatenate([near_sums, far_sums])[:, 1 : E + 1].T.reshape(E, 4, part)
     recv = swap(jnp.stack([gate_parts[:, 1], gate_parts[:, 3]]), "col")
     gate_grad = gate_parts[:, 0] + recv[0] + swap(gate_parts[:, 2] + recv[1], "row")
-    down_grad, up_grad = ffn_weights(near, far, tokens, act, pre_grad)
-    pre_grad, gate_grad, up_grad = lax.optimization_barrier((pre_grad, gate_grad, up_grad))
+    up_grad = ffn_up(tokens, pre_grad)
+    up_grad = up_grad.reshape(slots, 2, n_dp, owner_d, 2 * quarter)
+    up_keep, up_send = x_halves(up_grad[:BESIDE], 2)
+    pre_grad, gate_grad, up_send, first_recv = lax.optimization_barrier(
+        (pre_grad, gate_grad, up_send, first_recv)
+    )
     far = ffn_input(pre_grad, up_own, up_peer, 1, 2)
     (normed_ffn_grad,) = collect_tokens(
         far, lambda operand: (ffn_input(operand, up_own, up_peer, 0, 2),), pre_grad
     )
+    normed_ffn_grad, second_recv = lax.optimization_barrier((normed_ffn_grad, second_recv))
+    down_recv = jnp.concatenate([first_recv, second_recv])
+    down_own_sum, *down_sends = z_blocks(add_low(down_keep, down_recv), 1)
+    normed_ffn_grad, down_sends, up_send = lax.optimization_barrier(
+        (normed_ffn_grad, down_sends, up_send)
+    )
+    up_recv = along_dp(up_send, 1)
+    down_recvs = [along_dp(block, 2 * k + 2) for k, block in enumerate(down_sends)]
     mix_own = mixing[:part].T
     centre = jnp.sum(mix_own * gate_grad, axis=0, keepdims=True)
     logit_grad = (mix_own * (gate_grad - centre)).T.astype(BF)
@@ -1126,6 +1170,12 @@
         ],
         axis=2,
     )
+    qkv_grad, down_recvs, up_recv = lax.optimization_barrier((qkv_grad, down_recvs, up_recv))
+    up_own_sum, *up_sends = z_blocks(add_low(up_keep, up_recv), 2)
+    qkv_grad, up_sends = lax.optimization_barrier((qkv_grad, up_sends))
+    up_recvs = [along_dp(block, 2 * k + 2) for k, block in enumerate(up_sends)]
+    down_sum = add_low(down_own_sum, *down_recvs)
+    down_peer_sum = swap(down_sum[:, :, half:], "row")
     w_qkv_grad = jnp.einsum(
         "td,kte->dke", normed_attn, qkv_grad, preferred_element_type=F32
     ).astype(BF)
@@ -1137,9 +1187,6 @@
     input_back, gain_attn_grad = norm_backward(x_own, rstd_attn, gain_a, normed_attn_grad)
     input_grad = hidden_grad + input_back
 
-    owner_f = quarter // n_dp
-    owner_d = half // n_dp
-    deep = n_dp // 2
     grad_pair = jnp.concatenate(
         [
             w_qkv_grad.reshape(2, n_dp, owner_d, 3, half),
@@ -1147,13 +1194,16 @@
         ],
         axis=3,
     ).transpose(0, 1, 3, 2, 4)
-    up_pair, down_pair, attn_piece = dp_reduce(
+    up_pair, attn_piece = dp_reduce(
         up_grad.reshape(slots, 2, deep, 2, owner_d, 2 * quarter),
-        down_grad.reshape(slots, deep, 2, owner_f, D),
         grad_pair.reshape(2, deep, 2, 4 * owner_d, half),
     )
+    up_pair, attn_piece, up_recvs = lax.optimization_barrier((up_pair, attn_piece, up_recvs))
+    up_sum = add_low(up_own_sum, *up_recvs)
+    up_peer_sum = swap(up_sum[:, 1], "row")
     attn_piece = attn_piece.reshape(4, owner_d, half)
-    down_piece = jnp.where(r == 0, down_pair, down_pair[::-1]).swapaxes(0, 1)
+    down_piece = order_pair(r == 0, down_sum[:, None, :, :half], down_peer_sum[:, None], 1)
+    up_pair = jnp.concatenate([jnp.stack([up_sum[:, 0], up_peer_sum]), up_pair], axis=1)
     up_pair = up_pair.reshape(2, slots, owner_d, 2, quarter)
     up_piece = order_pair(r == 0, up_pair[0], up_pair[1], 3)
 

time: 733 us -> 724 us (0.988)
  Pallas kernels: 558 us -> 494 us
  starting transfers between devices: 22 us -> 44.7 us
  local copies, waits for them, and re-layouts: 46.5 us -> 59.6 us
  other arithmetic: 41.9 us -> 54 us
    pallas_call x1, Pallas kernels: 158 us -> 96 us  [dp_reduce(): pl.pallas_call(functools.partial(reduce_kernel, n, slots), out_shape=[jax...]
    ppermute x0 -> x9, starting transfers between devices: none -> 17.5 us  [along_dp(): lax.ppermute(values, 'dp', [(i, i ^ step) for i in range(lax.axis_size('d...]
    ppermute x0 -> x9, waiting for transfers between devices: none -> 15.2 us  [along_dp(): lax.ppermute(values, 'dp', [(i, i ^ step) for i in range(lax.axis_size('d...]
    ppermute x2, waiting for transfers between devices: 15.4 us -> 4.64 us  [from_sequence(): moved = lax.ppermute(whole, ('row', 'col'), [(1, 2), (2, 1)])]
    ppermute x18 -> x20, starting transfers between devices: 12.3 us -> 17.6 us  [swap(): return lax.ppermute(values, axis, [(0, 1), (1, 0)])]
    ppermute x18 -> x20, waiting for transfers between devices: 13.8 us -> 15.9 us  [swap(): return lax.ppermute(values, axis, [(0, 1), (1, 0)])]
    unnamed x127 -> x141, local copies, waits for them, and re-layouts: 15.1 us -> 16.2 us
    pallas_call x1 -> x2, Pallas kernels: 31.6 us -> 30.7 us  [the longest x1 19.9 us: ffn_up(): pl.pallas_call(ffn_up_kernel, grid=(slots,), out_shape=jax.ShapeDtypeStru...]
  transfers between devices with their start and end apart: 20 -> 31, of which waited for: 12 -> 15; matrix products, arithmetic and copies ran while one was open for 8% -> 11% of each run, Pallas kernels for 56% -> 49%
where the time goes in v6:
time: 724 us; the launch traced here: 711 us
  Pallas kernels  494 us (68%)
  local copies, waits for them, and re-layouts  59.6 us (8%)
  other arithmetic  54 us (7%)
  starting transfers between devices  44.7 us (6%)
  waiting for transfers between devices  35.7 us (5%)
  matrix products  15 us (2%)
  between operations  7.39 us (1%)
    pallas_call x1, Pallas kernels, dp_gather(): pl.pallas_call(functools.partial(gather_kernel, n, plan), out_shape=[jax....  165 us
    pallas_call x1, Pallas kernels, dp_reduce(): pl.pallas_call(functools.partial(reduce_kernel, n, slots), out_shape=[jax...  96 us
    pallas_call x1, Pallas kernels, front(): pl.pallas_call(functools.partial(front_kernel, n), out_shape=[shape((rows...  91.1 us
    pallas_call x2, Pallas kernels, ffn_forward(): pl.pallas_call(ffn_kernel, grid=(slots,), out_shape=[jax.ShapeDtypeStruct...  39 us
    pallas_call x2, Pallas kernels, ffn_backward(): pl.pallas_call(ffn_back_kernel, grid=(slots,), out_shape=[jax.ShapeDtypeS...  30.9 us
    pallas_call x2, Pallas kernels, ffn_input(): pl.pallas_call(ffn_input_kernel, grid=(slots,), out_shape=jax.ShapeDtypeS...  22.5 us
    pallas_call x1, Pallas kernels, ffn_up(): pl.pallas_call(ffn_up_kernel, grid=(slots,), out_shape=jax.ShapeDtypeStru...  19.9 us
    pallas_call x3, Pallas kernels, attend_backward(): pl.pallas_call(attend_back_kernel, grid=(pairs,), out_shape=jax.ShapeDtyp...  19 us
  transfers between devices with their start and end apart: 31, of which 15 were waited for; matrix products, arithmetic and copies ran while one was open for 11% of the time, Pallas kernels for 49%

profile of v6, /device:TPU:27, one launch (start us, length us, event | category | flops | bytes accessed | tf_op | source)
XLA Modules:
  0.0 710.8 jit_solution(17421996054231326072)
XLA Ops:
  5.3 91.1 %shard_map.229 = (bf16[1024,384]{1,0:T(8,128)(2,1)S(1)}, bf16[1024,384]{1,0:T(8,128)(2,1)S(1)}, bf16[1024,384]{1,0:T(8,128)(2,1)S(1)}, bf16[1024,384]{1,0:T(8,12...) custom-call(bf16[1024,384]{1,0:T(8,128)(2,1)} %x_in.1, ...), custom_call_target="tpu_custom_call" | custom-call | tf_op jit(solution)/shard_map/pallas_call | solution.py:375
  102.0 2.9 fusion.41
  109.6 19.4 %shard_map.230 = (bf16[5,2048,1024]{2,1,0:T(8,128)(2,1)}, bf16[5,2048,512]{2,1,0:T(8,128)(2,1)}, f32[1024,768]{1,0:T(8,128)}) custom-call(bf16[2048,768]{1,0:T(8,128)(2,1)} %bitcast.165, bf16[5,384,1024]{2,1,0:T(8,128)(2,1)} %get-tuple-element.99.up_own, bf16[5,384,1024]{2,1,0:T(8,128)(2,1)} %get-tuple-element.100.up_peer, ...), custom_call_target="tpu_custom_call" | custom-call | flops 12079595520 | bytes 20971520 | tf_op jit(solution)/shard_map/pallas_call | solution.py:835
  134.8 19.6 %shard_map.231 = (bf16[5,2048,1024]{2,1,0:T(8,128)(2,1)}, bf16[5,2048,512]{2,1,0:T(8,128)(2,1)}, f32[1024,768]{1,0:T(8,128)}) custom-call(bf16[2048,768]{1,0:T(8,128)(2,1)} %bitcast.166, bf16[5,384,1024]{2,1,0:T(8,128)(2,1)} %get-tuple-element.99.up_own, ...), custom_call_target="tpu_custom_call", output_to_operand_aliasing={{0}: (6, {}), {1}: (7, {})} | custom-call | flops 12079595520 | bytes 20971520 | tf_op jit(solution)/shard_map/pallas_call | solution.py:835
  159.7 2.9 multiply_reduce_fusion
  167.6 15.3 %shard_map.232 = (bf16[5,2048,1024]{2,1,0:T(8,128)(2,1)}, f32[1024,8]{1,0:T(8,128)}) custom-call(bf16[1024,768]{1,0:T(8,128)(2,1)} %pad_maximum_fusion.2.grads.near, bf16[5,2048,1024]{2,1,0:T(8,128)(2,1)} %get-tuple-element.114.pre, bf16[5,512,384]{2,1,0:T(8,128)(2,1)} %fusion.2.down_own, bf16[5,512,384]{2,1,0:T(8,128)(2,1)} %get-tuple-element.101.down_peer, ...), custom_call_target="tpu_custom_call" | custom-call | flops 8053063680 | bytes 26214400 | tf_op jit(solution)/shard_map/pallas_call | solution.py:892
  187.2 10.8 %shard_map.233 = bf16[5,512,768]{2,1,0:T(8,128)(2,1)S(1)} custom-call(bf16[1024,768]{1,0:T(8,128)(2,1)S(1)} %copy-done.15, bf16[1024,768]{1,0:T(8,128)(2,1)S(1)} %constant_dynamic-update-slice_fusion.far.grads, bf16[5,2048,512]{2,1,0:T(8,128)(2,1)} %get-tuple-element.118.act), custom_call_target="tpu_custom_call" | custom-call | flops 8053063680 | bytes 20971520 | tf_op jit(solution)/shard_map/pallas_call | solution.py:930
  201.2 15.5 %shard_map.234 = (bf16[5,2048,1024]{2,1,0:T(8,128)(2,1)}, f32[1024,8]{1,0:T(8,128)}) custom-call(bf16[1024,768]{1,0:T(8,128)(2,1)} %copy-done.8, bf16[5,2048,1024]{2,1,0:T(8,128)(2,1)} %get-tuple-element.114.pre, bf16[5,512,384]{2,1,0:T(8,128)(2,1)} %fusion.2.down_own, ...), custom_call_target="tpu_custom_call", output_to_operand_aliasing={{0}: (5, {})} | custom-call | flops 8053063680 | bytes 26214400 | tf_op jit(solution)/shard_map/pallas_call | solution.py:892
  220.9 19.9 %shard_map.235 = bf16[5,768,1024]{2,1,0:T(8,128)(2,1)S(1)} custom-call(bf16[2048,768]{1,0:T(8,128)(2,1)S(1)} %bitcast.167, bf16[5,2048,1024]{2,1,0:T(8,128)(2,1)} %get-tuple-element.129.pre_grad), custom_call_target="tpu_custom_call" | custom-call | flops 16106127360 | bytes 36700160 | tf_op jit(solution)/shard_map/pallas_call | solution.py:955
  248.9 11.3 %shard_map.236 = f32[1024,768]{1,0:T(8,128)S(1)} custom-call(bf16[5,2048,1024]{2,1,0:T(8,128)(2,1)} %get-tuple-element.129.pre_grad, bf16[5,384,1024]{2,1,0:T(8,128)(2,1)S(1)} %copy-done.2, bf16[5,384,1024]{2,1,0:T(8,128)(2,1)S(1)} %copy-done.3), custom_call_target="tpu_custom_call" | custom-call | flops 8053063680 | bytes 20971520 | tf_op jit(solution)/shard_map/pallas_call | solution.py:984
  267.2 11.3 %shard_map.237 = f32[1024,768]{1,0:T(8,128)S(1)} custom-call(bf16[5,2048,1024]{2,1,0:T(8,128)(2,1)} %get-tuple-element.129.pre_grad, bf16[5,384,1024]{2,1,0:T(8,128)(2,1)S(1)} %copy-done.2, bf16[5,384,1024]{2,1,0:T(8,128)(2,1)S(1)} %copy-done.3), custom_call_target="tpu_custom_call" | custom-call | flops 8053063680 | bytes 20971520 | tf_op jit(solution)/shard_map/pallas_call | solution.py:984
  278.5 4.3 collective-permute-done.13
  290.1 2.8 maximum_select_fusion
  292.9 3.5 collective-permute-start.4
  298.2 10.7 %collective-permute-done.15 = bf16[2,4,64,768]{3,2,0,1:T(8,128)(2,1)S(1)} collective-permute-done((bf16[2,4,64,768]{3,2,0,1:T(8,128)(2,1)S(1)}, bf16[2,4,64,768]{3,2,0,1:T(8,128)(2,1)S(1)}, u32[]{:S(2)}, u32[]{:S(2)}) %collective-permute-start.15) | collective-permute-done | bytes 786464 | tf_op jit(solution)/shard_map/ppermute | solution.py:685
  320.3 2.8 broadcast_select_fusion.1
  327.3 3.0 convolution_convert_fusion.1.context_grad
  330.4 6.3 shard_map.238
  336.6 6.4 shard_map.239
  343.1 6.3 shard_map.240
  349.4 3.6 convolution_convert_fusion.2
  355.4 3.9 collective-permute-done.18
  371.8 9.8 %collective-permute-start.21 = (bf16[2,2,48,1024]{3,2,0,1:T(8,128)(2,1)S(1)}, bf16[2,2,48,1024]{3,2,0,1:T(8,128)(2,1)S(1)}, u32[]{:S(2)}, u32[]{:S(2)}) collective-permute-start(bf16[2,2,48,1024]{3,2,0,1:T(8,128)(2,1)S(1)} %get-tuple-element.151), channel_id=1, source_target_pairs={{0,8},{4,12},{8,0},{12,4},{16,24},{20,28},{24,16},{28,20},{1,9},{5... | collective-permute-start | bytes 1179656 | tf_op jit(solution)/shard_map/ppermute | solution.py:685
  386.3 96.0 %shard_map.241 = (bf16[2,3,48,1024]{3,2,1,0:T(8,128)(2,1)S(1)}, bf16[192,384]{1,0:T(8,128)(2,1)S(1)}) custom-call(bf16[5,2,4,2,48,1024]{5,4,3,2,1,0:T(8,128)(2,1)} %bitcast.168, bf16[2,4,2,192,384]{4,3,2,1,0:T(8,128)(2,1)S(1)} %bitcast.169), custom_call_target="tpu_custom_call" | custom-call | tf_op jit(solution)/shard_map/pallas_call | solution.py:641
  484.4 4.1 collective-permute-done.24
  494.0 3.2 broadcast_select_fusion
  504.3 3.6 collective-permute-start.28
  509.4 165.2 %shard_map.242 = (bf16[4,384,2,1024]{3,2,1,0:T(2,128)(2,1)}, bf16[384,2,1024]{2,1,0:T(2,128)(2,1)}, bf16[4,2,512,384]{3,2,1,0:T(8,128)(2,1)}, bf16[2,512,384]{2,...) custom-call(bf16[4,48,2,1024]{3,2,1,0:T(2,128)(2,1)} %slice.296.refs_0_, ...), custom_call_target="tpu_custom_call" | custom-call | tf_op jit(solution)/shard_map/pallas_call | solution.py:779
  683.8 6.1 collective-permute-start.30
  693.5 3.2 convert_multiply_fusion.1
  696.7 6.6 convert_multiply_fusion
  703.3 4.6 collective-permute-done.30
  (329 shorter events, 127.2 us)
Async XLA Ops:
  5.3 96.3 %copy-start.64 = (s32[2048,2]{0,1:T(2,128)S(1)}, s32[2048,2]{0,1:T(2,128)}, u32[]{:S(2)}) copy-start(s32[2048,2]{0,1:T(2,128)} %param.19) | copy-start | bytes 49156
  130.5 2.4 collective-permute-start
  134.6 19.9 %collective-permute-start.1 = (bf16[512,768]{1,0:T(8,128)(2,1)S(1)}, bf16[512,768]{1,0:T(8,128)(2,1)S(1)}, u32[]{:S(2)}, u32[]{:S(2)}) collective-permute-start(bf16[512,768]{1,0:T(8,128)(2,1)S(1)} %pad_maximum_fusion.4), channel_id=1, source_target_pairs={{0,2},{2,0},{1,3},{3,1},{4,6},{6,4},{5,7},{7,5},{8,10},{10,8},{9,1... | collective-permute-start | bytes 2359304 | tf_op jit(solution)/shard_map/ppermute | solution.py:492
  157.0 2.7 collective-permute-start.2
  157.5 1.9 collective-permute-start.5
  164.0 2.3 collective-permute-start.6
  164.6 19.1 %collective-permute-start.7 = (bf16[512,768]{1,0:T(8,128)(2,1)S(1)}, bf16[512,768]{1,0:T(8,128)(2,1)S(1)}, u32[]{:S(2)}, u32[]{:S(2)}) collective-permute-start(bf16[512,768]{1,0:T(8,128)(2,1)S(1)} %pad_maximum_fusion.5), channel_id=1, source_target_pairs={{0,2},{2,0},{1,3},{3,1},{4,6},{6,4},{5,7},{7,5},{8,10},{10,8},{9,1... | collective-permute-start | bytes 2359304 | tf_op jit(solution)/shard_map/ppermute | solution.py:492
  183.6 2.9 collective-permute-start.8
  218.0 23.1 %collective-permute-start.9 = (f32[2,4,512]{2,1,0:T(4,128)S(1)}, f32[2,4,512]{2,1,0:T(4,128)S(1)}, u32[]{:S(2)}, u32[]{:S(2)}) collective-permute-start(f32[2,4,512]{2,1,0:T(4,128)S(1)} %pad_maximum_fusion.12), channel_id=1, source_target_pairs={{0,1},{1,0},{2,3},{3,2},{4,5},{5,4},{6,7},{7,6},{8,9},{9,8},{10,11... | collective-permute-start | bytes 49160 | tf_op jit(solution)/shard_map/ppermute | solution.py:492
  219.7 27.4 %collective-permute-start.11 = (bf16[3,4,64,768]{3,2,0,1:T(8,128)(2,1)S(1)}, bf16[3,4,64,768]{3,2,0,1:T(8,128)(2,1)S(1)}, u32[]{:S(2)}, u32[]{:S(2)}) collective-permute-start(bf16[3,4,64,768]{3,2,0,1:T(8,128)(2,1)S(1)} %slice.230), channel_id=1, source_target_pairs={{0,4},{4,0},{8,12},{12,8},{16,20},{20,16},{24,28},{28,24},{1,5},{5... | collective-permute-start | bytes 3538952 | tf_op jit(solution)/shard_map/ppermute | solution.py:685
  241.1 5.7 collective-permute-start.10
  260.3 3.3 collective-permute-start.12
  264.0 18.9 %collective-permute-start.13 = (bf16[512,768]{1,0:T(8,128)(2,1)S(1)}, bf16[512,768]{1,0:T(8,128)(2,1)S(1)}, u32[]{:S(2)}, u32[]{:S(2)}) collective-permute-start(bf16[512,768]{1,0:T(8,128)(2,1)S(1)} %pad_maximum_fusion.6), channel_id=1, source_target_pairs={{0,2},{2,0},{1,3},{3,1},{4,6},{6,4},{5,7},{7,5},{8,10},{10,8},{9,1... | collective-permute-start | bytes 2359304 | tf_op jit(solution)/shard_map/ppermute | solution.py:492
  266.7 23.4 %collective-permute-start.3 = (f32[512,384]{1,0:T(8,128)}, f32[512,384]{1,0:T(8,128)}, u32[]{:S(2)}, u32[]{:S(2)}) collective-permute-start(f32[512,384]{1,0:T(8,128)} %get-tuple-element.201), channel_id=1, source_target_pairs={{0,1},{1,0},{2,3},{3,2},{4,5},{5,4},{6,7},{7,6},{8,9},{9,8},{10,11... | collective-permute-start | bytes 2359304 | tf_op jit(solution)/shard_map/ppermute | solution.py:492
  284.0 12.5 %collective-permute-start.14 = (bf16[512,768]{1,0:T(8,128)(2,1)}, bf16[512,768]{1,0:T(8,128)(2,1)}, u32[]{:S(2)}, u32[]{:S(2)}) collective-permute-start(bf16[512,768]{1,0:T(8,128)(2,1)} %slice.374), channel_id=1, source_target_pairs={{0,1},{1,0},{2,3},{3,2},{4,5},{5,4},{6,7},{7,6},{8,9},{9,8},{10,11... | collective-permute-start | bytes 2359304 | tf_op jit(solution)/shard_map/ppermute | solution.py:492
  289.6 19.2 %collective-permute-start.15 = (bf16[2,4,64,768]{3,2,0,1:T(8,128)(2,1)S(1)}, bf16[2,4,64,768]{3,2,0,1:T(8,128)(2,1)S(1)}, u32[]{:S(2)}, u32[]{:S(2)}) collective-permute-start(bf16[2,4,64,768]{3,2,0,1:T(8,128)(2,1)S(1)} %slice.237), channel_id=1, source_target_pairs={{0,4},{4,0},{8,12},{12,8},{16,20},{20,16},{24,28},{28,24},{1,5},{5... | collective-permute-start | bytes 2359304 | tf_op jit(solution)/shard_map/ppermute | solution.py:685
  292.9 27.3 %collective-permute-start.4 = (f32[1024,384]{1,0:T(8,128)}, f32[1024,384]{1,0:T(8,128)}, u32[]{:S(2)}, u32[]{:S(2)}) collective-permute-start(f32[1024,384]{1,0:T(8,128)} %maximum_select_fusion), channel_id=1, source_target_pairs={{1,2},{2,1},{5,6},{6,5},{9,10},{10,9},{13,14},{14,13},{17,18},{18,... | collective-permute-start | bytes 4718600 | tf_op jit(solution)/shard_map/ppermute | solution.py:1023
  315.7 11.6 %collective-permute-start.16 = (bf16[512,768]{1,0:T(8,128)(2,1)}, bf16[512,768]{1,0:T(8,128)(2,1)}, u32[]{:S(2)}, u32[]{:S(2)}) collective-permute-start(bf16[512,768]{1,0:T(8,128)(2,1)} %get-tuple-element.183), channel_id=1, source_target_pairs={{0,1},{1,0},{2,3},{3,2},{4,5},{5,4},{6,7},{7,6},{8,9},{9,8},{10,11... | collective-permute-start | bytes 2359304 | tf_op jit(solution)/shard_map/ppermute | solution.py:492
  323.3 36.4 %collective-permute-start.20 = (bf16[2,2,4,48,1024]{4,3,0,1,2:T(8,128)(2,1)}, bf16[2,2,4,48,1024]{4,3,0,1,2:T(8,128)(2,1)}, u32[]{:S(2)}, u32[]{:S(2)}) collective-permute-start(bf16[2,2,4,48,1024]{4,3,0,1,2:T(8,128)(2,1)} %bitcast.157), channel_id=1, source_target_pairs={{0,4},{4,0},{8,12},{12,8},{16,20},{20,16},{24,28},{28,24},{1,5},{5... | collective-permute-start | bytes 4718600 | tf_op jit(solution)/shard_map/ppermute | solution.py:685
  323.7 31.7 %collective-permute-start.17 = (bf16[5,64,768]{2,1,0:T(8,128)(2,1)}, bf16[5,64,768]{2,1,0:T(8,128)(2,1)}, u32[]{:S(2)}, u32[]{:S(2)}) collective-permute-start(bf16[5,64,768]{2,1,0:T(8,128)(2,1)} %get-tuple-element.140), channel_id=1, source_target_pairs={{0,8},{4,12},{8,0},{12,4},{16,24},{20,28},{24,16},{28,20},{1,9},{5... | collective-permute-start | bytes 1474568 | tf_op jit(solution)/shard_map/ppermute | solution.py:685
  324.8 34.6 %collective-permute-start.18 = (bf16[5,64,768]{2,1,0:T(8,128)(2,1)}, bf16[5,64,768]{2,1,0:T(8,128)(2,1)}, u32[]{:S(2)}, u32[]{:S(2)}) collective-permute-start(bf16[5,64,768]{2,1,0:T(8,128)(2,1)} %get-tuple-element.141), channel_id=1, source_target_pairs={{0,16},{4,20},{8,24},{12,28},{16,0},{20,4},{24,8},{28,12},{1,17},{... | collective-permute-start | bytes 1474568 | tf_op jit(solution)/shard_map/ppermute | solution.py:685
  324.8 34.5 %collective-permute-start.19 = (bf16[5,64,768]{2,1,0:T(8,128)(2,1)}, bf16[5,64,768]{2,1,0:T(8,128)(2,1)}, u32[]{:S(2)}, u32[]{:S(2)}) collective-permute-start(bf16[5,64,768]{2,1,0:T(8,128)(2,1)} %get-tuple-element.142), channel_id=1, source_target_pairs={{0,24},{4,28},{8,16},{12,20},{16,8},{20,12},{24,0},{28,4},{1,25},{... | collective-permute-start | bytes 1474568 | tf_op jit(solution)/shard_map/ppermute | solution.py:685
  366.4 133.0 %collective-permute-start.26 = (bf16[512,768]{1,0:T(8,128)(2,1)}, bf16[512,768]{1,0:T(8,128)(2,1)}, u32[]{:S(2)}, u32[]{:S(2)}) collective-permute-start(bf16[512,768]{1,0:T(8,128)(2,1)} %fusion.19), channel_id=1, source_target_pairs={{0,1},{1,0},{2,3},{3,2},{4,5},{5,4},{6,7},{7,6},{8,9},{9,8},{10,11... | collective-permute-start | bytes 2359304 | tf_op jit(solution)/shard_map/ppermute | solution.py:492
  370.3 112.1 %collective-permute-start.25 = (bf16[5,64,384]{2,1,0:T(8,128)(2,1)S(1)}, bf16[5,64,384]{2,1,0:T(8,128)(2,1)S(1)}, u32[]{:S(2)}, u32[]{:S(2)}) collective-permute-start(bf16[5,64,384]{2,1,0:T(8,128)(2,1)S(1)} %get-tuple-element.215), channel_id=1, source_target_pairs={{0,2},{2,0},{1,3},{3,1},{4,6},{6,4},{5,7},{7,5},{8,10},{10,8},{9,1... | collective-permute-start | bytes 737288 | tf_op jit(solution)/shard_map/ppermute | solution.py:492
  371.8 111.5 %collective-permute-start.21 = (bf16[2,2,48,1024]{3,2,0,1:T(8,128)(2,1)S(1)}, bf16[2,2,48,1024]{3,2,0,1:T(8,128)(2,1)S(1)}, u32[]{:S(2)}, u32[]{:S(2)}) collective-permute-start(bf16[2,2,48,1024]{3,2,0,1:T(8,128)(2,1)S(1)} %get-tuple-element.151), channel_id=1, source_target_pairs={{0,8},{4,12},{8,0},{12,4},{16,24},{20,28},{24,16},{28,20},{1,9},{5... | collective-permute-start | bytes 1179656 | tf_op jit(solution)/shard_map/ppermute | solution.py:685
  381.6 101.6 %collective-permute-start.22 = (bf16[2,2,48,1024]{3,2,0,1:T(8,128)(2,1)S(1)}, bf16[2,2,48,1024]{3,2,0,1:T(8,128)(2,1)S(1)}, u32[]{:S(2)}, u32[]{:S(2)}) collective-permute-start(bf16[2,2,48,1024]{3,2,0,1:T(8,128)(2,1)S(1)} %get-tuple-element.152), channel_id=1, source_target_pairs={{0,16},{4,20},{8,24},{12,28},{16,0},{20,4},{24,8},{28,12},{1,17},{... | collective-permute-start | bytes 1179656 | tf_op jit(solution)/shard_map/ppermute | solution.py:685
  381.6 101.6 %collective-permute-start.23 = (bf16[2,2,48,1024]{3,2,0,1:T(8,128)(2,1)S(1)}, bf16[2,2,48,1024]{3,2,0,1:T(8,128)(2,1)S(1)}, u32[]{:S(2)}, u32[]{:S(2)}) collective-permute-start(bf16[2,2,48,1024]{3,2,0,1:T(8,128)(2,1)S(1)} %get-tuple-element.153), channel_id=1, source_target_pairs={{0,24},{4,28},{8,16},{12,20},{16,8},{20,12},{24,0},{28,4},{1,25},{... | collective-permute-start | bytes 1179656 | tf_op jit(solution)/shard_map/ppermute | solution.py:685
  483.6 4.9 collective-permute-start.24
  501.5 2.7 collective-permute-start.27
  504.3 4.5 collective-permute-start.28
  508.0 175.7 %collective-permute-start.29 = (f32[512,384]{1,0:T(8,128)S(1)}, f32[512,384]{1,0:T(8,128)S(1)}, u32[]{:S(2)}, u32[]{:S(2)}) collective-permute-start(f32[512,384]{1,0:T(8,128)S(1)} %get-tuple-element.193), channel_id=1, source_target_pairs={{0,1},{1,0},{2,3},{3,2},{4,5},{5,4},{6,7},{7,6},{8,9},{9,8},{10,11... | collective-permute-start | bytes 2359304 | tf_op jit(solution)/shard_map/ppermute | solution.py:492
  683.8 24.2 %collective-permute-start.30 = (f32[1024,384]{1,0:T(8,128)S(1)}, f32[1024,384]{1,0:T(8,128)S(1)}, u32[]{:S(2)}, u32[]{:S(2)}) collective-permute-start(f32[1024,384]{1,0:T(8,128)S(1)} %maximum_select_fusion.2), channel_id=1, source_target_pairs={{1,2},{2,1},{5,6},{6,5},{9,10},{10,9},{13,14},{14,13},{17,18},{18,... | collective-permute-start | bytes 4718600 | tf_op jit(solution)/shard_map/ppermute | solution.py:1023
  (69 other events, 498.1 us)

commit v7 on v6

--- a/solution.py
+++ b/solution.py
@@ -1137,14 +1137,6 @@
     (normed_ffn_grad,) = collect_tokens(
         far, lambda operand: (ffn_input(operand, up_own, up_peer, 0, 2),), pre_grad
     )
-    normed_ffn_grad, second_recv = lax.optimization_barrier((normed_ffn_grad, second_recv))
-    down_recv = jnp.concatenate([first_recv, second_recv])
-    down_own_sum, *down_sends = z_blocks(add_low(down_keep, down_recv), 1)
-    normed_ffn_grad, down_sends, up_send = lax.optimization_barrier(
-        (normed_ffn_grad, down_sends, up_send)
-    )
-    up_recv = along_dp(up_send, 1)
-    down_recvs = [along_dp(block, 2 * k + 2) for k, block in enumerate(down_sends)]
     mix_own = mixing[:part].T
     centre = jnp.sum(mix_own * gate_grad, axis=0, keepdims=True)
     logit_grad = (mix_own * (gate_grad - centre)).T.astype(BF)
@@ -1161,6 +1153,14 @@
     normed_attn = jnp.concatenate([normed_attn[0], normed_attn[1]], axis=1)
     context_grad = jnp.dot(low_seq, w_out_full.T, preferred_element_type=F32)
     context_grad = context_grad.astype(BF)
+    context_grad, second_recv = lax.optimization_barrier((context_grad, second_recv))
+    down_recv = jnp.concatenate([first_recv, second_recv])
+    down_own_sum, *down_sends = z_blocks(add_low(down_keep, down_recv), 1)
+    context_grad, down_sends, up_send = lax.optimization_barrier(
+        (context_grad, down_sends, up_send)
+    )
+    up_recv = along_dp(up_send, 1)
+    down_recvs = [along_dp(block, 2 * k + 2) for k, block in enumerate(down_sends)]
     qkv_grad = jnp.concatenate(
         [
             attend_backward(
@@ -1170,12 +1170,10 @@
         ],
         axis=2,
     )
-    qkv_grad, down_recvs, up_recv = lax.optimization_barrier((qkv_grad, down_recvs, up_recv))
+    qkv_grad, up_recv = lax.optimization_barrier((qkv_grad, up_recv))
     up_own_sum, *up_sends = z_blocks(add_low(up_keep, up_recv), 2)
     qkv_grad, up_sends = lax.optimization_barrier((qkv_grad, up_sends))
     up_recvs = [along_dp(block, 2 * k + 2) for k, block in enumerate(up_sends)]
-    down_sum = add_low(down_own_sum, *down_recvs)
-    down_peer_sum = swap(down_sum[:, :, half:], "row")
     w_qkv_grad = jnp.einsum(
         "td,kte->dke", normed_attn, qkv_grad, preferred_element_type=F32
     ).astype(BF)
@@ -1187,6 +1185,9 @@
     input_back, gain_attn_grad = norm_backward(x_own, rstd_attn, gain_a, normed_attn_grad)
     input_grad = hidden_grad + input_back
 
+    w_qkv_grad, down_recvs = lax.optimization_barrier((w_qkv_grad, down_recvs))
+    down_sum = add_low(down_own_sum, *down_recvs)
+    down_peer_sum = swap(down_sum[:, :, half:], "row")
     grad_pair = jnp.concatenate(
         [
             w_qkv_grad.reshape(2, n_dp, owner_d, 3, half),

time: 724 us -> 734 us (1.014)
  waiting for transfers between devices: 35.7 us -> 44.4 us
  starting transfers between devices: 44.7 us -> 36.2 us
    ppermute x2, waiting for transfers between devices: 4.64 us -> 13 us  [from_sequence(): moved = lax.ppermute(whole, ('row', 'col'), [(1, 2), (2, 1)])]
    ppermute x9, starting transfers between devices: 17.5 us -> 9.21 us  [along_dp(): lax.ppermute(values, 'dp', [(i, i ^ step) for i in range(lax.axis_size('d...]
    unnamed x141 -> x149, local copies, waits for them, and re-layouts: 16.2 us -> 20.3 us
  transfers between devices with their start and end apart: 31 -> 31, of which waited for: 15 -> 15; matrix products, arithmetic and copies ran while one was open for 11% -> 12% of each run, Pallas kernels for 49% -> 47%
where the time goes in v7:
time: 734 us; the launch traced here: 723 us
  Pallas kernels  500 us (68%)
  local copies, waits for them, and re-layouts  65.2 us (9%)
  other arithmetic  52.7 us (7%)
  waiting for transfers between devices  44.4 us (6%)
  starting transfers between devices  36.2 us (5%)
  matrix products  16.8 us (2%)
  between operations  7.43 us (1%)
    pallas_call x1, Pallas kernels, dp_gather(): pl.pallas_call(functools.partial(gather_kernel, n, plan), out_shape=[jax....  170 us
    pallas_call x1, Pallas kernels, dp_reduce(): pl.pallas_call(functools.partial(reduce_kernel, n, slots), out_shape=[jax...  96.8 us
    pallas_call x1, Pallas kernels, front(): pl.pallas_call(functools.partial(front_kernel, n), out_shape=[shape((rows...  91.2 us
    pallas_call x2, Pallas kernels, ffn_forward(): pl.pallas_call(ffn_kernel, grid=(slots,), out_shape=[jax.ShapeDtypeStruct...  39 us
    pallas_call x2, Pallas kernels, ffn_backward(): pl.pallas_call(ffn_back_kernel, grid=(slots,), out_shape=[jax.ShapeDtypeS...  30.9 us
    pallas_call x2, Pallas kernels, ffn_input(): pl.pallas_call(ffn_input_kernel, grid=(slots,), out_shape=jax.ShapeDtypeS...  22.5 us
    unnamed x149, local copies, waits for them, and re-layouts  20.3 us
    pallas_call x1, Pallas kernels, ffn_up(): pl.pallas_call(ffn_up_kernel, grid=(slots,), out_shape=jax.ShapeDtypeStru...  19.9 us
  transfers between devices with their start and end apart: 31, of which 15 were waited for; matrix products, arithmetic and copies ran while one was open for 12% of the time, Pallas kernels for 47%

profile of v7, /device:TPU:27, one launch (start us, length us, event | category | flops | bytes accessed | tf_op | source)
XLA Modules:
  0.0 723.0 jit_solution(1857208476163388291)
XLA Ops:
  5.3 91.2 %shard_map.229 = (bf16[1024,384]{1,0:T(8,128)(2,1)S(1)}, bf16[1024,384]{1,0:T(8,128)(2,1)S(1)}, bf16[1024,384]{1,0:T(8,128)(2,1)S(1)}, bf16[1024,384]{1,0:T(8,12...) custom-call(bf16[1024,384]{1,0:T(8,128)(2,1)} %x_in.1, ...), custom_call_target="tpu_custom_call" | custom-call | tf_op jit(solution)/shard_map/pallas_call | solution.py:375
  102.0 2.9 fusion.41
  109.7 19.4 %shard_map.230 = (bf16[5,2048,1024]{2,1,0:T(8,128)(2,1)}, bf16[5,2048,512]{2,1,0:T(8,128)(2,1)}, f32[1024,768]{1,0:T(8,128)}) custom-call(bf16[2048,768]{1,0:T(8,128)(2,1)} %bitcast.165, bf16[5,384,1024]{2,1,0:T(8,128)(2,1)} %get-tuple-element.100.up_own, bf16[5,384,1024]{2,1,0:T(8,128)(2,1)} %get-tuple-element.101.up_peer, ...), custom_call_target="tpu_custom_call" | custom-call | flops 12079595520 | bytes 20971520 | tf_op jit(solution)/shard_map/pallas_call | solution.py:835
  134.9 19.6 %shard_map.231 = (bf16[5,2048,1024]{2,1,0:T(8,128)(2,1)}, bf16[5,2048,512]{2,1,0:T(8,128)(2,1)}, f32[1024,768]{1,0:T(8,128)}) custom-call(bf16[2048,768]{1,0:T(8,128)(2,1)} %bitcast.166, bf16[5,384,1024]{2,1,0:T(8,128)(2,1)} %get-tuple-element.100.up_own, ...), custom_call_target="tpu_custom_call", output_to_operand_aliasing={{0}: (6, {}), {1}: (7, {})} | custom-call | flops 12079595520 | bytes 20971520 | tf_op jit(solution)/shard_map/pallas_call | solution.py:835
  159.8 2.9 multiply_reduce_fusion
  167.7 15.4 %shard_map.232 = (bf16[5,2048,1024]{2,1,0:T(8,128)(2,1)}, f32[1024,8]{1,0:T(8,128)}) custom-call(bf16[1024,768]{1,0:T(8,128)(2,1)} %pad_maximum_fusion.2.grads.near, bf16[5,2048,1024]{2,1,0:T(8,128)(2,1)} %get-tuple-element.115.pre, bf16[5,512,384]{2,1,0:T(8,128)(2,1)} %fusion.2.down_own, bf16[5,512,384]{2,1,0:T(8,128)(2,1)} %get-tuple-element.102.down_peer, ...), custom_call_target="tpu_custom_call" | custom-call | flops 8053063680 | bytes 26214400 | tf_op jit(solution)/shard_map/pallas_call | solution.py:892
  187.3 10.8 %shard_map.233 = bf16[5,512,768]{2,1,0:T(8,128)(2,1)S(1)} custom-call(bf16[1024,768]{1,0:T(8,128)(2,1)S(1)} %copy-done.15, bf16[1024,768]{1,0:T(8,128)(2,1)S(1)} %constant_dynamic-update-slice_fusion.far.grads, bf16[5,2048,512]{2,1,0:T(8,128)(2,1)} %get-tuple-element.119.act), custom_call_target="tpu_custom_call" | custom-call | flops 8053063680 | bytes 20971520 | tf_op jit(solution)/shard_map/pallas_call | solution.py:930
  201.3 15.5 %shard_map.234 = (bf16[5,2048,1024]{2,1,0:T(8,128)(2,1)}, f32[1024,8]{1,0:T(8,128)}) custom-call(bf16[1024,768]{1,0:T(8,128)(2,1)} %copy-done.8, bf16[5,2048,1024]{2,1,0:T(8,128)(2,1)} %get-tuple-element.115.pre, bf16[5,512,384]{2,1,0:T(8,128)(2,1)} %fusion.2.down_own, ...), custom_call_target="tpu_custom_call", output_to_operand_aliasing={{0}: (5, {})} | custom-call | flops 8053063680 | bytes 26214400 | tf_op jit(solution)/shard_map/pallas_call | solution.py:892
  220.9 19.9 %shard_map.235 = bf16[5,768,1024]{2,1,0:T(8,128)(2,1)S(1)} custom-call(bf16[2048,768]{1,0:T(8,128)(2,1)S(1)} %bitcast.167, bf16[5,2048,1024]{2,1,0:T(8,128)(2,1)} %get-tuple-element.130.pre_grad), custom_call_target="tpu_custom_call" | custom-call | flops 16106127360 | bytes 36700160 | tf_op jit(solution)/shard_map/pallas_call | solution.py:955
  248.9 11.3 %shard_map.236 = f32[1024,768]{1,0:T(8,128)S(1)} custom-call(bf16[5,2048,1024]{2,1,0:T(8,128)(2,1)} %get-tuple-element.130.pre_grad, bf16[5,384,1024]{2,1,0:T(8,128)(2,1)S(1)} %copy-done.2, bf16[5,384,1024]{2,1,0:T(8,128)(2,1)S(1)} %copy-done.3), custom_call_target="tpu_custom_call" | custom-call | flops 8053063680 | bytes 20971520 | tf_op jit(solution)/shard_map/pallas_call | solution.py:984
  267.2 11.3 %shard_map.237 = f32[1024,768]{1,0:T(8,128)S(1)} custom-call(bf16[5,2048,1024]{2,1,0:T(8,128)(2,1)} %get-tuple-element.130.pre_grad, bf16[5,384,1024]{2,1,0:T(8,128)(2,1)S(1)} %copy-done.2, bf16[5,384,1024]{2,1,0:T(8,128)(2,1)S(1)} %copy-done.3), custom_call_target="tpu_custom_call" | custom-call | flops 8053063680 | bytes 20971520 | tf_op jit(solution)/shard_map/pallas_call | solution.py:984
  278.5 4.3 collective-permute-done.13
  288.5 3.3 maximum_select_fusion
  291.8 3.2 collective-permute-start.4
  305.4 8.6 %collective-permute-done.4 = f32[1024,384]{1,0:T(8,128)} collective-permute-done((f32[1024,384]{1,0:T(8,128)}, f32[1024,384]{1,0:T(8,128)}, u32[]{:S(2)}, u32[]{:S(2)}) %collective-permute-start.4) | collective-permute-done | bytes 1572896 | tf_op jit(solution)/shard_map/ppermute | solution.py:1023
  314.1 2.7 broadcast_select_fusion.1
  317.0 3.0 convolution_convert_fusion.1.context_grad
  320.0 3.5 collective-permute-done.16
  327.2 6.3 shard_map.238
  333.5 6.4 shard_map.239
  344.0 3.5 convolution_convert_fusion.2
  355.7 6.3 shard_map.240
  362.3 12.5 %collective-permute-done.17 = bf16[2,2,4,48,1024]{4,3,0,1,2:T(8,128)(2,1)} collective-permute-done((bf16[2,2,4,48,1024]{4,3,0,1,2:T(8,128)(2,1)}, bf16[2,2,4,48,1024]{4,3,0,1,2:T(8,128)(2,1)}, u32[]{:S(2)}, u32[]{:S(2)}) %collective-permute-start.17) | collective-permute-done | bytes 1572896 | tf_op jit(solution)/shard_map/ppermute | solution.py:685
  393.0 96.8 %shard_map.241 = (bf16[2,3,48,1024]{3,2,1,0:T(8,128)(2,1)S(1)}, bf16[192,384]{1,0:T(8,128)(2,1)S(1)}) custom-call(bf16[5,2,4,2,48,1024]{5,4,3,2,1,0:T(8,128)(2,1)} %bitcast.168, bf16[2,4,2,192,384]{4,3,2,1,0:T(8,128)(2,1)S(1)} %bitcast.169), custom_call_target="tpu_custom_call" | custom-call | tf_op jit(solution)/shard_map/pallas_call | solution.py:641
  492.2 3.5 collective-permute-done.24
  501.1 2.9 broadcast_select_fusion
  511.2 5.0 collective-permute-start.28
  517.7 170.2 %shard_map.242 = (bf16[4,384,2,1024]{3,2,1,0:T(2,128)(2,1)}, bf16[384,2,1024]{2,1,0:T(2,128)(2,1)}, bf16[4,2,512,384]{3,2,1,0:T(8,128)(2,1)}, bf16[2,512,384]{2,...) custom-call(bf16[4,48,2,1024]{3,2,1,0:T(2,128)(2,1)} %slice.296.refs_0_, ...), custom_call_target="tpu_custom_call" | custom-call | tf_op jit(solution)/shard_map/pallas_call | solution.py:779
  697.1 5.1 collective-permute-start.30
  705.9 3.2 convert_multiply_fusion.1
  709.1 6.6 convert_multiply_fusion
  715.7 4.4 collective-permute-done.30
  (336 shorter events, 133.9 us)
Async XLA Ops:
  5.3 96.4 %copy-start.68 = (s32[2048,2]{0,1:T(2,128)S(1)}, s32[2048,2]{0,1:T(2,128)}, u32[]{:S(2)}) copy-start(s32[2048,2]{0,1:T(2,128)} %param.19) | copy-start | bytes 49156
  130.6 2.4 collective-permute-start
  134.7 19.9 %collective-permute-start.1 = (bf16[512,768]{1,0:T(8,128)(2,1)S(1)}, bf16[512,768]{1,0:T(8,128)(2,1)S(1)}, u32[]{:S(2)}, u32[]{:S(2)}) collective-permute-start(bf16[512,768]{1,0:T(8,128)(2,1)S(1)} %pad_maximum_fusion.4), channel_id=1, source_target_pairs={{0,2},{2,0},{1,3},{3,1},{4,6},{6,4},{5,7},{7,5},{8,10},{10,8},{9,1... | collective-permute-start | bytes 2359304 | tf_op jit(solution)/shard_map/ppermute | solution.py:492
  157.1 2.7 collective-permute-start.2
  157.5 1.9 collective-permute-start.5
  164.1 2.3 collective-permute-start.6
  164.7 19.1 %collective-permute-start.7 = (bf16[512,768]{1,0:T(8,128)(2,1)S(1)}, bf16[512,768]{1,0:T(8,128)(2,1)S(1)}, u32[]{:S(2)}, u32[]{:S(2)}) collective-permute-start(bf16[512,768]{1,0:T(8,128)(2,1)S(1)} %pad_maximum_fusion.5), channel_id=1, source_target_pairs={{0,2},{2,0},{1,3},{3,1},{4,6},{6,4},{5,7},{7,5},{8,10},{10,8},{9,1... | collective-permute-start | bytes 2359304 | tf_op jit(solution)/shard_map/ppermute | solution.py:492
  183.7 2.9 collective-permute-start.8
  218.1 23.1 %collective-permute-start.9 = (f32[2,4,512]{2,1,0:T(4,128)S(1)}, f32[2,4,512]{2,1,0:T(4,128)S(1)}, u32[]{:S(2)}, u32[]{:S(2)}) collective-permute-start(f32[2,4,512]{2,1,0:T(4,128)S(1)} %pad_maximum_fusion.12), channel_id=1, source_target_pairs={{0,1},{1,0},{2,3},{3,2},{4,5},{5,4},{6,7},{7,6},{8,9},{9,8},{10,11... | collective-permute-start | bytes 49160 | tf_op jit(solution)/shard_map/ppermute | solution.py:492
  219.8 27.4 %collective-permute-start.11 = (bf16[3,4,64,768]{3,2,0,1:T(8,128)(2,1)S(1)}, bf16[3,4,64,768]{3,2,0,1:T(8,128)(2,1)S(1)}, u32[]{:S(2)}, u32[]{:S(2)}) collective-permute-start(bf16[3,4,64,768]{3,2,0,1:T(8,128)(2,1)S(1)} %slice.230), channel_id=1, source_target_pairs={{0,4},{4,0},{8,12},{12,8},{16,20},{20,16},{24,28},{28,24},{1,5},{5... | collective-permute-start | bytes 3538952 | tf_op jit(solution)/shard_map/ppermute | solution.py:685
  241.2 5.7 collective-permute-start.10
  260.3 3.3 collective-permute-start.12
  264.0 18.8 %collective-permute-start.13 = (bf16[512,768]{1,0:T(8,128)(2,1)S(1)}, bf16[512,768]{1,0:T(8,128)(2,1)S(1)}, u32[]{:S(2)}, u32[]{:S(2)}) collective-permute-start(bf16[512,768]{1,0:T(8,128)(2,1)S(1)} %pad_maximum_fusion.6), channel_id=1, source_target_pairs={{0,2},{2,0},{1,3},{3,1},{4,6},{6,4},{5,7},{7,5},{8,10},{10,8},{9,1... | collective-permute-start | bytes 2359304 | tf_op jit(solution)/shard_map/ppermute | solution.py:492
  266.7 21.8 %collective-permute-start.3 = (f32[512,384]{1,0:T(8,128)}, f32[512,384]{1,0:T(8,128)}, u32[]{:S(2)}, u32[]{:S(2)}) collective-permute-start(f32[512,384]{1,0:T(8,128)} %get-tuple-element.203), channel_id=1, source_target_pairs={{0,1},{1,0},{2,3},{3,2},{4,5},{5,4},{6,7},{7,6},{8,9},{9,8},{10,11... | collective-permute-start | bytes 2359304 | tf_op jit(solution)/shard_map/ppermute | solution.py:492
  284.0 11.1 %collective-permute-start.14 = (bf16[512,768]{1,0:T(8,128)(2,1)}, bf16[512,768]{1,0:T(8,128)(2,1)}, u32[]{:S(2)}, u32[]{:S(2)}) collective-permute-start(bf16[512,768]{1,0:T(8,128)(2,1)} %slice.376), channel_id=1, source_target_pairs={{0,1},{1,0},{2,3},{3,2},{4,5},{5,4},{6,7},{7,6},{8,9},{9,8},{10,11... | collective-permute-start | bytes 2359304 | tf_op jit(solution)/shard_map/ppermute | solution.py:492
  291.8 22.2 %collective-permute-start.4 = (f32[1024,384]{1,0:T(8,128)}, f32[1024,384]{1,0:T(8,128)}, u32[]{:S(2)}, u32[]{:S(2)}) collective-permute-start(f32[1024,384]{1,0:T(8,128)} %maximum_select_fusion), channel_id=1, source_target_pairs={{1,2},{2,1},{5,6},{6,5},{9,10},{10,9},{13,14},{14,13},{17,18},{18,... | collective-permute-start | bytes 4718600 | tf_op jit(solution)/shard_map/ppermute | solution.py:1023
  299.9 17.1 %collective-permute-start.15 = (bf16[512,768]{1,0:T(8,128)(2,1)}, bf16[512,768]{1,0:T(8,128)(2,1)}, u32[]{:S(2)}, u32[]{:S(2)}) collective-permute-start(bf16[512,768]{1,0:T(8,128)(2,1)} %get-tuple-element.185), channel_id=1, source_target_pairs={{0,1},{1,0},{2,3},{3,2},{4,5},{5,4},{6,7},{7,6},{8,9},{9,8},{10,11... | collective-permute-start | bytes 2359304 | tf_op jit(solution)/shard_map/ppermute | solution.py:492
  304.9 18.7 %collective-permute-start.16 = (bf16[2,4,64,768]{3,2,0,1:T(8,128)(2,1)S(1)}, bf16[2,4,64,768]{3,2,0,1:T(8,128)(2,1)S(1)}, u32[]{:S(2)}, u32[]{:S(2)}) collective-permute-start(bf16[2,4,64,768]{3,2,0,1:T(8,128)(2,1)S(1)} %slice.239), channel_id=1, source_target_pairs={{0,4},{4,0},{8,12},{12,8},{16,20},{20,16},{24,28},{28,24},{1,5},{5... | collective-permute-start | bytes 2359304 | tf_op jit(solution)/shard_map/ppermute | solution.py:685
  340.0 34.9 %collective-permute-start.17 = (bf16[2,2,4,48,1024]{4,3,0,1,2:T(8,128)(2,1)}, bf16[2,2,4,48,1024]{4,3,0,1,2:T(8,128)(2,1)}, u32[]{:S(2)}, u32[]{:S(2)}) collective-permute-start(bf16[2,2,4,48,1024]{4,3,0,1,2:T(8,128)(2,1)} %bitcast.157), channel_id=1, source_target_pairs={{0,4},{4,0},{8,12},{12,8},{16,20},{20,16},{24,28},{28,24},{1,5},{5... | collective-permute-start | bytes 4718600 | tf_op jit(solution)/shard_map/ppermute | solution.py:685
  340.5 45.7 %collective-permute-start.18 = (bf16[5,64,768]{2,1,0:T(8,128)(2,1)}, bf16[5,64,768]{2,1,0:T(8,128)(2,1)}, u32[]{:S(2)}, u32[]{:S(2)}) collective-permute-start(bf16[5,64,768]{2,1,0:T(8,128)(2,1)} %get-tuple-element.146), channel_id=1, source_target_pairs={{0,8},{4,12},{8,0},{12,4},{16,24},{20,28},{24,16},{28,20},{1,9},{5... | collective-permute-start | bytes 1474568 | tf_op jit(solution)/shard_map/ppermute | solution.py:685
  341.6 44.6 %collective-permute-start.19 = (bf16[5,64,768]{2,1,0:T(8,128)(2,1)}, bf16[5,64,768]{2,1,0:T(8,128)(2,1)}, u32[]{:S(2)}, u32[]{:S(2)}) collective-permute-start(bf16[5,64,768]{2,1,0:T(8,128)(2,1)} %get-tuple-element.147), channel_id=1, source_target_pairs={{0,16},{4,20},{8,24},{12,28},{16,0},{20,4},{24,8},{28,12},{1,17},{... | collective-permute-start | bytes 1474568 | tf_op jit(solution)/shard_map/ppermute | solution.py:685
  341.6 44.6 %collective-permute-start.20 = (bf16[5,64,768]{2,1,0:T(8,128)(2,1)}, bf16[5,64,768]{2,1,0:T(8,128)(2,1)}, u32[]{:S(2)}, u32[]{:S(2)}) collective-permute-start(bf16[5,64,768]{2,1,0:T(8,128)(2,1)} %get-tuple-element.148), channel_id=1, source_target_pairs={{0,24},{4,28},{8,16},{12,20},{16,8},{20,12},{24,0},{28,4},{1,25},{... | collective-permute-start | bytes 1474568 | tf_op jit(solution)/shard_map/ppermute | solution.py:685
  381.6 124.6 %collective-permute-start.26 = (bf16[512,768]{1,0:T(8,128)(2,1)}, bf16[512,768]{1,0:T(8,128)(2,1)}, u32[]{:S(2)}, u32[]{:S(2)}) collective-permute-start(bf16[512,768]{1,0:T(8,128)(2,1)} %fusion.19), channel_id=1, source_target_pairs={{0,1},{1,0},{2,3},{3,2},{4,5},{5,4},{6,7},{7,6},{8,9},{9,8},{10,11... | collective-permute-start | bytes 2359304 | tf_op jit(solution)/shard_map/ppermute | solution.py:492
  388.0 101.8 %collective-permute-start.25 = (bf16[5,64,384]{2,1,0:T(8,128)(2,1)S(1)}, bf16[5,64,384]{2,1,0:T(8,128)(2,1)S(1)}, u32[]{:S(2)}, u32[]{:S(2)}) collective-permute-start(bf16[5,64,384]{2,1,0:T(8,128)(2,1)S(1)} %get-tuple-element.217), channel_id=1, source_target_pairs={{0,2},{2,0},{1,3},{3,1},{4,6},{6,4},{5,7},{7,5},{8,10},{10,8},{9,1... | collective-permute-start | bytes 737288 | tf_op jit(solution)/shard_map/ppermute | solution.py:492
  389.2 101.6 %collective-permute-start.21 = (bf16[2,2,48,1024]{3,2,0,1:T(8,128)(2,1)S(1)}, bf16[2,2,48,1024]{3,2,0,1:T(8,128)(2,1)S(1)}, u32[]{:S(2)}, u32[]{:S(2)}) collective-permute-start(bf16[2,2,48,1024]{3,2,0,1:T(8,128)(2,1)S(1)} %get-tuple-element.153), channel_id=1, source_target_pairs={{0,8},{4,12},{8,0},{12,4},{16,24},{20,28},{24,16},{28,20},{1,9},{5... | collective-permute-start | bytes 1179656 | tf_op jit(solution)/shard_map/ppermute | solution.py:685
  390.3 100.5 %collective-permute-start.22 = (bf16[2,2,48,1024]{3,2,0,1:T(8,128)(2,1)S(1)}, bf16[2,2,48,1024]{3,2,0,1:T(8,128)(2,1)S(1)}, u32[]{:S(2)}, u32[]{:S(2)}) collective-permute-start(bf16[2,2,48,1024]{3,2,0,1:T(8,128)(2,1)S(1)} %get-tuple-element.154), channel_id=1, source_target_pairs={{0,16},{4,20},{8,24},{12,28},{16,0},{20,4},{24,8},{28,12},{1,17},{... | collective-permute-start | bytes 1179656 | tf_op jit(solution)/shard_map/ppermute | solution.py:685
  390.3 100.4 %collective-permute-start.23 = (bf16[2,2,48,1024]{3,2,0,1:T(8,128)(2,1)S(1)}, bf16[2,2,48,1024]{3,2,0,1:T(8,128)(2,1)S(1)}, u32[]{:S(2)}, u32[]{:S(2)}) collective-permute-start(bf16[2,2,48,1024]{3,2,0,1:T(8,128)(2,1)S(1)} %get-tuple-element.155), channel_id=1, source_target_pairs={{0,24},{4,28},{8,16},{12,20},{16,8},{20,12},{24,0},{28,4},{1,25},{... | collective-permute-start | bytes 1179656 | tf_op jit(solution)/shard_map/ppermute | solution.py:685
  491.1 4.6 collective-permute-start.24
  508.4 2.7 collective-permute-start.27
  511.2 5.9 collective-permute-start.28
  516.3 180.7 %collective-permute-start.29 = (f32[512,384]{1,0:T(8,128)S(1)}, f32[512,384]{1,0:T(8,128)S(1)}, u32[]{:S(2)}, u32[]{:S(2)}) collective-permute-start(f32[512,384]{1,0:T(8,128)S(1)} %get-tuple-element.195), channel_id=1, source_target_pairs={{0,1},{1,0},{2,3},{3,2},{4,5},{5,4},{6,7},{7,6},{8,9},{9,8},{10,11... | collective-permute-start | bytes 2359304 | tf_op jit(solution)/shard_map/ppermute | solution.py:492
  697.1 23.0 %collective-permute-start.30 = (f32[1024,384]{1,0:T(8,128)S(1)}, f32[1024,384]{1,0:T(8,128)S(1)}, u32[]{:S(2)}, u32[]{:S(2)}) collective-permute-start(f32[1024,384]{1,0:T(8,128)S(1)} %maximum_select_fusion.2), channel_id=1, source_target_pairs={{1,2},{2,1},{5,6},{6,5},{9,10},{10,9},{13,14},{14,13},{17,18},{18,... | collective-permute-start | bytes 4718600 | tf_op jit(solution)/shard_map/ppermute | solution.py:1023
  (73 other events, 488.6 us)
